TPU v7x, 512 devices: a whole 4x8x8 slice. The times are simulated.
512 devices in a mesh: ctx: 8 (over x, core), exp: 64 (over y, z).
Axes of the slice: x: 4, y: 8, z: 8, core: 2. Of those that a mesh axis runs over, the one named last changes fastest.
Arguments:
- queries: float32 [64, 2048, 128], P('exp', 'ctx'), may hold values from -0.5 to 0.5
- key_vectors: float32 [64, 2048, 128], P('exp', 'ctx'), may hold values from -1 to 1, as said below
- values: float32 [64, 2048, 128], P('exp', 'ctx'), may hold values from -6 to 6
- out_gate: float32 [64, 2048, 128], P('exp', 'ctx'), may hold values from -6 to 6
- write_strength: float32 [64, 2048], P('exp', 'ctx'), may hold values from 0.2 to 0.9
- log_fading_factor: float32 [64, 2048], P('exp', 'ctx'), may hold values from -2 to 0
- block_inverse: float32 [64, 32, 64, 64], P('exp', 'ctx'), may hold values from -1 to 1, as said below
- norm_gain: float32 [128], replicated, may hold values from 0.5 to 1.5
- hidden: bfloat16 [65536, 1024], P(('ctx', 'exp')), may hold values from -6 to 6
- routes: int32 [65536, 10], P(('ctx', 'exp')), may hold values from 0 to 511, all different within a row; in each aligned block of 128 rows (0 to 127, 128 to 255, ...) at most 3 rows name the same one
- route_weights: float32 [65536, 10], P(('ctx', 'exp')), may hold values from 0.1 to 1.9
- gate_weights: bfloat16 [512, 1024, 512], P(('ctx', 'exp')), may hold values from -0.1875 to 0.1875
- up_weights: bfloat16 [512, 1024, 512], P(('ctx', 'exp')), may hold values from -0.1875 to 0.1875
- down_weights: bfloat16 [512, 512, 1024], P(('ctx', 'exp')), may hold values from -0.25 to 0.25
Outputs:
- mixer_output: float32 [64, 2048, 128], P('exp', 'ctx')
- expert_output: bfloat16 [65536, 1024], P(('ctx', 'exp'))
Inputs may be any that keep to these rules, and one draw needn't show every extreme that they name: `routes`: each row names 10 different experts. Among the 128 rows of one device no expert is named more than 3 times, and in every draw some expert is named exactly 3 times by one device's rows. `key_vectors`: every row has Euclidean length 1. `block_inverse`: each block's matrix has ones on its diagonal and zeros above it.
All inputs are finite; a program needn't handle non-finite values.
Results may differ from a plain program's by a relative error of at most 0.0058.
Values may be sent and summed in bfloat16 or wider, within the bound.
No kernel may reach another device: no remote copies, remote signals or barrier semaphores. Data moves between devices by JAX's collectives and lax.ppermute only.
A program may use at most 128 MiB of HBM per device.

v0:
```python
import jax
import jax.numpy as jnp
from jax import lax
from jax.sharding import PartitionSpec as P

TOP_PRECISION = lax.Precision.HIGHEST
NORM_EPSILON = 1e-06


def passed_along(block, axis, distance):
    devices = range(lax.axis_size(axis))
    route = [(i - distance, i) for i in devices if i - distance in devices]
    return lax.ppermute(block, axis, route)


def block_parts(queries, key_vectors, values, write_strength, log_fading_factor, block_inverse):
    tracks, length, head_width = queries.shape
    block_size = block_inverse.shape[-1]
    blocks = length // block_size
    shape_four = (tracks, blocks, block_size, head_width)
    query_blocks = queries.reshape(shape_four)
    key_blocks = key_vectors.reshape(shape_four)
    value_blocks = values.reshape(shape_four)
    strength = write_strength.reshape(tracks, blocks, block_size)
    running = jnp.cumsum(log_fading_factor.reshape(tracks, blocks, block_size), axis=-1)
    growth = jnp.exp(running)
    final_log = running[..., -1:]
    write_keys = jnp.einsum(
        "sbij,sbjh->sbih",
        block_inverse,
        key_blocks * (strength * growth)[..., None],
        precision=TOP_PRECISION,
    )
    write_values = jnp.einsum(
        "sbij,sbjh->sbih",
        block_inverse,
        value_blocks * strength[..., None],
        precision=TOP_PRECISION,
    )
    faded_keys = key_blocks * jnp.exp(final_log - running)[..., None]
    faded_queries = query_blocks * growth[..., None]
    row_index = lax.broadcasted_iota(jnp.int32, (block_size, block_size), 0)
    col_index = lax.broadcasted_iota(jnp.int32, (block_size, block_size), 1)
    spread = running[..., :, None] - running[..., None, :]
    causal_fade = jnp.where(row_index >= col_index, jnp.exp(jnp.minimum(spread, 0.0)), 0.0)
    causal = (
        jnp.einsum("sbih,sbjh->sbij", query_blocks, key_blocks, precision=TOP_PRECISION)
        * causal_fade
    )
    return (faded_queries, write_keys, write_values, faded_keys, causal, jnp.exp(final_log))


def block_step(states, pieces):
    faded_queries, write_keys, write_values, faded_keys, causal, decays = pieces
    fresh_values = write_values - jnp.einsum(
        "sch,shv->scv", write_keys, states, precision=TOP_PRECISION
    )
    attended = jnp.einsum("sch,shv->scv", faded_queries, states, precision=TOP_PRECISION)
    attended = attended + jnp.einsum("sij,sjv->siv", causal, fresh_values, precision=TOP_PRECISION)
    states = decays[..., None] * states + jnp.einsum(
        "sch,scv->shv", faded_keys, fresh_values, precision=TOP_PRECISION
    )
    return (states, attended)


def run_blocks(pieces, states):
    moved = tuple((jnp.moveaxis(piece_item, 1, 0) for piece_item in pieces))
    states, attended = lax.scan(block_step, states, moved)
    return (states, jnp.moveaxis(attended, 0, 1))


def gated_norm(attended, norm_gain, out_gate):
    root_mean = jnp.sqrt(jnp.mean(attended * attended, axis=-1, keepdims=True) + NORM_EPSILON)
    return attended / root_mean * norm_gain * jax.nn.silu(out_gate)


def compose(carried, block_piece):
    current_mapping, current_addend = carried
    segment_mapping, segment_addend = block_piece
    updated_mapping = jnp.einsum(
        "qfz,qze->qfe", segment_mapping, current_mapping, precision=TOP_PRECISION
    )
    updated_addend = (
        jnp.einsum("qfz,qze->qfe", segment_mapping, current_addend, precision=TOP_PRECISION)
        + segment_addend
    )
    return ((updated_mapping, updated_addend), None)


def over_ctx_send(buffer):
    return lax.all_to_all(buffer, "ctx", split_axis=0, concat_axis=0, tiled=True)


def over_exp_send(buffer):
    return lax.all_to_all(buffer, "exp", split_axis=1, concat_axis=1, tiled=True)


def over_exp_back(buffer):
    return lax.all_to_all(buffer, "exp", split_axis=1, concat_axis=1, tiled=True)


def over_ctx_back(buffer):
    return lax.all_to_all(buffer, "ctx", split_axis=0, concat_axis=0, tiled=True)


def expert_rows(received, gate_weights, up_weights, down_weights, capacity, model_width):
    local_experts = gate_weights.shape[0]
    senders = received.shape[0] * received.shape[1]
    shaped = received.reshape(senders, local_experts, capacity, model_width)
    shaped = jnp.moveaxis(shaped, 1, 0).reshape(local_experts, senders * capacity, model_width)
    gate_part = jnp.einsum("jrd,jdf->jrf", shaped, gate_weights, preferred_element_type=jnp.float32)
    up_part = jnp.einsum("jrd,jdf->jrf", shaped, up_weights, preferred_element_type=jnp.float32)
    active = (jax.nn.silu(gate_part) * up_part).astype(jnp.bfloat16)
    produced = jnp.einsum(
        "jrf,jfd->jrd", active, down_weights, preferred_element_type=jnp.float32
    ).astype(jnp.bfloat16)
    produced = jnp.moveaxis(produced.reshape(local_experts, senders, capacity, model_width), 0, 1)
    return produced.reshape(received.shape)


def body(
    queries,
    key_vectors,
    values,
    out_gate,
    write_strength,
    log_fading_factor,
    block_inverse,
    norm_gain,
    hidden,
    routes,
    route_weights,
    gate_weights,
    up_weights,
    down_weights,
):
    tracks, length, head_width = queries.shape
    pieces = block_parts(
        queries, key_vectors, values, write_strength, log_fading_factor, block_inverse
    )
    faded_queries, write_keys, write_values, faded_keys, causal, decays = pieces
    unit_matrix = jnp.eye(head_width, dtype=jnp.float32)
    identity_map = jnp.broadcast_to(unit_matrix, (tracks, head_width, head_width))
    block_maps = decays[..., None] * unit_matrix - jnp.einsum(
        "sbch,sbck->sbhk", faded_keys, write_keys, precision=TOP_PRECISION
    )
    block_adds = jnp.einsum("sbch,sbcv->sbhv", faded_keys, write_values, precision=TOP_PRECISION)
    (section_mapping, section_addend), _ = lax.scan(
        compose,
        (identity_map, jnp.zeros_like(identity_map)),
        (jnp.moveaxis(block_maps, 1, 0), jnp.moveaxis(block_adds, 1, 0)),
    )
    incoming_state = jnp.zeros_like(section_addend)
    for relay_turn in range(lax.axis_size("ctx") - 1):
        departing_state = (
            jnp.einsum("qfz,qze->qfe", section_mapping, incoming_state, precision=TOP_PRECISION)
            + section_addend
        )
        incoming_state = passed_along(departing_state.astype(jnp.bfloat16), "ctx", 1).astype(
            departing_state.dtype
        )
    _, attended = run_blocks(pieces, incoming_state)
    mixer_output = gated_norm(attended.reshape(tracks, length, head_width), norm_gain, out_gate)
    token_rows, model_width = hidden.shape
    top_count = routes.shape[1]
    local_experts = gate_weights.shape[0]
    context_size = lax.axis_size("ctx")
    owner_count = lax.axis_size("exp")
    experts = local_experts * context_size * owner_count
    capacity = max(2, (token_rows * top_count * 6 + experts * 5 - 1) // (experts * 5))
    expert_ids = lax.broadcasted_iota(jnp.int32, (1, experts), 1)
    named_count = jnp.zeros((token_rows, experts), jnp.int32)
    for pick_index in range(top_count):
        named_count = named_count + (routes[:, pick_index, None] == expert_ids).astype(jnp.int32)
    earlier = jnp.cumsum(named_count, axis=0) - named_count
    slot_rank = jnp.take_along_axis(earlier, routes, axis=1)
    slot_index = routes * capacity + slot_rank
    token_ids = lax.broadcasted_iota(jnp.int32, (token_rows, top_count), 0)
    slot_token = (
        jnp.zeros((experts * capacity,), jnp.int32)
        .at[slot_index.reshape(-1)]
        .set(token_ids.reshape(-1))
    )
    outgoing = hidden[slot_token]
    outgoing = outgoing.reshape(context_size, owner_count, local_experts * capacity * model_width)
    received = over_exp_send(over_ctx_send(outgoing))
    produced = expert_rows(received, gate_weights, up_weights, down_weights, capacity, model_width)
    returned = over_ctx_back(over_exp_back(produced))
    returned = returned.reshape(experts * capacity, model_width)
    summed = jnp.zeros((token_rows, model_width), jnp.float32)
    for pick_index in range(top_count):
        summed = summed + route_weights[:, pick_index, None] * returned[
            slot_index[:, pick_index]
        ].astype(jnp.float32)
    expert_output = summed.astype(jnp.bfloat16)
    return (mixer_output, expert_output)


def solution(mesh):
    placed = (
        P("exp", "ctx", None),
        P("exp", "ctx", None),
        P("exp", "ctx", None),
        P("exp", "ctx", None),
        P("exp", "ctx"),
        P("exp", "ctx"),
        P("exp", "ctx", None, None),
        P(),
        P(("ctx", "exp"), None),
        P(("ctx", "exp"), None),
        P(("ctx", "exp"), None),
        P(("ctx", "exp"), None, None),
        P(("ctx", "exp"), None, None),
        P(("ctx", "exp"), None, None),
    )
    return jax.shard_map(
        body,
        mesh=mesh,
        in_specs=placed,
        out_specs=(P("exp", "ctx", None), P(("ctx", "exp"), None)),
        check_vma=False,
    )
```

profile of v0, /device:TPU:40, one launch (start us, length us, event | category | flops | bytes accessed | tf_op | source)
XLA Modules:
  0.0 395.5 jit_solution(14602041467640665971)
XLA Ops:
  0.6 1.0 slice_bitcast_fusion.18
  3.5 10.1 %gather_fusion.11 = s32[1280]{0:T(1024)S(1)} fusion(s32[128,512]{1,0:T(8,128)S(1)} %fusion.93, s32[1280]{0:T(1024)S(1)} %reshape.538), kind=kCustom, calls=%fused_computation.11 | custom fusion | bytes 20480 | tf_op jit(solution)/shard_map/jit(take_along_axis)/gather | solution.py:176
  14.3 5.2 %scatter_custom_fusion = s32[1536]{0:T(1024)S(1)} fusion(s32[1280]{0:T(1024)S(1)} %fusion.77, s32[1280]{0:T(1024)S(1)} %reshape.548, s32[]{:T(128)} %copy.125), kind=kCustom, calls=%fused_computation.143 | custom fusion | bytes 6148 | tf_op jit(solution)/shard_map/scatter | solution.py:182
  19.6 5.8 %gather_fusion = bf16[1536,1024]{1,0:T(8,128)(2,1)} fusion(bf16[128,1024]{1,0:T(8,128)(2,1)S(1)} %copy-done.1, s32[2048]{0:T(1024)S(1)} %pad_clamp_fusion), kind=kCustom, calls=%fused_computation | custom fusion | bytes 6297600 | tf_op jit(solution)/shard_map/gather | solution.py:184
  25.5 5.8 %reshape.444 = bf16[8,64,3072]{2,1,0:T(8,128)(2,1)} reshape(bf16[1536,1024]{1,0:T(8,128)(2,1)} %gather_fusion) | data formatting | bytes 6291456 | tf_op jit(solution)/shard_map/reshape | solution.py:185
  31.3 43.2 %all_to_all.20 = bf16[8,64,3072]{2,1,0:T(8,128)(2,1)S(1)} all-to-all(bf16[8,64,3072]{2,1,0:T(8,128)(2,1)} %reshape.444), channel_id=1, replica_groups=mesh['ctx'=8,'exp'=64] {'ctx'}, dimensions={0} | all-to-all | bytes 6291456 | tf_op jit(solution)/shard_map/all_to_all | solution.py:91
  74.5 1.7 copy.100
  76.2 92.3 %all_to_all.21 = bf16[8,64,3072]{2,0,1:T(8,128)(2,1)S(1)} all-to-all(bf16[8,64,3072]{2,0,1:T(8,128)(2,1)S(1)} %copy.100), channel_id=1, replica_groups=mesh['ctx'=8,'exp'=64] {'exp'}, dimensions={1} | all-to-all | bytes 6291456 | tf_op jit(solution)/shard_map/all_to_all | solution.py:95
  168.5 3.4 copy.101
  171.9 5.9 %reshape.445 = bf16[1536,1024]{1,0:T(8,128)(2,1)} reshape(bf16[8,64,3072]{2,1,0:T(8,128)(2,1)} %copy.101) | data formatting | bytes 6291456 | tf_op jit(solution)/shard_map/reshape.83
  177.8 5.5 %fusion.47 = f32[1536,512]{1,0:T(8,128)} fusion(bf16[1536,1024]{1,0:T(8,128)(2,1)} %reshape.445, bf16[1,1024,512]{2,1,0:T(8,128)(2,1)S(1)} %copy-done.12), kind=kOutput, calls=%fused_computation.77 | convolution fusion | flops 1610612736 | bytes 7340032 | tf_op jit(solution)/shard_map/jrd,jdf->jrf/dot_general | solution.py:111
  183.3 8.3 %convolution_convert_fusion = bf16[1536,1024]{1,0:T(8,128)(2,1)} fusion(bf16[1536,1024]{1,0:T(8,128)(2,1)} %reshape.445, f32[1536,512]{1,0:T(8,128)} %fusion.47, bf16[1,512,1024]{2,1,0:T(8,128)(2,1)S(1)} %copy-done, bf16[1,1024,512]{2,1,0:T(8,128)(2,1)S(1)} %copy-done.13), kind=kOutput, calls=%fused_computation.46 | convolution fusion | flops 3227516928 | bytes 11534336 | tf_op jit(solution)/shard_map/jrf,jfd->jrd/dot_general | solution.py:114
  191.6 5.9 %reshape_transpose_reshape.4 = bf16[8,64,3072]{2,1,0:T(8,128)(2,1)} reshape(bf16[1536,1024]{1,0:T(8,128)(2,1)} %convolution_convert_fusion) | data formatting | bytes 6291456 | tf_op jit(solution)/shard_map/reshape;transpose;reshape | solution.py:118
  197.5 5.3 %copy.102 = bf16[8,64,3072]{2,0,1:T(8,128)(2,1)} copy(bf16[8,64,3072]{2,1,0:T(8,128)(2,1)} %reshape_transpose_reshape.4) | data formatting | bytes 6291456 | tf_op jit(solution)/shard_map/reshape;transpose;reshape | solution.py:118
  202.8 9.1 %all-to-all-start.2 = ((bf16[8,64,3072]{2,0,1:T(8,128)(2,1)}), bf16[8,64,3072]{2,0,1:T(8,128)(2,1)}, u32[]{:S(2)}, u32[]{:S(2)}) async-start(bf16[8,64,3072]{2,0,1:T(8,128)(2,1)} %copy.102), calls=%async_computation.2 | async-start | bytes 6291456 | tf_op jit(solution)/shard_map/all_to_all | solution.py:99
  216.6 1.9 while.24
  218.7 1.3 collective-permute-start
  221.0 3.4 collective-permute-start.1
  225.4 4.4 %collective-permute-start.2 = (bf16[1,128,128]{2,1,0:T(8,128)(2,1)S(1)}, bf16[1,128,128]{2,1,0:T(8,128)(2,1)S(1)}, u32[]{:S(2)}, u32[]{:S(2)}) collective-permute-start(bf16[1,128,128]{2,1,0:T(8,128)(2,1)S(1)} %fusion.41), channel_id=1, source_target_pairs={{0,64},{64,128},{128,192},{192,256},{256,320},{320,384},{384,448},... | collective-permute-start | bytes 98312 | tf_op jit(solution)/shard_map/ppermute | solution.py:13
  229.8 0.8 collective-permute-done.2
  230.8 4.4 %collective-permute-start.3 = (bf16[1,128,128]{2,1,0:T(8,128)(2,1)S(1)}, bf16[1,128,128]{2,1,0:T(8,128)(2,1)S(1)}, u32[]{:S(2)}, u32[]{:S(2)}) collective-permute-start(bf16[1,128,128]{2,1,0:T(8,128)(2,1)S(1)} %fusion.40), channel_id=1, source_target_pairs={{0,64},{64,128},{128,192},{192,256},{256,320},{320,384},{384,448},... | collective-permute-start | bytes 98312 | tf_op jit(solution)/shard_map/ppermute | solution.py:13
  235.2 0.8 collective-permute-done.3
  236.2 4.4 %collective-permute-start.4 = (bf16[1,128,128]{2,1,0:T(8,128)(2,1)S(1)}, bf16[1,128,128]{2,1,0:T(8,128)(2,1)S(1)}, u32[]{:S(2)}, u32[]{:S(2)}) collective-permute-start(bf16[1,128,128]{2,1,0:T(8,128)(2,1)S(1)} %fusion.39), channel_id=1, source_target_pairs={{0,64},{64,128},{128,192},{192,256},{256,320},{320,384},{384,448},... | collective-permute-start | bytes 98312 | tf_op jit(solution)/shard_map/ppermute | solution.py:13
  240.6 0.8 collective-permute-done.4
  241.7 4.4 %collective-permute-start.5 = (bf16[1,128,128]{2,1,0:T(8,128)(2,1)S(1)}, bf16[1,128,128]{2,1,0:T(8,128)(2,1)S(1)}, u32[]{:S(2)}, u32[]{:S(2)}) collective-permute-start(bf16[1,128,128]{2,1,0:T(8,128)(2,1)S(1)} %fusion.38), channel_id=1, source_target_pairs={{0,64},{64,128},{128,192},{192,256},{256,320},{320,384},{384,448},... | collective-permute-start | bytes 98312 | tf_op jit(solution)/shard_map/ppermute | solution.py:13
  246.1 0.8 collective-permute-done.5
  247.1 4.4 %collective-permute-start.6 = (bf16[1,128,128]{2,1,0:T(8,128)(2,1)S(1)}, bf16[1,128,128]{2,1,0:T(8,128)(2,1)S(1)}, u32[]{:S(2)}, u32[]{:S(2)}) collective-permute-start(bf16[1,128,128]{2,1,0:T(8,128)(2,1)S(1)} %fusion.37), channel_id=1, source_target_pairs={{0,64},{64,128},{128,192},{192,256},{256,320},{320,384},{384,448},... | collective-permute-start | bytes 98312 | tf_op jit(solution)/shard_map/ppermute | solution.py:13
  252.3 52.8 %all-to-all-done.2 = bf16[8,64,3072]{2,0,1:T(8,128)(2,1)} async-done(((bf16[8,64,3072]{2,0,1:T(8,128)(2,1)}), bf16[8,64,3072]{2,0,1:T(8,128)(2,1)}, u32[]{:S(2)}, u32[]{:S(2)}) %all-to-all-start.2) | async-done | bytes 3145760 | tf_op jit(solution)/shard_map/all_to_all | solution.py:99
  305.1 5.3 %copy.103 = bf16[8,64,3072]{2,1,0:T(8,128)(2,1)} copy(bf16[8,64,3072]{2,0,1:T(8,128)(2,1)} %all-to-all-done.2) | data formatting | bytes 6291456 | tf_op jit(solution)/shard_map/all_to_all | solution.py:99
  310.4 4.4 %all-to-all-start.3 = ((bf16[8,64,3072]{2,1,0:T(8,128)(2,1)}), bf16[8,64,3072]{2,1,0:T(8,128)(2,1)}, u32[]{:S(2)}, u32[]{:S(2)}) async-start(bf16[8,64,3072]{2,1,0:T(8,128)(2,1)} %copy.103), calls=%async_computation.3 | async-start | bytes 6291456 | tf_op jit(solution)/shard_map/all_to_all | solution.py:103
  314.9 8.5 %while.25 = (s32[]{:T(128)}, f32[1,128,128]{2,1,0:T(8,128)S(1)}, f32[4,1,64,128]{3,2,1,0:T(8,128)S(1)}, f32[4,1,1]{0,2,1:T(1,128)S(1)}, f32[4,1,64,128]{3,2,1,0:...) while((s32[]{:T(128)}, f32[1,128,128]{2,1,0:T(8,128)S(1)}, ...), condition=%wide.region_4.5_spmd, body=%wide.region_3.4_spmd.sunk | while | flops 44089344 | bytes 624765 | solution.py:68
  316.0 0.9 fusion.131
  318.2 0.9 fusion.131
  320.3 0.9 fusion.131
  322.4 0.9 fusion.131
  324.3 29.0 %all-to-all-done.3 = bf16[8,64,3072]{2,1,0:T(8,128)(2,1)} async-done(((bf16[8,64,3072]{2,1,0:T(8,128)(2,1)}), bf16[8,64,3072]{2,1,0:T(8,128)(2,1)}, u32[]{:S(2)}, u32[]{:S(2)}) %all-to-all-start.3) | async-done | bytes 3145760 | tf_op jit(solution)/shard_map/all_to_all | solution.py:103
  353.3 5.8 %reshape.449 = bf16[1536,1024]{1,0:T(8,128)(2,1)} reshape(bf16[8,64,3072]{2,1,0:T(8,128)(2,1)} %all-to-all-done.3) | data formatting | bytes 6291456 | tf_op jit(solution)/shard_map/reshape | solution.py:189
  359.1 3.3 gather_fusion.1
  362.5 3.3 gather_fusion.2
  365.8 3.3 gather_fusion.3
  369.1 3.3 gather_fusion.4
  372.5 3.3 gather_fusion.5
  375.8 3.3 gather_fusion.6
  379.2 3.3 gather_fusion.7
  382.5 3.3 gather_fusion.8
  385.9 3.3 gather_fusion.9
  389.2 4.0 %gather_fusion.10 = bf16[128,1024]{1,0:T(8,128)(2,1)} fusion(bf16[1536,1024]{1,0:T(8,128)(2,1)} %reshape.449, s32[1024]{0:T(1024)S(1)} %get-tuple-element.243), kind=kCustom, calls=%fused_computation.10 | custom fusion | bytes 524800 | tf_op jit(solution)/shard_map/gather | solution.py:192
  393.2 2.2 add_convert_fusion
  (117 shorter events, 18.1 us)
Async XLA Ops:
  0.6 182.7 %copy-start = (bf16[1,512,1024]{2,1,0:T(8,128)(2,1)S(1)}, bf16[1,512,1024]{2,1,0:T(8,128)(2,1)}, u32[]{:S(2)}) copy-start(bf16[1,512,1024]{2,1,0:T(8,128)(2,1)} %param.31) | copy-start | bytes 3145732
  3.5 10.4 %copy-start.7 = (s32[128,10]{0,1:T(8,128)S(1)}, s32[128,10]{0,1:T(8,128)}, u32[]{:S(2)}) copy-start(s32[128,10]{0,1:T(8,128)} %param.27) | copy-start | bytes 15364
  13.7 6.0 %copy-start.1 = (bf16[128,1024]{1,0:T(8,128)(2,1)S(1)}, bf16[128,1024]{1,0:T(8,128)(2,1)}, u32[]{:S(2)}) copy-start(bf16[128,1024]{1,0:T(8,128)(2,1)} %param.26) | copy-start | bytes 786436
  171.9 6.0 %copy-start.12 = (bf16[1,1024,512]{2,1,0:T(8,128)(2,1)S(1)}, bf16[1,1024,512]{2,1,0:T(8,128)(2,1)}, u32[]{:S(2)}) copy-start(bf16[1,1024,512]{2,1,0:T(8,128)(2,1)} %param.29) | copy-start | bytes 3145732
  177.8 5.5 %copy-start.13 = (bf16[1,1024,512]{2,1,0:T(8,128)(2,1)S(1)}, bf16[1,1024,512]{2,1,0:T(8,128)(2,1)}, u32[]{:S(2)}) copy-start(bf16[1,1024,512]{2,1,0:T(8,128)(2,1)} %param.30) | copy-start | bytes 3145732
  202.8 9.7 %copy-start.9 = (f32[1,256]{1,0:T(1,128)S(1)}, f32[1,256]{1,0:T(1,128)}, u32[]{:S(2)}) copy-start(f32[1,256]{1,0:T(1,128)} %param.23) | copy-start | bytes 3076
  202.8 10.4 %copy-start.10 = (f32[1,256]{1,0:T(1,128)S(1)}, f32[1,256]{1,0:T(1,128)}, u32[]{:S(2)}) copy-start(f32[1,256]{1,0:T(1,128)} %param.22) | copy-start | bytes 3076
  202.8 11.7 %copy-start.3 = (f32[1,4,64,64]{3,2,1,0:T(8,128)S(1)}, f32[1,4,64,64]{3,2,1,0:T(8,128)}, u32[]{:S(2)}) copy-start(f32[1,4,64,64]{3,2,1,0:T(8,128)} %param.24) | copy-start | bytes 196612
  202.8 11.7 %copy-start.5 = (f32[1,256,128]{2,1,0:T(8,128)S(1)}, f32[1,256,128]{2,1,0:T(8,128)}, u32[]{:S(2)}) copy-start(f32[1,256,128]{2,1,0:T(8,128)} %param.20) | copy-start | bytes 393220
  202.8 12.1 %copy-start.2 = (f32[1,256,128]{2,1,0:T(8,128)S(1)}, f32[1,256,128]{2,1,0:T(8,128)}, u32[]{:S(2)}) copy-start(f32[1,256,128]{2,1,0:T(8,128)} %param.19) | copy-start | bytes 393220
  202.8 102.3 %all-to-all-start.2 = ((bf16[8,64,3072]{2,0,1:T(8,128)(2,1)}), bf16[8,64,3072]{2,0,1:T(8,128)(2,1)}, u32[]{:S(2)}, u32[]{:S(2)}) async-start(bf16[8,64,3072]{2,0,1:T(8,128)(2,1)} %copy.102), calls=%async_computation.2 | async-start | bytes 6291456 | tf_op jit(solution)/shard_map/all_to_all | solution.py:99
  211.9 8.1 %copy-start.8 = (f32[128,10]{0,1:T(8,128)S(1)}, f32[128,10]{0,1:T(8,128)}, u32[]{:S(2)}) copy-start(f32[128,10]{0,1:T(8,128)} %param.28) | copy-start | bytes 15364
  211.9 8.1 %copy-start.4 = (f32[1,256,128]{2,1,0:T(8,128)S(1)}, f32[1,256,128]{2,1,0:T(8,128)}, u32[]{:S(2)}) copy-start(f32[1,256,128]{2,1,0:T(8,128)} %param.18) | copy-start | bytes 393220
  218.7 2.1 collective-permute-start
  221.0 4.2 %collective-permute-start.1 = (bf16[1,128,128]{2,1,0:T(8,128)(2,1)S(1)}, bf16[1,128,128]{2,1,0:T(8,128)(2,1)S(1)}, u32[]{:S(2)}, u32[]{:S(2)}) collective-permute-start(bf16[1,128,128]{2,1,0:T(8,128)(2,1)S(1)} %fusion.42), channel_id=1, source_target_pairs={{0,64},{64,128},{128,192},{192,256},{256,320},{320,384},{384,448},... | collective-permute-start | bytes 98312 | tf_op jit(solution)/shard_map/ppermute | solution.py:13
  225.4 5.2 %collective-permute-start.2 = (bf16[1,128,128]{2,1,0:T(8,128)(2,1)S(1)}, bf16[1,128,128]{2,1,0:T(8,128)(2,1)S(1)}, u32[]{:S(2)}, u32[]{:S(2)}) collective-permute-start(bf16[1,128,128]{2,1,0:T(8,128)(2,1)S(1)} %fusion.41), channel_id=1, source_target_pairs={{0,64},{64,128},{128,192},{192,256},{256,320},{320,384},{384,448},... | collective-permute-start | bytes 98312 | tf_op jit(solution)/shard_map/ppermute | solution.py:13
  230.8 5.2 %collective-permute-start.3 = (bf16[1,128,128]{2,1,0:T(8,128)(2,1)S(1)}, bf16[1,128,128]{2,1,0:T(8,128)(2,1)S(1)}, u32[]{:S(2)}, u32[]{:S(2)}) collective-permute-start(bf16[1,128,128]{2,1,0:T(8,128)(2,1)S(1)} %fusion.40), channel_id=1, source_target_pairs={{0,64},{64,128},{128,192},{192,256},{256,320},{320,384},{384,448},... | collective-permute-start | bytes 98312 | tf_op jit(solution)/shard_map/ppermute | solution.py:13
  236.2 5.2 %collective-permute-start.4 = (bf16[1,128,128]{2,1,0:T(8,128)(2,1)S(1)}, bf16[1,128,128]{2,1,0:T(8,128)(2,1)S(1)}, u32[]{:S(2)}, u32[]{:S(2)}) collective-permute-start(bf16[1,128,128]{2,1,0:T(8,128)(2,1)S(1)} %fusion.39), channel_id=1, source_target_pairs={{0,64},{64,128},{128,192},{192,256},{256,320},{320,384},{384,448},... | collective-permute-start | bytes 98312 | tf_op jit(solution)/shard_map/ppermute | solution.py:13
  241.7 5.2 %collective-permute-start.5 = (bf16[1,128,128]{2,1,0:T(8,128)(2,1)S(1)}, bf16[1,128,128]{2,1,0:T(8,128)(2,1)S(1)}, u32[]{:S(2)}, u32[]{:S(2)}) collective-permute-start(bf16[1,128,128]{2,1,0:T(8,128)(2,1)S(1)} %fusion.38), channel_id=1, source_target_pairs={{0,64},{64,128},{128,192},{192,256},{256,320},{320,384},{384,448},... | collective-permute-start | bytes 98312 | tf_op jit(solution)/shard_map/ppermute | solution.py:13
  247.1 5.2 %collective-permute-start.6 = (bf16[1,128,128]{2,1,0:T(8,128)(2,1)S(1)}, bf16[1,128,128]{2,1,0:T(8,128)(2,1)S(1)}, u32[]{:S(2)}, u32[]{:S(2)}) collective-permute-start(bf16[1,128,128]{2,1,0:T(8,128)(2,1)S(1)} %fusion.37), channel_id=1, source_target_pairs={{0,64},{64,128},{128,192},{192,256},{256,320},{320,384},{384,448},... | collective-permute-start | bytes 98312 | tf_op jit(solution)/shard_map/ppermute | solution.py:13
  310.4 42.9 %all-to-all-start.3 = ((bf16[8,64,3072]{2,1,0:T(8,128)(2,1)}), bf16[8,64,3072]{2,1,0:T(8,128)(2,1)}, u32[]{:S(2)}, u32[]{:S(2)}) async-start(bf16[8,64,3072]{2,1,0:T(8,128)(2,1)} %copy.103), calls=%async_computation.3 | async-start | bytes 6291456 | tf_op jit(solution)/shard_map/all_to_all | solution.py:103
  314.9 8.7 %copy-start.6 = (f32[1,256,128]{2,1,0:T(8,128)S(1)}, f32[1,256,128]{2,1,0:T(8,128)}, u32[]{:S(2)}) copy-start(f32[1,256,128]{2,1,0:T(8,128)} %param.21) | copy-start | bytes 393220
  314.9 8.7 %copy-start.11 = (f32[128]{0:T(128)S(1)}, f32[128]{0:T(128)}, u32[]{:S(2)}) copy-start(f32[128]{0:T(128)} %param.25) | copy-start | bytes 1540
where the time goes:
time: 397 us; the launch traced here: 395 us
  blocking collectives  135 us (34%)
  local copies, waits for them, and re-layouts  99.8 us (25%)
  waiting for transfers between devices  87 us (22%)
  starting transfers between devices  40.1 us (10%)
  matrix products  24.9 us (6%)
  other arithmetic  6.6 us (2%)
    all_to_all x1, blocking collectives, over_exp_send(): lax.all_to_all(buffer, 'exp', split_axis=1, concat_axis=1, tiled=True)  92.3 us
    all_to_all x1, waiting for transfers between devices, over_exp_back(): lax.all_to_all(buffer, 'exp', split_axis=1, concat_axis=1, tiled=True)  52.8 us
    all_to_all x1, blocking collectives, over_ctx_send(): lax.all_to_all(buffer, 'ctx', split_axis=0, concat_axis=0, tiled=True)  43.2 us
    gather x10, local copies, waits for them, and re-layouts, body(): returned[slot_index[:, pick_index]].astype(jnp.float32)  34.1 us
    all_to_all x1, waiting for transfers between devices, over_ctx_back(): lax.all_to_all(buffer, 'ctx', split_axis=0, concat_axis=0, tiled=True)  29 us
    ppermute x7, starting transfers between devices, passed_along(): return lax.ppermute(block, axis, route)  26.6 us
    another operation x2, local copies, waits for them, and re-layouts, expert_rows(): return produced.reshape(received.shape)  11.2 us
    gather x5, local copies, waits for them, and re-layouts, body(): slot_rank = jnp.take_along_axis(earlier, routes, axis=1)  10.6 us
  transfers between devices with their start and end apart: 9, of which 9 were waited for; matrix products, arithmetic and copies ran while one was open for 4% of the time, Pallas kernels for 0%

commit v1 on v0

v1 whole, which is shorter than its diff:
```python
import functools

import jax
import jax.numpy as jnp
from jax import lax
from jax.experimental import pallas as pl
from jax.experimental.pallas import tpu as pltpu
from jax.sharding import PartitionSpec as P

TOP_PRECISION = lax.Precision.HIGHEST
NORM_EPSILON = 1e-06
CAPACITY = 3
LANES = 128


def passed_along(block, axis, distance):
    devices = range(lax.axis_size(axis))
    route = [(i - distance, i) for i in devices if i - distance in devices]
    return lax.ppermute(block, axis, route)


def block_parts(queries, key_vectors, values, write_strength, log_fading_factor, block_inverse):
    tracks, length, head_width = queries.shape
    block_size = block_inverse.shape[-1]
    blocks = length // block_size
    shape_four = (tracks, blocks, block_size, head_width)
    query_blocks = queries.reshape(shape_four)
    key_blocks = key_vectors.reshape(shape_four)
    value_blocks = values.reshape(shape_four)
    strength = write_strength.reshape(tracks, blocks, block_size)
    running = jnp.cumsum(log_fading_factor.reshape(tracks, blocks, block_size), axis=-1)
    growth = jnp.exp(running)
    final_log = running[..., -1:]
    write_keys = jnp.einsum(
        "sbij,sbjh->sbih",
        block_inverse,
        key_blocks * (strength * growth)[..., None],
        precision=TOP_PRECISION,
    )
    write_values = jnp.einsum(
        "sbij,sbjh->sbih",
        block_inverse,
        value_blocks * strength[..., None],
        precision=TOP_PRECISION,
    )
    faded_keys = key_blocks * jnp.exp(final_log - running)[..., None]
    faded_queries = query_blocks * growth[..., None]
    row_index = lax.broadcasted_iota(jnp.int32, (block_size, block_size), 0)
    col_index = lax.broadcasted_iota(jnp.int32, (block_size, block_size), 1)
    spread = running[..., :, None] - running[..., None, :]
    causal_fade = jnp.where(row_index >= col_index, jnp.exp(jnp.minimum(spread, 0.0)), 0.0)
    causal = (
        jnp.einsum("sbih,sbjh->sbij", query_blocks, key_blocks, precision=TOP_PRECISION)
        * causal_fade
    )
    return (faded_queries, write_keys, write_values, faded_keys, causal, jnp.exp(final_log))


def block_step(states, pieces):
    faded_queries, write_keys, write_values, faded_keys, causal, decays = pieces
    fresh_values = write_values - jnp.einsum(
        "sch,shv->scv", write_keys, states, precision=TOP_PRECISION
    )
    attended = jnp.einsum("sch,shv->scv", faded_queries, states, precision=TOP_PRECISION)
    attended = attended + jnp.einsum("sij,sjv->siv", causal, fresh_values, precision=TOP_PRECISION)
    states = decays[..., None] * states + jnp.einsum(
        "sch,scv->shv", faded_keys, fresh_values, precision=TOP_PRECISION
    )
    return (states, attended)


def run_blocks(pieces, states):
    moved = tuple((jnp.moveaxis(piece_item, 1, 0) for piece_item in pieces))
    states, attended = lax.scan(block_step, states, moved)
    return (states, jnp.moveaxis(attended, 0, 1))


def gated_norm(attended, norm_gain, out_gate):
    root_mean = jnp.sqrt(jnp.mean(attended * attended, axis=-1, keepdims=True) + NORM_EPSILON)
    return attended / root_mean * norm_gain * jax.nn.silu(out_gate)


def compose(carried, block_piece):
    current_mapping, current_addend = carried
    segment_mapping, segment_addend = block_piece
    updated_mapping = jnp.einsum(
        "qfz,qze->qfe", segment_mapping, current_mapping, precision=TOP_PRECISION
    )
    updated_addend = (
        jnp.einsum("qfz,qze->qfe", segment_mapping, current_addend, precision=TOP_PRECISION)
        + segment_addend
    )
    return ((updated_mapping, updated_addend), None)


def delta_net(
    queries, key_vectors, values, out_gate, write_strength, log_fading_factor, block_inverse, norm_gain
):
    tracks, length, head_width = queries.shape
    pieces = block_parts(
        queries, key_vectors, values, write_strength, log_fading_factor, block_inverse
    )
    faded_queries, write_keys, write_values, faded_keys, causal, decays = pieces
    unit_matrix = jnp.eye(head_width, dtype=jnp.float32)
    identity_map = jnp.broadcast_to(unit_matrix, (tracks, head_width, head_width))
    block_maps = decays[..., None] * unit_matrix - jnp.einsum(
        "sbch,sbck->sbhk", faded_keys, write_keys, precision=TOP_PRECISION
    )
    block_adds = jnp.einsum("sbch,sbcv->sbhv", faded_keys, write_values, precision=TOP_PRECISION)
    (section_mapping, section_addend), _ = lax.scan(
        compose,
        (identity_map, jnp.zeros_like(identity_map)),
        (jnp.moveaxis(block_maps, 1, 0), jnp.moveaxis(block_adds, 1, 0)),
    )
    incoming_state = jnp.zeros_like(section_addend)
    for relay_turn in range(lax.axis_size("ctx") - 1):
        departing_state = (
            jnp.einsum("qfz,qze->qfe", section_mapping, incoming_state, precision=TOP_PRECISION)
            + section_addend
        )
        incoming_state = passed_along(departing_state.astype(jnp.bfloat16), "ctx", 1).astype(
            departing_state.dtype
        )
    _, attended = run_blocks(pieces, incoming_state)
    return gated_norm(attended.reshape(tracks, length, head_width), norm_gain, out_gate)


def named_and_rank(ranks, first, count, tokens):
    row = lax.broadcasted_iota(jnp.int32, (count, tokens), 0) + first
    named = jnp.zeros((count, tokens), jnp.bool_)
    for pick in range(ranks.shape[0]):
        named = jnp.logical_or(named, ranks[pick : pick + 1, :] == row)
    before = lax.broadcasted_iota(jnp.int32, (tokens, tokens), 0) < lax.broadcasted_iota(
        jnp.int32, (tokens, tokens), 1
    )
    earlier = jnp.dot(
        named.astype(jnp.float32).astype(jnp.bfloat16),
        before.astype(jnp.float32).astype(jnp.bfloat16),
        preferred_element_type=jnp.float32,
    )
    return named, earlier


def pack_kernel(ranks_ref, hidden_ref, out_ref, spread_ref):
    tokens, width = hidden_ref.shape
    parts = width // LANES
    per = CAPACITY * parts
    count = out_ref.shape[0] // per
    named, earlier = named_and_rank(
        ranks_ref[...], pl.program_id(0) * count, count, tokens
    )
    for slot in range(CAPACITY):
        chosen = jnp.where(jnp.logical_and(named, earlier == slot), 1.0, 0.0).astype(jnp.bfloat16)
        rows = jnp.dot(chosen, hidden_ref[...], preferred_element_type=jnp.float32)
        for part in range(parts):
            spread_ref[pl.ds(slot * parts + part, count, stride=per), :] = rows[
                :, part * LANES : (part + 1) * LANES
            ]
    out_ref[...] = spread_ref[...].astype(jnp.bfloat16)


def pack_rows(ranks, hidden, experts, steps):
    tokens, width = hidden.shape
    rows = experts * CAPACITY * width // LANES
    return pl.pallas_call(
        pack_kernel,
        grid=(steps,),
        out_shape=jax.ShapeDtypeStruct((rows, LANES), jnp.bfloat16),
        in_specs=[
            pl.BlockSpec(ranks.shape, lambda i: (0, 0)),
            pl.BlockSpec(hidden.shape, lambda i: (0, 0)),
        ],
        out_specs=pl.BlockSpec((rows // steps, LANES), lambda i: (i, 0)),
        scratch_shapes=[pltpu.VMEM((rows // steps, LANES), jnp.float32)],
        compiler_params=pltpu.CompilerParams(vmem_limit_bytes=32 * 1024 * 1024),
        cost_estimate=pl.CostEstimate(
            flops=2 * experts * CAPACITY * tokens * width, bytes_accessed=rows * 256, transcendentals=0
        ),
        name="pack_rows",
    )(ranks, hidden)


def weight_kernel(ranks_ref, weights_ref, high_ref, low_ref):
    tokens = ranks_ref.shape[1]
    experts = high_ref.shape[0] // CAPACITY
    ranks = ranks_ref[...]
    named, earlier = named_and_rank(ranks, 0, experts, tokens)
    row = lax.broadcasted_iota(jnp.int32, (experts, tokens), 0)
    scale = jnp.zeros((experts, tokens), jnp.float32)
    for pick in range(ranks.shape[0]):
        scale = jnp.where(ranks[pick : pick + 1, :] == row, weights_ref[pick : pick + 1, :], scale)
    high = scale.astype(jnp.bfloat16).astype(jnp.float32)
    low = scale - high
    for slot in range(CAPACITY):
        here = jnp.logical_and(named, earlier == slot)
        at = pl.ds(slot * experts, experts)
        high_ref[at, :] = jnp.where(here, high, 0.0).astype(jnp.bfloat16)
        low_ref[at, :] = jnp.where(here, low, 0.0).astype(jnp.bfloat16)


def weight_table(ranks, weights, experts):
    tokens = ranks.shape[1]
    shape = jax.ShapeDtypeStruct((CAPACITY * experts, tokens), jnp.bfloat16)
    return pl.pallas_call(
        weight_kernel,
        out_shape=(shape, shape),
        compiler_params=pltpu.CompilerParams(vmem_limit_bytes=32 * 1024 * 1024),
        cost_estimate=pl.CostEstimate(
            flops=40 * experts * tokens, bytes_accessed=4 * CAPACITY * experts * tokens, transcendentals=0
        ),
        name="weight_table",
    )(ranks, weights)


def expert_kernel(received_ref, gate_ref, up_ref, down_ref, out_ref, spread_ref):
    width = gate_ref.shape[0]
    parts = width // LANES
    per = CAPACITY * parts
    count = received_ref.shape[0] // per
    spread_ref[...] = received_ref[...].astype(jnp.float32)
    rows = jnp.concatenate(
        [
            jnp.concatenate(
                [
                    spread_ref[pl.ds(slot * parts + part, count, stride=per), :].astype(jnp.bfloat16)
                    for part in range(parts)
                ],
                axis=1,
            )
            for slot in range(CAPACITY)
        ],
        axis=0,
    )
    gate = jnp.dot(rows, gate_ref[...], preferred_element_type=jnp.float32)
    up = jnp.dot(rows, up_ref[...], preferred_element_type=jnp.float32)
    active = (gate / (1.0 + jnp.exp(-gate)) * up).astype(jnp.bfloat16)
    produced = jnp.dot(active, down_ref[...], preferred_element_type=jnp.float32)
    for slot in range(CAPACITY):
        for part in range(parts):
            spread_ref[pl.ds(slot * parts + part, count, stride=per), :] = produced[
                slot * count : (slot + 1) * count, part * LANES : (part + 1) * LANES
            ]
    out_ref[...] = spread_ref[...].astype(jnp.bfloat16)


def expert_rows(received, gate_weights, up_weights, down_weights, steps):
    rows = received.shape[0]
    width, units = gate_weights.shape
    slots = rows * LANES // width
    block = pl.BlockSpec((rows // steps, LANES), lambda i: (i, 0))
    return pl.pallas_call(
        expert_kernel,
        grid=(steps,),
        out_shape=jax.ShapeDtypeStruct(received.shape, jnp.bfloat16),
        in_specs=[
            block,
            pl.BlockSpec(gate_weights.shape, lambda i: (0, 0)),
            pl.BlockSpec(up_weights.shape, lambda i: (0, 0)),
            pl.BlockSpec(down_weights.shape, lambda i: (0, 0)),
        ],
        out_specs=block,
        scratch_shapes=[pltpu.VMEM((rows // steps, LANES), jnp.float32)],
        compiler_params=pltpu.CompilerParams(vmem_limit_bytes=40 * 1024 * 1024),
        cost_estimate=pl.CostEstimate(
            flops=6 * slots * width * units,
            bytes_accessed=4 * rows * LANES + 6 * width * units,
            transcendentals=slots * units,
        ),
        name="expert_rows",
    )(received, gate_weights, up_weights, down_weights)


def combine_kernel(returned_ref, high_ref, low_ref, out_ref, spread_ref):
    tokens, width = out_ref.shape
    parts = width // LANES
    per = CAPACITY * parts
    count = returned_ref.shape[0] // per
    spread_ref[...] = returned_ref[...].astype(jnp.float32)
    total = jnp.zeros((tokens, width), jnp.float32)
    for slot in range(CAPACITY):
        rows = jnp.concatenate(
            [
                spread_ref[pl.ds(slot * parts + part, count, stride=per), :].astype(jnp.bfloat16)
                for part in range(parts)
            ],
            axis=1,
        )
        at = pl.ds(slot * count, count)
        for table in (high_ref, low_ref):
            total = total + lax.dot_general(
                table[at, :], rows, (((0,), (0,)), ((), ())), preferred_element_type=jnp.float32
            )
    out_ref[...] = total.astype(jnp.bfloat16)


def combine_rows(returned, high, low, tokens, width):
    rows = returned.shape[0]
    return pl.pallas_call(
        combine_kernel,
        out_shape=jax.ShapeDtypeStruct((tokens, width), jnp.bfloat16),
        scratch_shapes=[pltpu.VMEM((rows, LANES), jnp.float32)],
        compiler_params=pltpu.CompilerParams(vmem_limit_bytes=48 * 1024 * 1024),
        cost_estimate=pl.CostEstimate(
            flops=4 * rows * LANES * tokens, bytes_accessed=2 * rows * LANES, transcendentals=0
        ),
        name="combine_rows",
    )(returned, high, low)


def exchange(rows):
    return lax.all_to_all(rows, ("exp", "ctx"), split_axis=0, concat_axis=0, tiled=True)


def body(
    queries,
    key_vectors,
    values,
    out_gate,
    write_strength,
    log_fading_factor,
    block_inverse,
    norm_gain,
    hidden,
    routes,
    route_weights,
    gate_weights,
    up_weights,
    down_weights,
):
    tokens, width = hidden.shape
    context_size = lax.axis_size("ctx")
    owner_count = lax.axis_size("exp")
    experts = context_size * owner_count
    ranks = (routes % owner_count * context_size + routes // owner_count).T
    outgoing = pack_rows(ranks, hidden, experts, 4)
    received = exchange(outgoing)
    produced = expert_rows(received, gate_weights[0], up_weights[0], down_weights[0], 4)
    returned = exchange(produced)
    high, low = weight_table(ranks, route_weights.T, experts)
    expert_output = combine_rows(returned, high, low, tokens, width)
    mixer_output = delta_net(
        queries, key_vectors, values, out_gate, write_strength, log_fading_factor, block_inverse, norm_gain
    )
    return (mixer_output, expert_output)


def solution(mesh):
    placed = (
        P("exp", "ctx", None),
        P("exp", "ctx", None),
        P("exp", "ctx", None),
        P("exp", "ctx", None),
        P("exp", "ctx"),
        P("exp", "ctx"),
        P("exp", "ctx", None, None),
        P(),
        P(("ctx", "exp"), None),
        P(("ctx", "exp"), None),
        P(("ctx", "exp"), None),
        P(("ctx", "exp"), None, None),
        P(("ctx", "exp"), None, None),
        P(("ctx", "exp"), None, None),
    )
    return jax.shard_map(
        body,
        mesh=mesh,
        in_specs=placed,
        out_specs=(P("exp", "ctx", None), P(("ctx", "exp"), None)),
        check_vma=False,
    )
```

time: 397 us -> 211 us (0.53)
  the two profiles are of different devices: /device:TPU:40 before, /device:TPU:1 now
where the time goes in v1:
time: 211 us; the launch traced here: 208 us
  waiting for transfers between devices  72.9 us (35%)
  starting transfers between devices  62.2 us (29%)
  matrix products  33.5 us (16%)
  local copies, waits for them, and re-layouts  15.7 us (7%)
  Pallas kernels  13.9 us (7%)
  other arithmetic  8.22 us (4%)
    all_to_all x2, waiting for transfers between devices, exchange(): lax.all_to_all(rows, ('exp', 'ctx'), split_axis=0, concat_axis=0, tiled=T...  65.3 us
    all_to_all x2, starting transfers between devices, exchange(): lax.all_to_all(rows, ('exp', 'ctx'), split_axis=0, concat_axis=0, tiled=T...  33.5 us
    ppermute x7, starting transfers between devices, passed_along(): return lax.ppermute(block, axis, route)  28.7 us
    unnamed x41, local copies, waits for them, and re-layouts  10.3 us
    ppermute x7, waiting for transfers between devices, passed_along(): return lax.ppermute(block, axis, route)  7.59 us
    dot_general x4, matrix products, block_step(): jnp.einsum('sch,scv->shv', faded_keys, fresh_values, precision=TOP_PRECIS...  6.76 us
    pallas_call x1, Pallas kernels, expert_rows(): pl.pallas_call(expert_kernel, grid=(steps,), out_shape=jax.ShapeDtypeStru...  6.57 us
    dynamic_slice x4, local copies, waits for them, and re-layouts, run_blocks(): states, attended = lax.scan(block_step, states, moved)  4.9 us
  transfers between devices with their start and end apart: 9, of which 7 were waited for; matrix products, arithmetic and copies ran while one was open for 23% of the time, Pallas kernels for 0%

profile of v1, /device:TPU:1, one launch (start us, length us, event | category | flops | bytes accessed | tf_op | source)
XLA Modules:
  0.0 207.6 jit_solution(4140756129295346091)
XLA Ops:
  2.3 3.8 %pack_rows.1 = bf16[12288,128]{1,0:T(8,128)(2,1)} custom-call(s32[10,128]{1,0:T(8,128)S(1)} %fusion.73.ranks_ref, bf16[128,1024]{1,0:T(8,128)(2,1)S(1)} %copy-done.6), custom_call_target="tpu_custom_call" | custom-call | flops 402653184 | bytes 3145728 | tf_op jit(solution)/shard_map/pack_rows/pallas_call | solution.py:165
  6.1 22.2 %all-to-all-start = ((bf16[512,24,128]{2,1,0:T(8,128)(2,1)}), bf16[512,24,128]{2,1,0:T(8,128)(2,1)S(1)}, u32[]{:S(2)}, u32[]{:S(2)}) async-start(bf16[512,24,128]{2,1,0:T(8,128)(2,1)} %bitcast.50), calls=%async_computation | async-start | bytes 6291456 | tf_op jit(solution)/shard_map/all_to_all | solution.py:311
  31.4 1.3 fusion.43
  32.7 1.4 convolution_bitcast_fusion.2
  34.4 1.4 fusion.27
  35.8 8.8 %while.24 = (s32[]{:T(128)}, f32[1,128,128]{2,1,0:T(8,128)S(1)}, f32[1,128,128]{2,1,0:T(8,128)S(1)}, f32[4,1,128,128]{3,2,1,0:T(8,128)}, f32[4,1,128,128]{3,2,1,0:T(8,128)}, /*index=5*/s32[]{:T(128)}) while((s32[]{:T(128)}, f32[1,128,128]{2,1,0:T(8,128)S(1)}, f32[1,128,128]{2,1,0:T(8,128)S(1)}, f32[4,1,128,128]{3,2,1,0:T(8,128)}, ...), condition=%wide.region_2.3_spmd, body=%wide.region_1.2_spmd.sunk | while | flops 50348032 | bytes 722001 | solution.py:110
  35.9 1.0 convolution_bitcast_fusion.11
  36.9 1.1 fusion.106
  38.1 1.0 convolution_bitcast_fusion.11
  39.1 1.1 fusion.106
  40.2 1.0 convolution_bitcast_fusion.11
  41.3 1.1 fusion.106
  42.4 1.0 convolution_bitcast_fusion.11
  43.5 1.1 fusion.106
  44.6 59.3 %all-to-all-done = bf16[512,24,128]{2,1,0:T(8,128)(2,1)S(1)} async-done(((bf16[512,24,128]{2,1,0:T(8,128)(2,1)}), bf16[512,24,128]{2,1,0:T(8,128)(2,1)S(1)}, u32[]{:S(2)}, u32[]{:S(2)}) %all-to-all-start) | async-done | bytes 3145760 | tf_op jit(solution)/shard_map/all_to_all | solution.py:311
  103.9 1.2 copy-done.8
  105.1 1.2 copy-done.9
  106.4 1.2 copy-done.10
  107.6 6.6 %expert_rows.1 = bf16[12288,128]{1,0:T(8,128)(2,1)S(1)} custom-call(bf16[12288,128]{1,0:T(8,128)(2,1)S(1)} %bitcast.215, bf16[1024,512]{1,0:T(8,128)(2,1)S(1)} %bitcast.217, bf16[1024,512]{1,0:T(8,128)(2,1)S(1)} %bitcast.218, bf16[512,1024]{1,0:T(8,128)(2,1)S(1)} %bitcast.219), custom_call_target="tpu_custom_call" | custom-call | flops 4831838208 | bytes 9437184 | tf_op jit(solution)/shard_map/expert_rows/pallas_call | solution.py:251
  114.2 1.6 copy-done.1
  115.8 11.3 %all-to-all-start.1 = ((bf16[512,24,128]{2,1,0:T(8,128)(2,1)}), bf16[512,24,128]{2,1,0:T(8,128)(2,1)S(1)}, u32[]{:S(2)}, u32[]{:S(2)}) async-start(bf16[512,24,128]{2,1,0:T(8,128)(2,1)} %bitcast.214), calls=%async_computation.1 | async-start | bytes 6291456 | tf_op jit(solution)/shard_map/all_to_all | solution.py:311
  127.3 3.5 %collective-permute-start = (bf16[1,128,128]{2,1,0:T(8,128)(2,1)S(1)}, bf16[1,128,128]{2,1,0:T(8,128)(2,1)S(1)}, u32[]{:S(2)}, u32[]{:S(2)}) collective-permute-start(bf16[1,128,128]{2,1,0:T(8,128)(2,1)S(1)} %fusion.42), channel_id=1, source_target_pairs={{0,64},{64,128},{128,192},{192,256},{256,320},{320,384},{384,448},... | collective-permute-start | bytes 98312 | tf_op jit(solution)/shard_map/ppermute | solution.py:19
  130.8 2.7 %collective-permute-done = bf16[1,128,128]{2,1,0:T(8,128)(2,1)S(1)} collective-permute-done((bf16[1,128,128]{2,1,0:T(8,128)(2,1)S(1)}, bf16[1,128,128]{2,1,0:T(8,128)(2,1)S(1)}, u32[]{:S(2)}, u32[]{:S(2)}) %collective-permute-start) | collective-permute-done | bytes 32800 | tf_op jit(solution)/shard_map/ppermute | solution.py:19
  133.7 3.0 %collective-permute-start.1 = (bf16[1,128,128]{2,1,0:T(8,128)(2,1)S(1)}, bf16[1,128,128]{2,1,0:T(8,128)(2,1)S(1)}, u32[]{:S(2)}, u32[]{:S(2)}) collective-permute-start(bf16[1,128,128]{2,1,0:T(8,128)(2,1)S(1)} %fusion.41), channel_id=1, source_target_pairs={{0,64},{64,128},{128,192},{192,256},{256,320},{320,384},{384,448},... | collective-permute-start | bytes 98312 | tf_op jit(solution)/shard_map/ppermute | solution.py:19
  136.7 1.0 collective-permute-done.1
  137.9 4.3 %collective-permute-start.2 = (bf16[1,128,128]{2,1,0:T(8,128)(2,1)S(1)}, bf16[1,128,128]{2,1,0:T(8,128)(2,1)S(1)}, u32[]{:S(2)}, u32[]{:S(2)}) collective-permute-start(bf16[1,128,128]{2,1,0:T(8,128)(2,1)S(1)} %fusion.40), channel_id=1, source_target_pairs={{0,64},{64,128},{128,192},{192,256},{256,320},{320,384},{384,448},... | collective-permute-start | bytes 98312 | tf_op jit(solution)/shard_map/ppermute | solution.py:19
  142.3 1.3 collective-permute-done.2
  143.7 4.6 %collective-permute-start.3 = (bf16[1,128,128]{2,1,0:T(8,128)(2,1)S(1)}, bf16[1,128,128]{2,1,0:T(8,128)(2,1)S(1)}, u32[]{:S(2)}, u32[]{:S(2)}) collective-permute-start(bf16[1,128,128]{2,1,0:T(8,128)(2,1)S(1)} %fusion.39), channel_id=1, source_target_pairs={{0,64},{64,128},{128,192},{192,256},{256,320},{320,384},{384,448},... | collective-permute-start | bytes 98312 | tf_op jit(solution)/shard_map/ppermute | solution.py:19
  148.3 1.4 collective-permute-done.3
  149.9 4.7 %collective-permute-start.4 = (bf16[1,128,128]{2,1,0:T(8,128)(2,1)S(1)}, bf16[1,128,128]{2,1,0:T(8,128)(2,1)S(1)}, u32[]{:S(2)}, u32[]{:S(2)}) collective-permute-start(bf16[1,128,128]{2,1,0:T(8,128)(2,1)S(1)} %fusion.38), channel_id=1, source_target_pairs={{0,64},{64,128},{128,192},{192,256},{256,320},{320,384},{384,448},... | collective-permute-start | bytes 98312 | tf_op jit(solution)/shard_map/ppermute | solution.py:19
  154.6 1.8 broadcast_multiply_fusion
  156.5 3.8 %collective-permute-start.5 = (bf16[1,128,128]{2,1,0:T(8,128)(2,1)S(1)}, bf16[1,128,128]{2,1,0:T(8,128)(2,1)S(1)}, u32[]{:S(2)}, u32[]{:S(2)}) collective-permute-start(bf16[1,128,128]{2,1,0:T(8,128)(2,1)S(1)} %fusion.37), channel_id=1, source_target_pairs={{0,64},{64,128},{128,192},{192,256},{256,320},{320,384},{384,448},... | collective-permute-start | bytes 98312 | tf_op jit(solution)/shard_map/ppermute | solution.py:19
  160.4 1.2 collective-permute-done.5
  162.3 4.8 %collective-permute-start.6 = (bf16[1,128,128]{2,1,0:T(8,128)(2,1)}, bf16[1,128,128]{2,1,0:T(8,128)(2,1)}, u32[]{:S(2)}, u32[]{:S(2)}) collective-permute-start(bf16[1,128,128]{2,1,0:T(8,128)(2,1)} %fusion.36), channel_id=1, source_target_pairs={{0,64},{64,128},{128,192},{192,256},{256,320},{320,384},{384,448},... | collective-permute-start | bytes 98312 | tf_op jit(solution)/shard_map/ppermute | solution.py:19
  167.1 1.2 fusion.28
  171.4 22.5 %while.25 = (s32[]{:T(128)}, f32[1,128,128]{2,1,0:T(8,128)S(1)}, f32[4,1,64,128]{3,2,1,0:T(8,128)}, f32[4,1,1]{0,2,1:T(1,128)}, f32[4,1,64,128]{3,2,1,0:T(8,128)...) while((s32[]{:T(128)}, f32[1,128,128]{2,1,0:T(8,128)S(1)}, ...), condition=%wide.region_4.5_spmd, body=%wide.region_3.4_spmd.sunk | while | flops 44089344 | bytes 625281 | solution.py:74
  173.3 1.2 constant_dynamic-slice_fusion.2
  174.5 1.7 fusion.115
  178.9 1.2 constant_dynamic-slice_fusion.2
  180.1 1.7 fusion.115
  184.5 1.2 constant_dynamic-slice_fusion.2
  185.8 1.7 fusion.115
  190.2 1.2 constant_dynamic-slice_fusion.2
  191.4 1.7 fusion.115
  193.9 1.0 multiply_reduce_fusion
  195.0 1.7 multiply_multiply_fusion
  196.7 6.0 %all-to-all-done.1 = bf16[512,24,128]{2,1,0:T(8,128)(2,1)S(1)} async-done(((bf16[512,24,128]{2,1,0:T(8,128)(2,1)}), bf16[512,24,128]{2,1,0:T(8,128)(2,1)S(1)}, u32[]{:S(2)}, u32[]{:S(2)}) %all-to-all-start.1) | async-done | bytes 3145760 | tf_op jit(solution)/shard_map/all_to_all | solution.py:311
  204.7 2.9 %combine_rows.1 = bf16[128,1024]{1,0:T(8,128)(2,1)} custom-call(bf16[12288,128]{1,0:T(8,128)(2,1)S(1)} %bitcast.213, bf16[1536,128]{1,0:T(8,128)(2,1)S(1)} %copy-done.3, bf16[1536,128]{1,0:T(8,128)(2,1)S(1)} %copy-done.5), custom_call_target="tpu_custom_call" | custom-call | flops 805306368 | bytes 3145728 | tf_op jit(solution)/shard_map/combine_rows/pallas_call | solution.py:298
  (84 shorter events, 22.8 us)
Async XLA Ops:
  0.6 30.8 %copy-start = (f32[1,4,64,64]{3,2,1,0:T(8,128)S(1)}, f32[1,4,64,64]{3,2,1,0:T(8,128)}, u32[]{:S(2)}) copy-start(f32[1,4,64,64]{3,2,1,0:T(8,128)} %param.24) | copy-start | bytes 196612
  1.4 1.0 copy-start.6
  6.1 22.7 %copy-start.17 = (f32[1,256]{1,0:T(1,128)S(1)}, f32[1,256]{1,0:T(1,128)}, u32[]{:S(2)}) copy-start(f32[1,256]{1,0:T(1,128)} %param.23) | copy-start | bytes 3076
  6.1 23.5 %copy-start.18 = (f32[1,256]{1,0:T(1,128)S(1)}, f32[1,256]{1,0:T(1,128)}, u32[]{:S(2)}) copy-start(f32[1,256]{1,0:T(1,128)} %param.22) | copy-start | bytes 3076
  6.1 26.6 %copy-start.11 = (f32[1,256,128]{2,1,0:T(8,128)S(1)}, f32[1,256,128]{2,1,0:T(8,128)}, u32[]{:S(2)}) copy-start(f32[1,256,128]{2,1,0:T(8,128)} %param.19) | copy-start | bytes 393220
  6.1 97.8 %all-to-all-start = ((bf16[512,24,128]{2,1,0:T(8,128)(2,1)}), bf16[512,24,128]{2,1,0:T(8,128)(2,1)S(1)}, u32[]{:S(2)}, u32[]{:S(2)}) async-start(bf16[512,24,128]{2,1,0:T(8,128)(2,1)} %bitcast.50), calls=%async_computation | async-start | bytes 6291456 | tf_op jit(solution)/shard_map/all_to_all | solution.py:311
  30.6 3.8 %copy-start.14 = (f32[1,4,64]{2,1,0:T(4,128)}, f32[1,4,64]{2,1,0:T(4,128)S(1)}, u32[]{:S(2)}) copy-start(f32[1,4,64]{2,1,0:T(4,128)S(1)} %reduce_window_sum.13) | copy-start | bytes 3076
  30.8 5.1 %copy-start.16 = (f32[4]{0:T(128)}, f32[4]{0:T(128)S(1)}, u32[]{:S(2)}) copy-start(f32[4]{0:T(128)S(1)} %get-tuple-element.113) | copy-start | bytes 52
  31.4 4.4 %copy-start.15 = (f32[4,64]{1,0:T(4,128)}, f32[4,64]{1,0:T(4,128)S(1)}, u32[]{:S(2)}) copy-start(f32[4,64]{1,0:T(4,128)S(1)} %get-tuple-element.143) | copy-start | bytes 3076
  32.7 1.8 copy-start.12
  34.4 1.4 copy-start.13
  103.9 1.2 copy-start.8
  105.1 1.2 copy-start.9
  106.4 1.2 copy-start.10
  114.2 1.6 copy-start.1
  115.8 52.6 %copy-start.7 = (f32[128,10]{0,1:T(8,128)S(1)}, f32[128,10]{0,1:T(8,128)}, u32[]{:S(2)}) copy-start(f32[128,10]{0,1:T(8,128)} %param.28) | copy-start | bytes 15364
  115.8 86.9 %all-to-all-start.1 = ((bf16[512,24,128]{2,1,0:T(8,128)(2,1)}), bf16[512,24,128]{2,1,0:T(8,128)(2,1)S(1)}, u32[]{:S(2)}, u32[]{:S(2)}) async-start(bf16[512,24,128]{2,1,0:T(8,128)(2,1)} %bitcast.214), calls=%async_computation.1 | async-start | bytes 6291456 | tf_op jit(solution)/shard_map/all_to_all | solution.py:311
  127.3 6.3 %collective-permute-start = (bf16[1,128,128]{2,1,0:T(8,128)(2,1)S(1)}, bf16[1,128,128]{2,1,0:T(8,128)(2,1)S(1)}, u32[]{:S(2)}, u32[]{:S(2)}) collective-permute-start(bf16[1,128,128]{2,1,0:T(8,128)(2,1)S(1)} %fusion.42), channel_id=1, source_target_pairs={{0,64},{64,128},{128,192},{192,256},{256,320},{320,384},{384,448},... | collective-permute-start | bytes 98312 | tf_op jit(solution)/shard_map/ppermute | solution.py:19
  133.7 4.0 %collective-permute-start.1 = (bf16[1,128,128]{2,1,0:T(8,128)(2,1)S(1)}, bf16[1,128,128]{2,1,0:T(8,128)(2,1)S(1)}, u32[]{:S(2)}, u32[]{:S(2)}) collective-permute-start(bf16[1,128,128]{2,1,0:T(8,128)(2,1)S(1)} %fusion.41), channel_id=1, source_target_pairs={{0,64},{64,128},{128,192},{192,256},{256,320},{320,384},{384,448},... | collective-permute-start | bytes 98312 | tf_op jit(solution)/shard_map/ppermute | solution.py:19
  137.9 5.6 %collective-permute-start.2 = (bf16[1,128,128]{2,1,0:T(8,128)(2,1)S(1)}, bf16[1,128,128]{2,1,0:T(8,128)(2,1)S(1)}, u32[]{:S(2)}, u32[]{:S(2)}) collective-permute-start(bf16[1,128,128]{2,1,0:T(8,128)(2,1)S(1)} %fusion.40), channel_id=1, source_target_pairs={{0,64},{64,128},{128,192},{192,256},{256,320},{320,384},{384,448},... | collective-permute-start | bytes 98312 | tf_op jit(solution)/shard_map/ppermute | solution.py:19
  143.7 6.0 %collective-permute-start.3 = (bf16[1,128,128]{2,1,0:T(8,128)(2,1)S(1)}, bf16[1,128,128]{2,1,0:T(8,128)(2,1)S(1)}, u32[]{:S(2)}, u32[]{:S(2)}) collective-permute-start(bf16[1,128,128]{2,1,0:T(8,128)(2,1)S(1)} %fusion.39), channel_id=1, source_target_pairs={{0,64},{64,128},{128,192},{192,256},{256,320},{320,384},{384,448},... | collective-permute-start | bytes 98312 | tf_op jit(solution)/shard_map/ppermute | solution.py:19
  149.9 6.4 %collective-permute-start.4 = (bf16[1,128,128]{2,1,0:T(8,128)(2,1)S(1)}, bf16[1,128,128]{2,1,0:T(8,128)(2,1)S(1)}, u32[]{:S(2)}, u32[]{:S(2)}) collective-permute-start(bf16[1,128,128]{2,1,0:T(8,128)(2,1)S(1)} %fusion.38), channel_id=1, source_target_pairs={{0,64},{64,128},{128,192},{192,256},{256,320},{320,384},{384,448},... | collective-permute-start | bytes 98312 | tf_op jit(solution)/shard_map/ppermute | solution.py:19
  156.5 5.0 %collective-permute-start.5 = (bf16[1,128,128]{2,1,0:T(8,128)(2,1)S(1)}, bf16[1,128,128]{2,1,0:T(8,128)(2,1)S(1)}, u32[]{:S(2)}, u32[]{:S(2)}) collective-permute-start(bf16[1,128,128]{2,1,0:T(8,128)(2,1)S(1)} %fusion.37), channel_id=1, source_target_pairs={{0,64},{64,128},{128,192},{192,256},{256,320},{320,384},{384,448},... | collective-permute-start | bytes 98312 | tf_op jit(solution)/shard_map/ppermute | solution.py:19
  162.3 8.3 %collective-permute-start.6 = (bf16[1,128,128]{2,1,0:T(8,128)(2,1)}, bf16[1,128,128]{2,1,0:T(8,128)(2,1)}, u32[]{:S(2)}, u32[]{:S(2)}) collective-permute-start(bf16[1,128,128]{2,1,0:T(8,128)(2,1)} %fusion.36), channel_id=1, source_target_pairs={{0,64},{64,128},{128,192},{192,256},{256,320},{320,384},{384,448},... | collective-permute-start | bytes 98312 | tf_op jit(solution)/shard_map/ppermute | solution.py:19
  168.4 26.6 %copy-start.19 = (f32[128]{0:T(128)S(1)}, f32[128]{0:T(128)}, u32[]{:S(2)}) copy-start(f32[128]{0:T(128)} %param.25) | copy-start | bytes 1540
  169.1 0.8 copy-start.2
  169.8 0.7 copy-start.4
  202.7 1.0 copy-start.3
  203.7 1.0 copy-start.5

commit v2 on v1

--- a/solution.py
+++ b/solution.py
@@ -11,6 +11,7 @@
 NORM_EPSILON = 1e-06
 CAPACITY = 3
 LANES = 128
+VMEM_BYTES = 60 * 1024 * 1024
 
 
 def passed_along(block, axis, distance):
@@ -93,9 +94,7 @@
     return ((updated_mapping, updated_addend), None)
 
 
-def delta_net(
-    queries, key_vectors, values, out_gate, write_strength, log_fading_factor, block_inverse, norm_gain
-):
+def delta_front(queries, key_vectors, values, write_strength, log_fading_factor, block_inverse):
     tracks, length, head_width = queries.shape
     pieces = block_parts(
         queries, key_vectors, values, write_strength, log_fading_factor, block_inverse
@@ -121,8 +120,7 @@
         incoming_state = passed_along(departing_state.astype(jnp.bfloat16), "ctx", 1).astype(
             departing_state.dtype
         )
-    _, attended = run_blocks(pieces, incoming_state)
-    return gated_norm(attended.reshape(tracks, length, head_width), norm_gain, out_gate)
+    return pieces, incoming_state
 
 
 def named_and_rank(ranks, first, count, tokens):
@@ -141,14 +139,30 @@
     return named, earlier
 
 
-def pack_kernel(ranks_ref, hidden_ref, out_ref, spread_ref):
+def pack_kernel(owner_count, context_size, routes_ref, hidden_ref, out_ref, spread_ref):
     tokens, width = hidden_ref.shape
     parts = width // LANES
     per = CAPACITY * parts
     count = out_ref.shape[0] // per
-    named, earlier = named_and_rank(
-        ranks_ref[...], pl.program_id(0) * count, count, tokens
-    )
+    routes = routes_ref[...].astype(jnp.float32)
+    context = jnp.floor(routes * (1.0 / owner_count))
+    pieces = (context, routes - context * owner_count)
+    diagonal = (
+        lax.broadcasted_iota(jnp.int32, (tokens, tokens), 0)
+        == lax.broadcasted_iota(jnp.int32, (tokens, tokens), 1)
+    )
+    unit = diagonal.astype(jnp.float32).astype(jnp.bfloat16)
+    context, owner = (
+        lax.dot_general(
+            piece.astype(jnp.bfloat16),
+            unit,
+            (((0,), (0,)), ((), ())),
+            preferred_element_type=jnp.float32,
+        )
+        for piece in pieces
+    )
+    ranks = (owner * context_size + context).astype(jnp.int32)
+    named, earlier = named_and_rank(ranks, pl.program_id(0) * count, count, tokens)
     for slot in range(CAPACITY):
         chosen = jnp.where(jnp.logical_and(named, earlier == slot), 1.0, 0.0).astype(jnp.bfloat16)
         rows = jnp.dot(chosen, hidden_ref[...], preferred_element_type=jnp.float32)
@@ -159,30 +173,31 @@
     out_ref[...] = spread_ref[...].astype(jnp.bfloat16)
 
 
-def pack_rows(ranks, hidden, experts, steps):
+def pack_rows(routes, hidden, owner_count, context_size, steps):
     tokens, width = hidden.shape
+    experts = owner_count * context_size
     rows = experts * CAPACITY * width // LANES
     return pl.pallas_call(
-        pack_kernel,
+        functools.partial(pack_kernel, owner_count, context_size),
         grid=(steps,),
         out_shape=jax.ShapeDtypeStruct((rows, LANES), jnp.bfloat16),
         in_specs=[
-            pl.BlockSpec(ranks.shape, lambda i: (0, 0)),
+            pl.BlockSpec(routes.shape, lambda i: (0, 0)),
             pl.BlockSpec(hidden.shape, lambda i: (0, 0)),
         ],
         out_specs=pl.BlockSpec((rows // steps, LANES), lambda i: (i, 0)),
         scratch_shapes=[pltpu.VMEM((rows // steps, LANES), jnp.float32)],
-        compiler_params=pltpu.CompilerParams(vmem_limit_bytes=32 * 1024 * 1024),
+        compiler_params=pltpu.CompilerParams(vmem_limit_bytes=VMEM_BYTES),
         cost_estimate=pl.CostEstimate(
             flops=2 * experts * CAPACITY * tokens * width, bytes_accessed=rows * 256, transcendentals=0
         ),
         name="pack_rows",
-    )(ranks, hidden)
+    )(routes, hidden)
 
 
 def weight_kernel(ranks_ref, weights_ref, high_ref, low_ref):
     tokens = ranks_ref.shape[1]
-    experts = high_ref.shape[0] // CAPACITY
+    experts = high_ref.shape[1]
     ranks = ranks_ref[...]
     named, earlier = named_and_rank(ranks, 0, experts, tokens)
     row = lax.broadcasted_iota(jnp.int32, (experts, tokens), 0)
@@ -193,14 +208,13 @@
     low = scale - high
     for slot in range(CAPACITY):
         here = jnp.logical_and(named, earlier == slot)
-        at = pl.ds(slot * experts, experts)
-        high_ref[at, :] = jnp.where(here, high, 0.0).astype(jnp.bfloat16)
-        low_ref[at, :] = jnp.where(here, low, 0.0).astype(jnp.bfloat16)
+        high_ref[slot] = jnp.where(here, high, 0.0).astype(jnp.bfloat16)
+        low_ref[slot] = jnp.where(here, low, 0.0).astype(jnp.bfloat16)
 
 
 def weight_table(ranks, weights, experts):
     tokens = ranks.shape[1]
-    shape = jax.ShapeDtypeStruct((CAPACITY * experts, tokens), jnp.bfloat16)
+    shape = jax.ShapeDtypeStruct((CAPACITY, experts, tokens), jnp.bfloat16)
     return pl.pallas_call(
         weight_kernel,
         out_shape=(shape, shape),
@@ -212,11 +226,26 @@
     )(ranks, weights)
 
 
-def expert_kernel(received_ref, gate_ref, up_ref, down_ref, out_ref, spread_ref):
-    width = gate_ref.shape[0]
+def expert_kernel(
+    received_ref, gate_ref, up_ref, down_ref, out_ref, spread_ref, gate_here, up_here, down_here, ready
+):
+    width = gate_here.shape[0]
     parts = width // LANES
     per = CAPACITY * parts
     count = received_ref.shape[0] // per
+    loads = [
+        pltpu.make_async_copy(there, here, ready.at[i])
+        for i, (there, here) in enumerate(
+            ((gate_ref, gate_here), (up_ref, up_here), (down_ref, down_here))
+        )
+    ]
+    first = pl.program_id(0) == 0
+
+    @pl.when(first)
+    def _():
+        for load in loads:
+            load.start()
+
     spread_ref[...] = received_ref[...].astype(jnp.float32)
     rows = jnp.concatenate(
         [
@@ -231,10 +260,16 @@
         ],
         axis=0,
     )
-    gate = jnp.dot(rows, gate_ref[...], preferred_element_type=jnp.float32)
-    up = jnp.dot(rows, up_ref[...], preferred_element_type=jnp.float32)
+
+    @pl.when(first)
+    def _():
+        for load in loads:
+            load.wait()
+
+    gate = jnp.dot(rows, gate_here[...], preferred_element_type=jnp.float32)
+    up = jnp.dot(rows, up_here[...], preferred_element_type=jnp.float32)
     active = (gate / (1.0 + jnp.exp(-gate)) * up).astype(jnp.bfloat16)
-    produced = jnp.dot(active, down_ref[...], preferred_element_type=jnp.float32)
+    produced = jnp.dot(active, down_here[...], preferred_element_type=jnp.float32)
     for slot in range(CAPACITY):
         for part in range(parts):
             spread_ref[pl.ds(slot * parts + part, count, stride=per), :] = produced[
@@ -248,19 +283,21 @@
     width, units = gate_weights.shape
     slots = rows * LANES // width
     block = pl.BlockSpec((rows // steps, LANES), lambda i: (i, 0))
+    whole = pl.BlockSpec(memory_space=pl.ANY)
     return pl.pallas_call(
         expert_kernel,
         grid=(steps,),
         out_shape=jax.ShapeDtypeStruct(received.shape, jnp.bfloat16),
-        in_specs=[
-            block,
-            pl.BlockSpec(gate_weights.shape, lambda i: (0, 0)),
-            pl.BlockSpec(up_weights.shape, lambda i: (0, 0)),
-            pl.BlockSpec(down_weights.shape, lambda i: (0, 0)),
+        in_specs=[block, whole, whole, whole],
+        out_specs=block,
+        scratch_shapes=[
+            pltpu.VMEM((rows // steps, LANES), jnp.float32),
+            pltpu.VMEM(gate_weights.shape, jnp.bfloat16),
+            pltpu.VMEM(up_weights.shape, jnp.bfloat16),
+            pltpu.VMEM(down_weights.shape, jnp.bfloat16),
+            pltpu.SemaphoreType.DMA((3,)),
         ],
-        out_specs=block,
-        scratch_shapes=[pltpu.VMEM((rows // steps, LANES), jnp.float32)],
-        compiler_params=pltpu.CompilerParams(vmem_limit_bytes=40 * 1024 * 1024),
+        compiler_params=pltpu.CompilerParams(vmem_limit_bytes=VMEM_BYTES),
         cost_estimate=pl.CostEstimate(
             flops=6 * slots * width * units,
             bytes_accessed=4 * rows * LANES + 6 * width * units,
@@ -270,13 +307,19 @@
     )(received, gate_weights, up_weights, down_weights)
 
 
-def combine_kernel(returned_ref, high_ref, low_ref, out_ref, spread_ref):
+def combine_kernel(returned_ref, high_ref, low_ref, out_ref, spread_ref, total_ref):
     tokens, width = out_ref.shape
     parts = width // LANES
     per = CAPACITY * parts
     count = returned_ref.shape[0] // per
+    step = pl.program_id(0)
+
+    @pl.when(step == 0)
+    def _():
+        total_ref[...] = jnp.zeros_like(total_ref)
+
     spread_ref[...] = returned_ref[...].astype(jnp.float32)
-    total = jnp.zeros((tokens, width), jnp.float32)
+    total = total_ref[...]
     for slot in range(CAPACITY):
         rows = jnp.concatenate(
             [
@@ -285,21 +328,32 @@
             ],
             axis=1,
         )
-        at = pl.ds(slot * count, count)
         for table in (high_ref, low_ref):
             total = total + lax.dot_general(
-                table[at, :], rows, (((0,), (0,)), ((), ())), preferred_element_type=jnp.float32
+                table[slot], rows, (((0,), (0,)), ((), ())), preferred_element_type=jnp.float32
             )
-    out_ref[...] = total.astype(jnp.bfloat16)
-
-
-def combine_rows(returned, high, low, tokens, width):
+    total_ref[...] = total
+
+    @pl.when(step == pl.num_programs(0) - 1)
+    def _():
+        out_ref[...] = total.astype(jnp.bfloat16)
+
+
+def combine_rows(returned, high, low, tokens, width, steps):
     rows = returned.shape[0]
+    experts = high.shape[1]
+    table = pl.BlockSpec((CAPACITY, experts // steps, tokens), lambda i: (0, i, 0))
     return pl.pallas_call(
         combine_kernel,
+        grid=(steps,),
         out_shape=jax.ShapeDtypeStruct((tokens, width), jnp.bfloat16),
-        scratch_shapes=[pltpu.VMEM((rows, LANES), jnp.float32)],
-        compiler_params=pltpu.CompilerParams(vmem_limit_bytes=48 * 1024 * 1024),
+        in_specs=[pl.BlockSpec((rows // steps, LANES), lambda i: (i, 0)), table, table],
+        out_specs=pl.BlockSpec((tokens, width), lambda i: (0, 0)),
+        scratch_shapes=[
+            pltpu.VMEM((rows // steps, LANES), jnp.float32),
+            pltpu.VMEM((tokens, width), jnp.float32),
+        ],
+        compiler_params=pltpu.CompilerParams(vmem_limit_bytes=VMEM_BYTES),
         cost_estimate=pl.CostEstimate(
             flops=4 * rows * LANES * tokens, bytes_accessed=2 * rows * LANES, transcendentals=0
         ),
@@ -331,16 +385,19 @@
     context_size = lax.axis_size("ctx")
     owner_count = lax.axis_size("exp")
     experts = context_size * owner_count
-    ranks = (routes % owner_count * context_size + routes // owner_count).T
-    outgoing = pack_rows(ranks, hidden, experts, 4)
+    outgoing = pack_rows(routes, hidden, owner_count, context_size, 4)
     received = exchange(outgoing)
+    pieces, incoming_state = delta_front(
+        queries, key_vectors, values, write_strength, log_fading_factor, block_inverse
+    )
+    received, incoming_state = lax.optimization_barrier((received, incoming_state))
     produced = expert_rows(received, gate_weights[0], up_weights[0], down_weights[0], 4)
     returned = exchange(produced)
+    ranks = (routes % owner_count * context_size + routes // owner_count).T
     high, low = weight_table(ranks, route_weights.T, experts)
-    expert_output = combine_rows(returned, high, low, tokens, width)
-    mixer_output = delta_net(
-        queries, key_vectors, values, out_gate, write_strength, log_fading_factor, block_inverse, norm_gain
-    )
+    expert_output = combine_rows(returned, high, low, tokens, width, 4)
+    _, attended = run_blocks(pieces, incoming_state)
+    mixer_output = gated_norm(attended.reshape(out_gate.shape), norm_gain, out_gate)
     return (mixer_output, expert_output)
 
 

time: 211 us -> 213 us (level)
  Pallas kernels: 13.9 us -> 22.4 us
  local copies, waits for them, and re-layouts: 15.7 us -> 8.33 us
  waiting for transfers between devices: 72.9 us -> 79.7 us
  matrix products: 33.5 us -> 27.6 us
  starting transfers between devices: 62.2 us -> 64.9 us
    all_to_all x2, waiting for transfers between devices: 65.3 us -> 70.6 us  [exchange(): lax.all_to_all(rows, ('exp', 'ctx'), split_axis=0, concat_axis=0, tiled=T...]
    unnamed x41 -> x28, local copies, waits for them, and re-layouts: 10.3 us -> 5.16 us
    pallas_call x1, Pallas kernels: 6.57 us -> 11.4 us  [expert_rows(): pl.pallas_call(expert_kernel, grid=(steps,), out_shape=jax.ShapeDtypeStru...]
    pallas_call x2, Pallas kernels: 6.68 us -> 10.4 us  [the longest x1 5.24 us: pack_rows(): pl.pallas_call(functools.partial(pack_kernel, owner_count, context_size),...]
    dot_general x4, matrix products: 4.33 us -> 0.83 us  [compose(): jnp.einsum('qfz,qze->qfe', segment_mapping, current_addend, precision=TOP...]
    dot_general x4, matrix products: 4.19 us -> 0.82 us  [compose(): jnp.einsum('qfz,qze->qfe', segment_mapping, current_mapping, precision=TO...]
    dot_general x4, matrix products: 3.14 us -> 6.18 us  [block_step(): jnp.einsum('sij,sjv->siv', causal, fresh_values, precision=TOP_PRECISION)]
    dynamic_slice x4, local copies, waits for them, and re-layouts: 4.9 us -> 2.68 us  [run_blocks(): states, attended = lax.scan(block_step, states, moved)]
  transfers between devices with their start and end apart: 9 -> 9, of which waited for: 7 -> 9; matrix products, arithmetic and copies ran while one was open for 23% -> 18% of each run, Pallas kernels for 0% -> 0%
where the time goes in v2:
time: 213 us; the launch traced here: 210 us
  waiting for transfers between devices  79.7 us (37%)
  starting transfers between devices  64.9 us (30%)
  matrix products  27.6 us (13%)
  Pallas kernels  22.4 us (11%)
  local copies, waits for them, and re-layouts  8.33 us (4%)
  other arithmetic  6.18 us (3%)
    all_to_all x2, waiting for transfers between devices, exchange(): lax.all_to_all(rows, ('exp', 'ctx'), split_axis=0, concat_axis=0, tiled=T...  70.6 us
    all_to_all x2, starting transfers between devices, exchange(): lax.all_to_all(rows, ('exp', 'ctx'), split_axis=0, concat_axis=0, tiled=T...  35.3 us
    ppermute x7, starting transfers between devices, passed_along(): return lax.ppermute(block, axis, route)  29.6 us
    pallas_call x1, Pallas kernels, expert_rows(): pl.pallas_call(expert_kernel, grid=(steps,), out_shape=jax.ShapeDtypeStru...  11.4 us
    ppermute x7, waiting for transfers between devices, passed_along(): return lax.ppermute(block, axis, route)  9.12 us
    dot_general x4, matrix products, block_step(): jnp.einsum('sch,scv->shv', faded_keys, fresh_values, precision=TOP_PRECIS...  6.99 us
    dot_general x4, matrix products, block_step(): jnp.einsum('sij,sjv->siv', causal, fresh_values, precision=TOP_PRECISION)  6.18 us
    pallas_call x1, Pallas kernels, pack_rows(): pl.pallas_call(functools.partial(pack_kernel, owner_count, context_size),...  5.24 us
  transfers between devices with their start and end apart: 9, of which 9 were waited for; matrix products, arithmetic and copies ran while one was open for 18% of the time, Pallas kernels for 0%

profile of v2, /device:TPU:1, one launch (start us, length us, event | category | flops | bytes accessed | tf_op | source)
XLA Modules:
  0.0 210.3 jit_solution(2200285415624816984)
XLA Ops:
  0.6 1.5 copy.22.routes_ref
  2.1 5.2 %pack_rows.1 = bf16[12288,128]{1,0:T(8,128)(2,1)} custom-call(s32[128,10]{1,0:T(8,128)} %copy.22.routes_ref, bf16[128,1024]{1,0:T(8,128)(2,1)} %hidden_ref.1), custom_call_target="tpu_custom_call" | custom-call | flops 402653184 | bytes 3145728 | tf_op jit(solution)/shard_map/pack_rows/pallas_call | solution.py:180
  7.4 24.0 %all-to-all-start = ((bf16[512,24,128]{2,1,0:T(8,128)(2,1)}), bf16[512,24,128]{2,1,0:T(8,128)(2,1)}, u32[]{:S(2)}, u32[]{:S(2)}) async-start(bf16[512,24,128]{2,1,0:T(8,128)(2,1)} %bitcast.214), calls=%async_computation | async-start | bytes 6291456 | tf_op jit(solution)/shard_map/all_to_all | solution.py:365
  36.1 1.9 while.24
  38.2 3.5 %collective-permute-start = (bf16[1,128,128]{2,1,0:T(8,128)(2,1)S(1)}, bf16[1,128,128]{2,1,0:T(8,128)(2,1)S(1)}, u32[]{:S(2)}, u32[]{:S(2)}) collective-permute-start(bf16[1,128,128]{2,1,0:T(8,128)(2,1)S(1)} %fusion.42), channel_id=1, source_target_pairs={{0,64},{64,128},{128,192},{192,256},{256,320},{320,384},{384,448},... | collective-permute-start | bytes 98312 | tf_op jit(solution)/shard_map/ppermute | solution.py:20
  41.7 2.8 %collective-permute-done = bf16[1,128,128]{2,1,0:T(8,128)(2,1)S(1)} collective-permute-done((bf16[1,128,128]{2,1,0:T(8,128)(2,1)S(1)}, bf16[1,128,128]{2,1,0:T(8,128)(2,1)S(1)}, u32[]{:S(2)}, u32[]{:S(2)}) %collective-permute-start) | collective-permute-done | bytes 32800 | tf_op jit(solution)/shard_map/ppermute | solution.py:20
  44.7 3.1 %collective-permute-start.1 = (bf16[1,128,128]{2,1,0:T(8,128)(2,1)S(1)}, bf16[1,128,128]{2,1,0:T(8,128)(2,1)S(1)}, u32[]{:S(2)}, u32[]{:S(2)}) collective-permute-start(bf16[1,128,128]{2,1,0:T(8,128)(2,1)S(1)} %fusion.41), channel_id=1, source_target_pairs={{0,64},{64,128},{128,192},{192,256},{256,320},{320,384},{384,448},... | collective-permute-start | bytes 98312 | tf_op jit(solution)/shard_map/ppermute | solution.py:20
  47.8 1.0 collective-permute-done.1
  49.0 4.8 %collective-permute-start.2 = (bf16[1,128,128]{2,1,0:T(8,128)(2,1)S(1)}, bf16[1,128,128]{2,1,0:T(8,128)(2,1)S(1)}, u32[]{:S(2)}, u32[]{:S(2)}) collective-permute-start(bf16[1,128,128]{2,1,0:T(8,128)(2,1)S(1)} %fusion.40), channel_id=1, source_target_pairs={{0,64},{64,128},{128,192},{192,256},{256,320},{320,384},{384,448},... | collective-permute-start | bytes 98312 | tf_op jit(solution)/shard_map/ppermute | solution.py:20
  53.8 1.1 collective-permute-done.2
  55.0 4.4 %collective-permute-start.3 = (bf16[1,128,128]{2,1,0:T(8,128)(2,1)S(1)}, bf16[1,128,128]{2,1,0:T(8,128)(2,1)S(1)}, u32[]{:S(2)}, u32[]{:S(2)}) collective-permute-start(bf16[1,128,128]{2,1,0:T(8,128)(2,1)S(1)} %fusion.39), channel_id=1, source_target_pairs={{0,64},{64,128},{128,192},{192,256},{256,320},{320,384},{384,448},... | collective-permute-start | bytes 98312 | tf_op jit(solution)/shard_map/ppermute | solution.py:20
  59.5 1.0 collective-permute-done.3
  60.7 4.5 %collective-permute-start.4 = (bf16[1,128,128]{2,1,0:T(8,128)(2,1)S(1)}, bf16[1,128,128]{2,1,0:T(8,128)(2,1)S(1)}, u32[]{:S(2)}, u32[]{:S(2)}) collective-permute-start(bf16[1,128,128]{2,1,0:T(8,128)(2,1)S(1)} %fusion.38), channel_id=1, source_target_pairs={{0,64},{64,128},{128,192},{192,256},{256,320},{320,384},{384,448},... | collective-permute-start | bytes 98312 | tf_op jit(solution)/shard_map/ppermute | solution.py:20
  65.2 1.3 collective-permute-done.4
  66.6 4.4 %collective-permute-start.5 = (bf16[1,128,128]{2,1,0:T(8,128)(2,1)S(1)}, bf16[1,128,128]{2,1,0:T(8,128)(2,1)S(1)}, u32[]{:S(2)}, u32[]{:S(2)}) collective-permute-start(bf16[1,128,128]{2,1,0:T(8,128)(2,1)S(1)} %fusion.37), channel_id=1, source_target_pairs={{0,64},{64,128},{128,192},{192,256},{256,320},{320,384},{384,448},... | collective-permute-start | bytes 98312 | tf_op jit(solution)/shard_map/ppermute | solution.py:20
  71.1 1.0 collective-permute-done.5
  72.2 4.8 %collective-permute-start.6 = (bf16[1,128,128]{2,1,0:T(8,128)(2,1)S(1)}, bf16[1,128,128]{2,1,0:T(8,128)(2,1)S(1)}, u32[]{:S(2)}, u32[]{:S(2)}) collective-permute-start(bf16[1,128,128]{2,1,0:T(8,128)(2,1)S(1)} %fusion.36), channel_id=1, source_target_pairs={{0,64},{64,128},{128,192},{192,256},{256,320},{320,384},{384,448},... | collective-permute-start | bytes 98312 | tf_op jit(solution)/shard_map/ppermute | solution.py:20
  77.0 1.0 collective-permute-done.6
  78.0 27.3 %all-to-all-done = bf16[512,24,128]{2,1,0:T(8,128)(2,1)} async-done(((bf16[512,24,128]{2,1,0:T(8,128)(2,1)}), bf16[512,24,128]{2,1,0:T(8,128)(2,1)}, u32[]{:S(2)}, u32[]{:S(2)}) %all-to-all-start) | async-done | bytes 3145760 | tf_op jit(solution)/shard_map/all_to_all | solution.py:365
  105.3 11.4 %expert_rows.1 = bf16[12288,128]{1,0:T(8,128)(2,1)} custom-call(bf16[12288,128]{1,0:T(8,128)(2,1)} %bitcast.16.received_ref, bf16[1024,512]{1,0:T(8,128)(2,1)} %bitcast.230, bf16[1024,512]{1,0:T(8,128)(2,1)} %bitcast.231, bf16[512,1024]{1,0:T(8,128)(2,1)} %bitcast.232), custom_call_target="tpu_custom_call" | custom-call | flops 4831838208 | bytes 9437184 | tf_op jit(solution)/shard_map/expert_rows/pallas_call | solution.py:287
  116.7 11.3 %all-to-all-start.1 = ((bf16[512,24,128]{2,1,0:T(8,128)(2,1)}), bf16[512,24,128]{2,1,0:T(8,128)(2,1)S(1)}, u32[]{:S(2)}, u32[]{:S(2)}) async-start(bf16[512,24,128]{2,1,0:T(8,128)(2,1)} %bitcast.221), calls=%async_computation.1 | async-start | bytes 6291456 | tf_op jit(solution)/shard_map/all_to_all | solution.py:365
  128.7 0.7 copy-done.1
  129.4 0.8 copy-done.2
  130.2 1.9 fusion.28
  132.1 1.7 broadcast_multiply_fusion
  133.8 23.5 %while.25 = (s32[]{:T(128)}, f32[1,128,128]{2,1,0:T(8,128)S(1)}, f32[4,1,64,128]{3,2,1,0:T(8,128)}, f32[4,1,1]{0,2,1:T(1,128)S(1)}, f32[4,1,64,128]{3,2,1,0:T(8,...) while((s32[]{:T(128)}, f32[1,128,128]{2,1,0:T(8,128)S(1)}, ...), condition=%wide.region_4.5_spmd, body=%wide.region_3.4_spmd.sunk | while | flops 44089344 | bytes 625281 | solution.py:75
  133.8 0.9 fusion.116
  134.8 1.0 convolution_subtract_fusion.3
  136.4 1.7 fusion.115
  138.2 1.5 fusion.117
  139.7 0.9 fusion.116
  140.7 1.0 convolution_subtract_fusion.3
  141.6 0.7 constant_dynamic-slice_fusion.2
  142.3 1.7 fusion.115
  144.1 1.5 fusion.117
  145.6 0.9 fusion.116
  146.6 1.0 convolution_subtract_fusion.3
  148.2 1.7 fusion.115
  149.9 1.5 fusion.117
  151.5 0.9 fusion.116
  152.4 1.0 convolution_subtract_fusion.3
  154.1 1.7 fusion.115
  155.8 1.5 fusion.117
  157.4 1.0 multiply_reduce_fusion
  158.5 1.7 multiply_multiply_fusion
  160.2 43.3 %all-to-all-done.1 = bf16[512,24,128]{2,1,0:T(8,128)(2,1)S(1)} async-done(((bf16[512,24,128]{2,1,0:T(8,128)(2,1)}), bf16[512,24,128]{2,1,0:T(8,128)(2,1)S(1)}, u32[]{:S(2)}, u32[]{:S(2)}) %all-to-all-start.1) | async-done | bytes 3145760 | tf_op jit(solution)/shard_map/all_to_all | solution.py:365
  203.6 1.6 copy-done.4
  205.2 5.1 %combine_rows.1 = bf16[128,1024]{1,0:T(8,128)(2,1)} custom-call(bf16[12288,128]{1,0:T(8,128)(2,1)} %bitcast.215, bf16[3,512,128]{2,1,0:T(8,128)(2,1)} %copy-done.1, bf16[3,512,128]{2,1,0:T(8,128)(2,1)} %copy-done.2), custom_call_target="tpu_custom_call" | custom-call | flops 805306368 | bytes 3145728 | tf_op jit(solution)/shard_map/combine_rows/pallas_call | solution.py:346
  (71 shorter events, 10.4 us)
Async XLA Ops:
  0.6 33.3 %copy-start = (f32[1,4,64,64]{3,2,1,0:T(8,128)S(1)}, f32[1,4,64,64]{3,2,1,0:T(8,128)}, u32[]{:S(2)}) copy-start(f32[1,4,64,64]{3,2,1,0:T(8,128)} %param.24) | copy-start | bytes 196612
  7.3 24.6 %copy-start.10 = (f32[1,256]{1,0:T(1,128)S(1)}, f32[1,256]{1,0:T(1,128)}, u32[]{:S(2)}) copy-start(f32[1,256]{1,0:T(1,128)} %param.23) | copy-start | bytes 3076
  7.4 25.3 %copy-start.11 = (f32[1,256]{1,0:T(1,128)S(1)}, f32[1,256]{1,0:T(1,128)}, u32[]{:S(2)}) copy-start(f32[1,256]{1,0:T(1,128)} %param.22) | copy-start | bytes 3076
  7.4 26.6 %copy-start.8 = (f32[1,256,128]{2,1,0:T(8,128)S(1)}, f32[1,256,128]{2,1,0:T(8,128)}, u32[]{:S(2)}) copy-start(f32[1,256,128]{2,1,0:T(8,128)} %param.20) | copy-start | bytes 393220
  7.4 27.0 %copy-start.5 = (f32[1,256,128]{2,1,0:T(8,128)S(1)}, f32[1,256,128]{2,1,0:T(8,128)}, u32[]{:S(2)}) copy-start(f32[1,256,128]{2,1,0:T(8,128)} %param.19) | copy-start | bytes 393220
  7.4 97.9 %all-to-all-start = ((bf16[512,24,128]{2,1,0:T(8,128)(2,1)}), bf16[512,24,128]{2,1,0:T(8,128)(2,1)}, u32[]{:S(2)}, u32[]{:S(2)}) async-start(bf16[512,24,128]{2,1,0:T(8,128)(2,1)} %bitcast.214), calls=%async_computation | async-start | bytes 6291456 | tf_op jit(solution)/shard_map/all_to_all | solution.py:365
  34.3 1.1 copy-start.6
  35.4 0.7 copy-start.7
  38.2 6.3 %collective-permute-start = (bf16[1,128,128]{2,1,0:T(8,128)(2,1)S(1)}, bf16[1,128,128]{2,1,0:T(8,128)(2,1)S(1)}, u32[]{:S(2)}, u32[]{:S(2)}) collective-permute-start(bf16[1,128,128]{2,1,0:T(8,128)(2,1)S(1)} %fusion.42), channel_id=1, source_target_pairs={{0,64},{64,128},{128,192},{192,256},{256,320},{320,384},{384,448},... | collective-permute-start | bytes 98312 | tf_op jit(solution)/shard_map/ppermute | solution.py:20
  44.7 4.1 %collective-permute-start.1 = (bf16[1,128,128]{2,1,0:T(8,128)(2,1)S(1)}, bf16[1,128,128]{2,1,0:T(8,128)(2,1)S(1)}, u32[]{:S(2)}, u32[]{:S(2)}) collective-permute-start(bf16[1,128,128]{2,1,0:T(8,128)(2,1)S(1)} %fusion.41), channel_id=1, source_target_pairs={{0,64},{64,128},{128,192},{192,256},{256,320},{320,384},{384,448},... | collective-permute-start | bytes 98312 | tf_op jit(solution)/shard_map/ppermute | solution.py:20
  49.0 5.9 %collective-permute-start.2 = (bf16[1,128,128]{2,1,0:T(8,128)(2,1)S(1)}, bf16[1,128,128]{2,1,0:T(8,128)(2,1)S(1)}, u32[]{:S(2)}, u32[]{:S(2)}) collective-permute-start(bf16[1,128,128]{2,1,0:T(8,128)(2,1)S(1)} %fusion.40), channel_id=1, source_target_pairs={{0,64},{64,128},{128,192},{192,256},{256,320},{320,384},{384,448},... | collective-permute-start | bytes 98312 | tf_op jit(solution)/shard_map/ppermute | solution.py:20
  55.0 5.4 %collective-permute-start.3 = (bf16[1,128,128]{2,1,0:T(8,128)(2,1)S(1)}, bf16[1,128,128]{2,1,0:T(8,128)(2,1)S(1)}, u32[]{:S(2)}, u32[]{:S(2)}) collective-permute-start(bf16[1,128,128]{2,1,0:T(8,128)(2,1)S(1)} %fusion.39), channel_id=1, source_target_pairs={{0,64},{64,128},{128,192},{192,256},{256,320},{320,384},{384,448},... | collective-permute-start | bytes 98312 | tf_op jit(solution)/shard_map/ppermute | solution.py:20
  60.7 5.8 %collective-permute-start.4 = (bf16[1,128,128]{2,1,0:T(8,128)(2,1)S(1)}, bf16[1,128,128]{2,1,0:T(8,128)(2,1)S(1)}, u32[]{:S(2)}, u32[]{:S(2)}) collective-permute-start(bf16[1,128,128]{2,1,0:T(8,128)(2,1)S(1)} %fusion.38), channel_id=1, source_target_pairs={{0,64},{64,128},{128,192},{192,256},{256,320},{320,384},{384,448},... | collective-permute-start | bytes 98312 | tf_op jit(solution)/shard_map/ppermute | solution.py:20
  66.6 5.5 %collective-permute-start.5 = (bf16[1,128,128]{2,1,0:T(8,128)(2,1)S(1)}, bf16[1,128,128]{2,1,0:T(8,128)(2,1)S(1)}, u32[]{:S(2)}, u32[]{:S(2)}) collective-permute-start(bf16[1,128,128]{2,1,0:T(8,128)(2,1)S(1)} %fusion.37), channel_id=1, source_target_pairs={{0,64},{64,128},{128,192},{192,256},{256,320},{320,384},{384,448},... | collective-permute-start | bytes 98312 | tf_op jit(solution)/shard_map/ppermute | solution.py:20
  72.2 5.8 %collective-permute-start.6 = (bf16[1,128,128]{2,1,0:T(8,128)(2,1)S(1)}, bf16[1,128,128]{2,1,0:T(8,128)(2,1)S(1)}, u32[]{:S(2)}, u32[]{:S(2)}) collective-permute-start(bf16[1,128,128]{2,1,0:T(8,128)(2,1)S(1)} %fusion.36), channel_id=1, source_target_pairs={{0,64},{64,128},{128,192},{192,256},{256,320},{320,384},{384,448},... | collective-permute-start | bytes 98312 | tf_op jit(solution)/shard_map/ppermute | solution.py:20
  116.6 11.3 %copy-start.9 = (s32[128,10]{0,1:T(8,128)S(1)}, s32[128,10]{0,1:T(8,128)}, u32[]{:S(2)}) copy-start(s32[128,10]{0,1:T(8,128)} %param.27) | copy-start | bytes 15364
  116.7 11.4 %copy-start.3 = (f32[128,10]{0,1:T(8,128)S(1)}, f32[128,10]{0,1:T(8,128)}, u32[]{:S(2)}) copy-start(f32[128,10]{0,1:T(8,128)} %param.28) | copy-start | bytes 15364
  116.7 86.9 %all-to-all-start.1 = ((bf16[512,24,128]{2,1,0:T(8,128)(2,1)}), bf16[512,24,128]{2,1,0:T(8,128)(2,1)S(1)}, u32[]{:S(2)}, u32[]{:S(2)}) async-start(bf16[512,24,128]{2,1,0:T(8,128)(2,1)} %bitcast.221), calls=%async_computation.1 | async-start | bytes 6291456 | tf_op jit(solution)/shard_map/all_to_all | solution.py:365
  128.0 30.5 %copy-start.12 = (f32[128]{0:T(128)S(1)}, f32[128]{0:T(128)}, u32[]{:S(2)}) copy-start(f32[128]{0:T(128)} %param.25) | copy-start | bytes 1540
  128.7 0.7 copy-start.1
  129.4 0.8 copy-start.2
  203.6 1.6 copy-start.4

commit v3 on v0

v3 whole, which is shorter than its diff:
```python
import functools
import math

import jax
import jax.numpy as jnp
from jax import lax
from jax.experimental import pallas as pl
from jax.experimental.pallas import tpu as pltpu
from jax.sharding import PartitionSpec as P

TOP_PRECISION = lax.Precision.HIGHEST
NORM_EPSILON = 1e-06
CAPACITY = 3
CORES = 2
LANES = 128
META_ROWS = 16
VMEM_BYTES = 60 * 1024 * 1024


def passed_along(block, axis, distance):
    devices = range(lax.axis_size(axis))
    route = [(i - distance, i) for i in devices if i - distance in devices]
    return lax.ppermute(block, axis, route)


def block_parts(queries, key_vectors, values, write_strength, log_fading_factor, block_inverse):
    tracks, length, head_width = queries.shape
    block_size = block_inverse.shape[-1]
    blocks = length // block_size
    shape_four = (tracks, blocks, block_size, head_width)
    query_blocks = queries.reshape(shape_four)
    key_blocks = key_vectors.reshape(shape_four)
    value_blocks = values.reshape(shape_four)
    strength = write_strength.reshape(tracks, blocks, block_size)
    running = jnp.cumsum(log_fading_factor.reshape(tracks, blocks, block_size), axis=-1)
    growth = jnp.exp(running)
    final_log = running[..., -1:]
    write_keys = jnp.einsum(
        "sbij,sbjh->sbih",
        block_inverse,
        key_blocks * (strength * growth)[..., None],
        precision=TOP_PRECISION,
    )
    write_values = jnp.einsum(
        "sbij,sbjh->sbih",
        block_inverse,
        value_blocks * strength[..., None],
        precision=TOP_PRECISION,
    )
    faded_keys = key_blocks * jnp.exp(final_log - running)[..., None]
    faded_queries = query_blocks * growth[..., None]
    row_index = lax.broadcasted_iota(jnp.int32, (block_size, block_size), 0)
    col_index = lax.broadcasted_iota(jnp.int32, (block_size, block_size), 1)
    spread = running[..., :, None] - running[..., None, :]
    causal_fade = jnp.where(row_index >= col_index, jnp.exp(jnp.minimum(spread, 0.0)), 0.0)
    causal = (
        jnp.einsum("sbih,sbjh->sbij", query_blocks, key_blocks, precision=TOP_PRECISION)
        * causal_fade
    )
    return (faded_queries, write_keys, write_values, faded_keys, causal, jnp.exp(final_log))


def block_step(states, pieces):
    faded_queries, write_keys, write_values, faded_keys, causal, decays = pieces
    fresh_values = write_values - jnp.einsum(
        "sch,shv->scv", write_keys, states, precision=TOP_PRECISION
    )
    attended = jnp.einsum("sch,shv->scv", faded_queries, states, precision=TOP_PRECISION)
    attended = attended + jnp.einsum("sij,sjv->siv", causal, fresh_values, precision=TOP_PRECISION)
    states = decays[..., None] * states + jnp.einsum(
        "sch,scv->shv", faded_keys, fresh_values, precision=TOP_PRECISION
    )
    return (states, attended)


def run_blocks(pieces, states):
    moved = tuple((jnp.moveaxis(piece_item, 1, 0) for piece_item in pieces))
    states, attended = lax.scan(block_step, states, moved)
    return (states, jnp.moveaxis(attended, 0, 1))


def gated_norm(attended, norm_gain, out_gate):
    root_mean = jnp.sqrt(jnp.mean(attended * attended, axis=-1, keepdims=True) + NORM_EPSILON)
    return attended / root_mean * norm_gain * jax.nn.silu(out_gate)


def compose(carried, block_piece):
    current_mapping, current_addend = carried
    segment_mapping, segment_addend = block_piece
    updated_mapping = jnp.einsum(
        "qfz,qze->qfe", segment_mapping, current_mapping, precision=TOP_PRECISION
    )
    updated_addend = (
        jnp.einsum("qfz,qze->qfe", segment_mapping, current_addend, precision=TOP_PRECISION)
        + segment_addend
    )
    return ((updated_mapping, updated_addend), None)


def delta_front(queries, key_vectors, values, write_strength, log_fading_factor, block_inverse):
    tracks, length, head_width = queries.shape
    pieces = block_parts(
        queries, key_vectors, values, write_strength, log_fading_factor, block_inverse
    )
    faded_queries, write_keys, write_values, faded_keys, causal, decays = pieces
    unit_matrix = jnp.eye(head_width, dtype=jnp.float32)
    identity_map = jnp.broadcast_to(unit_matrix, (tracks, head_width, head_width))
    block_maps = decays[..., None] * unit_matrix - jnp.einsum(
        "sbch,sbck->sbhk", faded_keys, write_keys, precision=TOP_PRECISION
    )
    block_adds = jnp.einsum("sbch,sbcv->sbhv", faded_keys, write_values, precision=TOP_PRECISION)
    (section_mapping, section_addend), _ = lax.scan(
        compose,
        (identity_map, jnp.zeros_like(identity_map)),
        (jnp.moveaxis(block_maps, 1, 0), jnp.moveaxis(block_adds, 1, 0)),
    )
    incoming_state = jnp.zeros_like(section_addend)
    for relay_turn in range(lax.axis_size("ctx") - 1):
        departing_state = (
            jnp.einsum("qfz,qze->qfe", section_mapping, incoming_state, precision=TOP_PRECISION)
            + section_addend
        )
        incoming_state = passed_along(departing_state.astype(jnp.bfloat16), "ctx", 1).astype(
            departing_state.dtype
        )
    return pieces, incoming_state


def device_of(x, core, y, z, side):
    return ((x * CORES + core) * side + y) * side + z


def line_groups(chips, side):
    first = [[device_of(x, 0, y, z, side) for y in range(side)] for x in range(chips) for z in range(side)]
    second = [[device_of(x, 1, y, z, side) for z in range(side)] for x in range(chips) for y in range(side)]
    return first + second


def plane_groups(chips, side):
    first = [[device_of(x, 0, y, z, side) for x in range(chips) for z in range(side)] for y in range(side)]
    second = [[device_of(x, 1, y, z, side) for x in range(chips) for y in range(side)] for z in range(side)]
    return first + second


def exchange(rows, groups):
    return lax.all_to_all(
        rows, ("ctx", "exp"), split_axis=0, concat_axis=0, tiled=True, axis_index_groups=groups
    )


def head_kernel(experts, picks_ref, line_ref, place_ref, weights_ref, hidden_ref, out_ref, block_ref):
    tokens = hidden_ref.shape[0]
    top = picks_ref.shape[0]

    @pl.when(pl.program_id(0) == 0)
    def _():
        picks = picks_ref[...]
        row = lax.broadcasted_iota(jnp.int32, (experts, tokens), 0)
        named = jnp.zeros((experts, tokens), jnp.bool_)
        for pick in range(top):
            named = jnp.logical_or(named, picks[pick : pick + 1, :] == row)
        before = lax.broadcasted_iota(jnp.int32, (tokens, tokens), 0) < lax.broadcasted_iota(
            jnp.int32, (tokens, tokens), 1
        )
        earlier = jnp.dot(
            named.astype(jnp.float32).astype(jnp.bfloat16),
            before.astype(jnp.float32).astype(jnp.bfloat16),
            preferred_element_type=jnp.float32,
        )
        slot = jnp.concatenate(
            [
                jnp.sum(
                    jnp.where(picks[pick : pick + 1, :] == row, earlier, 0.0), axis=0, keepdims=True
                )
                for pick in range(top)
            ],
            axis=0,
        )
        weights = weights_ref[...]
        high = weights.astype(jnp.bfloat16).astype(jnp.float32)
        block_ref[...] = jnp.zeros_like(block_ref)
        block_ref[0:tokens, :] = hidden_ref[...].astype(jnp.float32)
        for column, item in enumerate(
            (line_ref[...], place_ref[0] + slot * place_ref[1], high, weights - high)
        ):
            block_ref[tokens : tokens + top, column * tokens : (column + 1) * tokens] = item

    out_ref[...] = block_ref[...].astype(jnp.bfloat16)


def head_rows(picks, line, place, weights, hidden, experts, copies):
    tokens, width = hidden.shape
    shape = (tokens + META_ROWS, width)
    return pl.pallas_call(
        functools.partial(head_kernel, experts),
        grid=(copies,),
        out_shape=jax.ShapeDtypeStruct((copies * shape[0], width), jnp.bfloat16),
        in_specs=[
            pl.BlockSpec(picks.shape, lambda i: (0, 0)),
            pl.BlockSpec(line.shape, lambda i: (0, 0)),
            pl.BlockSpec(place.shape, lambda i: (0, 0, 0)),
            pl.BlockSpec(weights.shape, lambda i: (0, 0)),
            pl.BlockSpec(hidden.shape, lambda i: (0, 0)),
        ],
        out_specs=pl.BlockSpec(shape, lambda i: (i, 0)),
        scratch_shapes=[pltpu.VMEM(shape, jnp.float32)],
        compiler_params=pltpu.CompilerParams(vmem_limit_bytes=VMEM_BYTES),
        cost_estimate=pl.CostEstimate(
            flops=2 * experts * tokens * tokens, bytes_accessed=2 * copies * shape[0] * width, transcendentals=0
        ),
        name="head_rows",
    )(picks, line, place, weights, hidden)


def table_at(meta, mine, count, value):
    tokens = value.shape[1]
    row = lax.broadcasted_iota(jnp.int32, (count, tokens), 0).astype(jnp.float32)
    place = jnp.where(meta[:, 0:tokens] == mine, meta[:, tokens : 2 * tokens], -1.0)
    table = jnp.zeros((count, tokens), jnp.float32)
    for pick in range(value.shape[0]):
        table = jnp.where(place[pick : pick + 1, :] == row, value[pick : pick + 1, :], table)
    return table


def pack_kernel(top, mine_ref, meta_ref, data_ref, out_ref, table_ref, spread_ref):
    sources, tokens, _ = data_ref.shape
    count = table_ref.shape[1]
    near = count // CAPACITY
    lanes = spread_ref.shape[2]

    @pl.when(pl.program_id(0) == 0)
    def _():
        mine = mine_ref[0].astype(jnp.float32)
        for source in range(sources):
            meta = meta_ref[source].astype(jnp.float32)[0:top]
            ones = jnp.ones((top, tokens), jnp.float32)
            table_ref[source] = table_at(meta, mine, count, ones).astype(jnp.bfloat16)

    for source in range(sources):
        rows = jnp.dot(table_ref[source], data_ref[source], preferred_element_type=jnp.float32)
        for slot in range(CAPACITY):
            at = pl.ds(slot * sources + source, near, stride=CAPACITY * sources)
            for part in range(spread_ref.shape[0]):
                spread_ref[part, at, :] = rows[
                    slot * near : (slot + 1) * near, part * lanes : (part + 1) * lanes
                ]
    for part in range(spread_ref.shape[0]):
        out_ref[:, part * lanes : (part + 1) * lanes] = spread_ref[part].astype(jnp.bfloat16)


def pack_rows(mine, gathered, tokens, top, near, columns):
    sources, _, width = gathered.shape
    rows = near * CAPACITY * sources
    return pl.pallas_call(
        functools.partial(pack_kernel, top),
        grid=(width // columns,),
        out_shape=jax.ShapeDtypeStruct((rows, width), jnp.bfloat16),
        in_specs=[
            pl.BlockSpec(memory_space=pltpu.SMEM),
            pl.BlockSpec((sources, META_ROWS, 4 * tokens), lambda i: (0, tokens // META_ROWS, 0)),
            pl.BlockSpec((sources, tokens, columns), lambda i: (0, 0, i)),
        ],
        out_specs=pl.BlockSpec((rows, columns), lambda i: (0, i)),
        scratch_shapes=[
            pltpu.VMEM((sources, near * CAPACITY, tokens), jnp.bfloat16),
            pltpu.VMEM((columns // LANES, rows, LANES), jnp.float32),
        ],
        compiler_params=pltpu.CompilerParams(vmem_limit_bytes=VMEM_BYTES),
        cost_estimate=pl.CostEstimate(
            flops=2 * rows * tokens * width, bytes_accessed=4 * rows * width, transcendentals=0
        ),
        name="pack_rows",
    )(mine, gathered, gathered)


def expert_kernel(received_ref, *refs):
    weight_refs, out_ref, here = refs[:6], refs[6], refs[7:13]
    spread_ref, ready = refs[13:]
    loads = [
        pltpu.make_async_copy(there, place, ready.at[i])
        for i, (there, place) in enumerate(zip(weight_refs, here))
    ]
    first = pl.program_id(0) == 0

    @pl.when(first)
    def _():
        for load in loads:
            load.start()

    senders, each, width = spread_ref.shape
    half = each // CORES
    spread_ref[...] = received_ref[...].astype(jnp.float32).reshape(spread_ref.shape)
    for turn in range(CORES):
        at = pl.ds(turn * half, half)
        rows = spread_ref[:, at, :].reshape(senders * half, width).astype(jnp.bfloat16)

        @pl.when(first)
        def _():
            for load in loads[3 * turn : 3 * turn + 3]:
                load.wait()

        gate_here, up_here, down_here = here[3 * turn : 3 * turn + 3]
        gate = jnp.dot(rows, gate_here[...], preferred_element_type=jnp.float32)
        up = jnp.dot(rows, up_here[...], preferred_element_type=jnp.float32)
        active = (gate / (1.0 + jnp.exp(-gate)) * up).astype(jnp.bfloat16)
        produced = jnp.dot(active, down_here[...], preferred_element_type=jnp.float32)
        spread_ref[:, at, :] = produced.reshape(senders, half, width)
    out_ref[...] = spread_ref[...].reshape(out_ref.shape).astype(jnp.bfloat16)


def expert_rows(received, weights, senders, steps):
    rows, width = received.shape
    units = weights[0].shape[1]
    block = pl.BlockSpec((rows // steps, width), lambda i: (i, 0))
    whole = pl.BlockSpec(memory_space=pl.ANY)
    return pl.pallas_call(
        expert_kernel,
        grid=(steps,),
        out_shape=jax.ShapeDtypeStruct(received.shape, jnp.bfloat16),
        in_specs=[block] + [whole] * len(weights),
        out_specs=block,
        scratch_shapes=[pltpu.VMEM(weight.shape, jnp.bfloat16) for weight in weights]
        + [
            pltpu.VMEM((senders // steps, rows // senders, width), jnp.float32),
            pltpu.SemaphoreType.DMA((len(weights),)),
        ],
        compiler_params=pltpu.CompilerParams(vmem_limit_bytes=VMEM_BYTES),
        cost_estimate=pl.CostEstimate(
            flops=6 * rows * width * units,
            bytes_accessed=4 * rows * width + 12 * width * units,
            transcendentals=rows * units,
        ),
        name="expert_rows",
    )(received, *weights)


def combine_kernel(top, mine_ref, meta_ref, returned_ref, out_ref, high_ref, low_ref, spread_ref):
    sources, tokens, _ = out_ref.shape
    count = high_ref.shape[1]
    near = count // CAPACITY
    lanes = spread_ref.shape[2]

    @pl.when(pl.program_id(0) == 0)
    def _():
        mine = mine_ref[0].astype(jnp.float32)
        for source in range(sources):
            meta = meta_ref[source].astype(jnp.float32)[0:top]
            for column, table in ((2, high_ref), (3, low_ref)):
                value = meta[:, column * tokens : (column + 1) * tokens]
                table[source] = table_at(meta, mine, count, value).astype(jnp.bfloat16)

    for part in range(spread_ref.shape[0]):
        spread_ref[part] = returned_ref[:, part * lanes : (part + 1) * lanes].astype(jnp.float32)
    for source in range(sources):
        rows = jnp.concatenate(
            [
                jnp.concatenate(
                    [
                        spread_ref[
                            part,
                            pl.ds(slot * sources + source, near, stride=CAPACITY * sources),
                            :,
                        ]
                        for part in range(spread_ref.shape[0])
                    ],
                    axis=1,
                )
                for slot in range(CAPACITY)
            ],
            axis=0,
        ).astype(jnp.bfloat16)
        total = sum(
            lax.dot_general(
                table[source], rows, (((0,), (0,)), ((), ())), preferred_element_type=jnp.float32
            )
            for table in (high_ref, low_ref)
        )
        out_ref[source] = total.astype(jnp.bfloat16)


def combine_rows(mine, gathered, returned, tokens, top, columns):
    sources = gathered.shape[0]
    rows, width = returned.shape
    near = rows // CAPACITY // sources
    table = pltpu.VMEM((sources, near * CAPACITY, tokens), jnp.bfloat16)
    return pl.pallas_call(
        functools.partial(combine_kernel, top),
        grid=(width // columns,),
        out_shape=jax.ShapeDtypeStruct((sources, tokens, width), jnp.bfloat16),
        in_specs=[
            pl.BlockSpec(memory_space=pltpu.SMEM),
            pl.BlockSpec((sources, META_ROWS, 4 * tokens), lambda i: (0, tokens // META_ROWS, 0)),
            pl.BlockSpec((rows, columns), lambda i: (0, i)),
        ],
        out_specs=pl.BlockSpec((sources, tokens, columns), lambda i: (0, 0, i)),
        scratch_shapes=[table, table, pltpu.VMEM((columns // LANES, rows, LANES), jnp.float32)],
        compiler_params=pltpu.CompilerParams(vmem_limit_bytes=VMEM_BYTES),
        cost_estimate=pl.CostEstimate(
            flops=4 * rows * tokens * width, bytes_accessed=4 * rows * width, transcendentals=0
        ),
        name="combine_rows",
    )(mine, gathered, returned)


def body(
    queries,
    key_vectors,
    values,
    out_gate,
    write_strength,
    log_fading_factor,
    block_inverse,
    norm_gain,
    hidden,
    routes,
    route_weights,
    gate_weights,
    up_weights,
    down_weights,
):
    tokens, width = hidden.shape
    top = routes.shape[1]
    context_size = lax.axis_size("ctx")
    owner_count = lax.axis_size("exp")
    experts = context_size * owner_count
    chips = context_size // CORES
    side = math.isqrt(owner_count)
    near = chips * side * CORES
    lines, planes = line_groups(chips, side), plane_groups(chips, side)
    core = lax.axis_index("ctx") % CORES
    own_y, own_z = lax.axis_index("exp") // side, lax.axis_index("exp") % side
    mine = jnp.where(core == 0, own_y, own_z).astype(jnp.int32).reshape(1)

    picks = routes.T
    owner = picks % owner_count
    pick_y, pick_z = owner // side, owner % side
    context = picks // owner_count
    pick_x, pick_core = context // CORES, context % CORES
    line = jnp.where(core == 0, pick_y, pick_z).astype(jnp.float32)
    across = jnp.where(core == 0, pick_z, pick_y)
    place = (pick_x * side + across) * CORES + (pick_core + core) % CORES
    place = jnp.stack([place.astype(jnp.float32), jnp.full(place.shape, near, jnp.float32)])

    swap = [(i, i + 1 - 2 * (i % CORES)) for i in range(context_size)]
    own_weights = [gate_weights[0], up_weights[0], down_weights[0]]
    partner_weights = [lax.ppermute(weight, "ctx", swap) for weight in own_weights]

    sent = head_rows(picks, line, place, route_weights.T, hidden, experts, side)
    gathered = exchange(sent, lines).reshape(side, tokens + META_ROWS, width)
    outgoing = pack_rows(mine, gathered, tokens, top, near, width // 4)
    received = exchange(outgoing, planes)
    pieces, incoming_state = delta_front(
        queries, key_vectors, values, write_strength, log_fading_factor, block_inverse
    )
    received, incoming_state = lax.optimization_barrier((received, incoming_state))
    produced = expert_rows(received, own_weights + partner_weights, chips * side, 4)
    returned = exchange(produced, planes)
    partial = combine_rows(mine, gathered, returned, tokens, top, width // 4)
    partial = exchange(partial.reshape(side * tokens, width), lines).reshape(side, tokens, width)
    expert_output = jnp.sum(partial.astype(jnp.float32), axis=0).astype(jnp.bfloat16)
    _, attended = run_blocks(pieces, incoming_state)
    mixer_output = gated_norm(attended.reshape(out_gate.shape), norm_gain, out_gate)
    return (mixer_output, expert_output)


def solution(mesh):
    placed = (
        P("exp", "ctx", None),
        P("exp", "ctx", None),
        P("exp", "ctx", None),
        P("exp", "ctx", None),
        P("exp", "ctx"),
        P("exp", "ctx"),
        P("exp", "ctx", None, None),
        P(),
        P(("ctx", "exp"), None),
        P(("ctx", "exp"), None),
        P(("ctx", "exp"), None),
        P(("ctx", "exp"), None, None),
        P(("ctx", "exp"), None, None),
        P(("ctx", "exp"), None, None),
    )
    return jax.shard_map(
        body,
        mesh=mesh,
        in_specs=placed,
        out_specs=(P("exp", "ctx", None), P(("ctx", "exp"), None)),
        check_vma=False,
    )
```

time: 397 us -> 246 us (0.62)
  the two profiles are of different devices: /device:TPU:40 before, /device:TPU:1 now
where the time goes in v3:
time: 246 us; the launch traced here: 242 us
  waiting for transfers between devices  91.3 us (37%)
  starting transfers between devices  81.4 us (33%)
  Pallas kernels  28.7 us (12%)
  matrix products  25 us (10%)
  local copies, waits for them, and re-layouts  7.15 us (3%)
  other arithmetic  6.76 us (3%)
    all_to_all x4, waiting for transfers between devices, exchange(): lax.all_to_all(rows, ('ctx', 'exp'), split_axis=0, concat_axis=0, tiled=T...  78.7 us
    all_to_all x4, starting transfers between devices, exchange(): lax.all_to_all(rows, ('ctx', 'exp'), split_axis=0, concat_axis=0, tiled=T...  41.8 us
    ppermute x7, starting transfers between devices, passed_along(): return lax.ppermute(block, axis, route)  33.3 us
    ppermute x7, waiting for transfers between devices, passed_along(): return lax.ppermute(block, axis, route)  12.6 us
    pallas_call x1, Pallas kernels, expert_rows(): pl.pallas_call(expert_kernel, grid=(steps,), out_shape=jax.ShapeDtypeStru...  11.7 us
    dot_general x4, matrix products, block_step(): jnp.einsum('sch,scv->shv', faded_keys, fresh_values, precision=TOP_PRECIS...  6.82 us
    pallas_call x1, Pallas kernels, combine_rows(): pl.pallas_call(functools.partial(combine_kernel, top), grid=(width // col...  6.52 us
    ppermute x3, starting transfers between devices, body(): lax.ppermute(weight, 'ctx', swap)  6.25 us
  transfers between devices with their start and end apart: 14, of which 9 were waited for; matrix products, arithmetic and copies ran while one was open for 13% of the time, Pallas kernels for 0%

profile of v3, /device:TPU:1, one launch (start us, length us, event | category | flops | bytes accessed | tf_op | source)
XLA Modules:
  0.0 241.6 jit_solution(12532062359619377024)
XLA Ops:
  0.7 1.4 fusion.76
  2.6 4.7 %head_rows.1 = bf16[1152,1024]{1,0:T(8,128)(2,1)} custom-call(s32[10,128]{1,0:T(8,128)} %bitcast.238, f32[10,128]{1,0:T(8,128)} %get-tuple-element.143.line_ref, f32[2,10,128]{2,1,0:T(8,128)} %stack.7.place_ref, f32[10,128]{1,0:T(8,128)} %bitcast.239, bf16[128,1024]{1,0:T(8,128)(2,1)} %hidden_ref.1), custom_call_target="tpu_custom_call" | custom-call | flops 16777216 | bytes 2359296 | tf_op jit(solution)/shard_map/head_rows/pallas_call | solution.py:194
  7.4 10.9 %all-to-all-start = ((bf16[8,144,1024]{2,1,0:T(8,128)(2,1)}), bf16[8,144,1024]{2,1,0:T(8,128)(2,1)S(1)}, u32[]{:S(2)}, u32[]{:S(2)}) async-start(bf16[8,144,1024]{2,1,0:T(8,128)(2,1)} %bitcast.224), calls=%async_computation | async-start | bytes 4718592 | tf_op jit(solution)/shard_map/all_to_all | solution.py:146
  18.2 32.1 %all-to-all-done.meta_ref.data_ref = bf16[8,144,1024]{2,1,0:T(8,128)(2,1)S(1)} async-done(((bf16[8,144,1024]{2,1,0:T(8,128)(2,1)}), bf16[8,144,1024]{2,1,0:T(8,128)(2,1)S(1)}, u32[]{:S(2)}, u32[]{:S(2)}) %all-to-all-start) | async-done | bytes 2359328 | tf_op jit(solution)/shard_map/all_to_all | solution.py:146
  50.4 1.5 copy-done.1
  51.9 5.7 %pack_rows.1 = bf16[1536,1024]{1,0:T(8,128)(2,1)} custom-call(s32[1]{0:T(128)} %bitcast.15.mine_ref, bf16[8,144,1024]{2,1,0:T(8,128)(2,1)} %copy-done.1, bf16[8,144,1024]{2,1,0:T(8,128)(2,1)} %copy-done.1), custom_call_target="tpu_custom_call" | custom-call | flops 402653184 | bytes 6291456 | tf_op jit(solution)/shard_map/pack_rows/pallas_call | solution.py:254
  57.6 9.7 %all-to-all-start.1 = ((bf16[32,48,1024]{2,1,0:T(8,128)(2,1)}), bf16[32,48,1024]{2,1,0:T(8,128)(2,1)}, u32[]{:S(2)}, u32[]{:S(2)}) async-start(bf16[32,48,1024]{2,1,0:T(8,128)(2,1)} %bitcast.222), calls=%async_computation.1 | async-start | bytes 6291456 | tf_op jit(solution)/shard_map/all_to_all | solution.py:146
  72.0 1.9 while.24
  74.1 5.7 %collective-permute-start = (bf16[1,128,128]{2,1,0:T(8,128)(2,1)S(1)}, bf16[1,128,128]{2,1,0:T(8,128)(2,1)S(1)}, u32[]{:S(2)}, u32[]{:S(2)}) collective-permute-start(bf16[1,128,128]{2,1,0:T(8,128)(2,1)S(1)} %fusion.42), channel_id=1, source_target_pairs={{0,64},{64,128},{128,192},{192,256},{256,320},{320,384},{384,448},... | collective-permute-start | bytes 98312 | tf_op jit(solution)/shard_map/ppermute | solution.py:23
  79.7 3.0 %collective-permute-done = bf16[1,128,128]{2,1,0:T(8,128)(2,1)S(1)} collective-permute-done((bf16[1,128,128]{2,1,0:T(8,128)(2,1)S(1)}, bf16[1,128,128]{2,1,0:T(8,128)(2,1)S(1)}, u32[]{:S(2)}, u32[]{:S(2)}) %collective-permute-start) | collective-permute-done | bytes 32800 | tf_op jit(solution)/shard_map/ppermute | solution.py:23
  82.9 4.4 %collective-permute-start.1 = (bf16[1,128,128]{2,1,0:T(8,128)(2,1)S(1)}, bf16[1,128,128]{2,1,0:T(8,128)(2,1)S(1)}, u32[]{:S(2)}, u32[]{:S(2)}) collective-permute-start(bf16[1,128,128]{2,1,0:T(8,128)(2,1)S(1)} %fusion.41), channel_id=1, source_target_pairs={{0,64},{64,128},{128,192},{192,256},{256,320},{320,384},{384,448},... | collective-permute-start | bytes 98312 | tf_op jit(solution)/shard_map/ppermute | solution.py:23
  87.3 5.5 %collective-permute-done.1 = bf16[1,128,128]{2,1,0:T(8,128)(2,1)S(1)} collective-permute-done((bf16[1,128,128]{2,1,0:T(8,128)(2,1)S(1)}, bf16[1,128,128]{2,1,0:T(8,128)(2,1)S(1)}, u32[]{:S(2)}, u32[]{:S(2)}) %collective-permute-start.1) | collective-permute-done | bytes 32800 | tf_op jit(solution)/shard_map/ppermute | solution.py:23
  93.1 4.4 %collective-permute-start.2 = (bf16[1,128,128]{2,1,0:T(8,128)(2,1)S(1)}, bf16[1,128,128]{2,1,0:T(8,128)(2,1)S(1)}, u32[]{:S(2)}, u32[]{:S(2)}) collective-permute-start(bf16[1,128,128]{2,1,0:T(8,128)(2,1)S(1)} %fusion.40), channel_id=1, source_target_pairs={{0,64},{64,128},{128,192},{192,256},{256,320},{320,384},{384,448},... | collective-permute-start | bytes 98312 | tf_op jit(solution)/shard_map/ppermute | solution.py:23
  97.5 1.9 collective-permute-start.7
  99.4 2.4 collective-permute-start.8
  101.8 1.9 collective-permute-start.9
  104.0 6.2 %collective-permute-start.3 = (bf16[1,128,128]{2,1,0:T(8,128)(2,1)S(1)}, bf16[1,128,128]{2,1,0:T(8,128)(2,1)S(1)}, u32[]{:S(2)}, u32[]{:S(2)}) collective-permute-start(bf16[1,128,128]{2,1,0:T(8,128)(2,1)S(1)} %fusion.39), channel_id=1, source_target_pairs={{0,64},{64,128},{128,192},{192,256},{256,320},{320,384},{384,448},... | collective-permute-start | bytes 98312 | tf_op jit(solution)/shard_map/ppermute | solution.py:23
  110.2 1.0 collective-permute-done.3
  111.4 4.2 %collective-permute-start.4 = (bf16[1,128,128]{2,1,0:T(8,128)(2,1)S(1)}, bf16[1,128,128]{2,1,0:T(8,128)(2,1)S(1)}, u32[]{:S(2)}, u32[]{:S(2)}) collective-permute-start(bf16[1,128,128]{2,1,0:T(8,128)(2,1)S(1)} %fusion.38), channel_id=1, source_target_pairs={{0,64},{64,128},{128,192},{192,256},{256,320},{320,384},{384,448},... | collective-permute-start | bytes 98312 | tf_op jit(solution)/shard_map/ppermute | solution.py:23
  115.6 1.0 collective-permute-done.4
  116.8 4.2 %collective-permute-start.5 = (bf16[1,128,128]{2,1,0:T(8,128)(2,1)S(1)}, bf16[1,128,128]{2,1,0:T(8,128)(2,1)S(1)}, u32[]{:S(2)}, u32[]{:S(2)}) collective-permute-start(bf16[1,128,128]{2,1,0:T(8,128)(2,1)S(1)} %fusion.37), channel_id=1, source_target_pairs={{0,64},{64,128},{128,192},{192,256},{256,320},{320,384},{384,448},... | collective-permute-start | bytes 98312 | tf_op jit(solution)/shard_map/ppermute | solution.py:23
  121.0 1.0 collective-permute-done.5
  122.2 4.2 %collective-permute-start.6 = (bf16[1,128,128]{2,1,0:T(8,128)(2,1)S(1)}, bf16[1,128,128]{2,1,0:T(8,128)(2,1)S(1)}, u32[]{:S(2)}, u32[]{:S(2)}) collective-permute-start(bf16[1,128,128]{2,1,0:T(8,128)(2,1)S(1)} %fusion.36), channel_id=1, source_target_pairs={{0,64},{64,128},{128,192},{192,256},{256,320},{320,384},{384,448},... | collective-permute-start | bytes 98312 | tf_op jit(solution)/shard_map/ppermute | solution.py:23
  126.4 1.0 collective-permute-done.6
  127.5 11.7 %expert_rows.1 = bf16[1536,1024]{1,0:T(8,128)(2,1)} custom-call(bf16[1536,1024]{1,0:T(8,128)(2,1)} %bitcast.21.received_ref, bf16[1024,512]{1,0:T(8,128)(2,1)} %bitcast.241, bf16[1024,512]{1,0:T(8,128)(2,1)} %bitcast.243, bf16[512,1024]{1,0:T(8,128)(2,1)} %bitcast.246, bf16[1024,512]{1,0:T(8,128)(2,1)} %collective-permute-done.7.refs_3_, ...), custom_call_target="tpu_custom_call" | custom-call | flops 4831838208 | bytes 12582912 | tf_op jit(solution)/shard_map/expert_rows/pallas_call | solution.py:316
  139.2 11.6 %all-to-all-start.2 = ((bf16[32,48,1024]{2,1,0:T(8,128)(2,1)}), bf16[32,48,1024]{2,1,0:T(8,128)(2,1)S(1)}, u32[]{:S(2)}, u32[]{:S(2)}) async-start(bf16[32,48,1024]{2,1,0:T(8,128)(2,1)} %bitcast.230), calls=%async_computation.2 | async-start | bytes 6291456 | tf_op jit(solution)/shard_map/all_to_all | solution.py:146
  150.8 1.9 fusion.28
  152.7 1.7 broadcast_multiply_fusion
  154.5 38.9 %all-to-all-done.2 = bf16[32,48,1024]{2,1,0:T(8,128)(2,1)S(1)} async-done(((bf16[32,48,1024]{2,1,0:T(8,128)(2,1)}), bf16[32,48,1024]{2,1,0:T(8,128)(2,1)S(1)}, u32[]{:S(2)}, u32[]{:S(2)}) %all-to-all-start.2) | async-done | bytes 3145760 | tf_op jit(solution)/shard_map/all_to_all | solution.py:146
  193.4 1.6 copy-done.2
  195.0 6.5 %combine_rows.1 = bf16[8,128,1024]{2,1,0:T(8,128)(2,1)} custom-call(s32[1]{0:T(128)} %bitcast.15.mine_ref, bf16[8,144,1024]{2,1,0:T(8,128)(2,1)} %copy-done.1, bf16[1536,1024]{1,0:T(8,128)(2,1)} %bitcast.223), custom_call_target="tpu_custom_call" | custom-call | flops 805306368 | bytes 6291456 | tf_op jit(solution)/shard_map/combine_rows/pallas_call | solution.py:386
  201.5 9.6 %all-to-all-start.3 = ((bf16[8,128,1024]{2,1,0:T(8,128)(2,1)}), bf16[8,128,1024]{2,1,0:T(8,128)(2,1)S(1)}, u32[]{:S(2)}, u32[]{:S(2)}) async-start(bf16[8,128,1024]{2,1,0:T(8,128)(2,1)} %combine_rows.1), calls=%async_computation.3 | async-start | bytes 4194304 | tf_op jit(solution)/shard_map/all_to_all | solution.py:146
  211.2 20.7 %while.25 = (s32[]{:T(128)}, f32[1,128,128]{2,1,0:T(8,128)S(1)}, f32[4,1,64,128]{3,2,1,0:T(8,128)S(1)}, f32[4,1,1]{0,2,1:T(1,128)S(1)}, f32[4,1,64,128]{3,2,1,0:...) while((s32[]{:T(128)}, f32[1,128,128]{2,1,0:T(8,128)S(1)}, ...), condition=%wide.region_4.5_spmd, body=%wide.region_3.4_spmd.sunk | while | flops 44089344 | bytes 625281 | solution.py:78
  211.2 0.9 fusion.123
  212.1 1.0 convolution_subtract_fusion.3
  213.7 1.7 fusion.122
  215.4 0.9 fusion.124
  216.4 0.9 fusion.123
  217.3 1.0 convolution_subtract_fusion.3
  218.9 1.7 fusion.122
  221.5 0.9 fusion.123
  222.5 1.0 convolution_subtract_fusion.3
  224.0 1.7 fusion.122
  226.7 0.9 fusion.123
  227.6 1.0 convolution_subtract_fusion.3
  229.2 1.7 fusion.122
  232.8 7.7 %all-to-all-done.3 = bf16[8,128,1024]{2,1,0:T(8,128)(2,1)S(1)} async-done(((bf16[8,128,1024]{2,1,0:T(8,128)(2,1)}), bf16[8,128,1024]{2,1,0:T(8,128)(2,1)S(1)}, u32[]{:S(2)}, u32[]{:S(2)}) %all-to-all-start.3) | async-done | bytes 2097184 | tf_op jit(solution)/shard_map/all_to_all | solution.py:146
  240.5 1.1 reduce_sum.22
  (84 shorter events, 14.3 us)
Async XLA Ops:
  0.6 69.2 %copy-start = (f32[1,4,64,64]{3,2,1,0:T(8,128)S(1)}, f32[1,4,64,64]{3,2,1,0:T(8,128)}, u32[]{:S(2)}) copy-start(f32[1,4,64,64]{3,2,1,0:T(8,128)} %param.24) | copy-start | bytes 196612
  7.4 43.0 %all-to-all-start = ((bf16[8,144,1024]{2,1,0:T(8,128)(2,1)}), bf16[8,144,1024]{2,1,0:T(8,128)(2,1)S(1)}, u32[]{:S(2)}, u32[]{:S(2)}) async-start(bf16[8,144,1024]{2,1,0:T(8,128)(2,1)} %bitcast.224), calls=%async_computation | async-start | bytes 4718592 | tf_op jit(solution)/shard_map/all_to_all | solution.py:146
  50.4 1.5 copy-start.1
  57.6 10.2 %copy-start.9 = (f32[1,256]{1,0:T(1,128)S(1)}, f32[1,256]{1,0:T(1,128)}, u32[]{:S(2)}) copy-start(f32[1,256]{1,0:T(1,128)} %param.23) | copy-start | bytes 3076
  57.6 11.0 %copy-start.10 = (f32[1,256]{1,0:T(1,128)S(1)}, f32[1,256]{1,0:T(1,128)}, u32[]{:S(2)}) copy-start(f32[1,256]{1,0:T(1,128)} %param.22) | copy-start | bytes 3076
  57.6 12.3 %copy-start.7 = (f32[1,256,128]{2,1,0:T(8,128)S(1)}, f32[1,256,128]{2,1,0:T(8,128)}, u32[]{:S(2)}) copy-start(f32[1,256,128]{2,1,0:T(8,128)} %param.20) | copy-start | bytes 393220
  57.6 12.6 %copy-start.3 = (f32[1,256,128]{2,1,0:T(8,128)S(1)}, f32[1,256,128]{2,1,0:T(8,128)}, u32[]{:S(2)}) copy-start(f32[1,256,128]{2,1,0:T(8,128)} %param.19) | copy-start | bytes 393220
  57.6 69.9 %all-to-all-start.1 = ((bf16[32,48,1024]{2,1,0:T(8,128)(2,1)}), bf16[32,48,1024]{2,1,0:T(8,128)(2,1)}, u32[]{:S(2)}, u32[]{:S(2)}) async-start(bf16[32,48,1024]{2,1,0:T(8,128)(2,1)} %bitcast.222), calls=%async_computation.1 | async-start | bytes 6291456 | tf_op jit(solution)/shard_map/all_to_all | solution.py:146
  69.8 27.7 %copy-start.12 = (bf16[1,1024,512]{2,1,0:T(8,128)(2,1)S(1)}, bf16[1,1024,512]{2,1,0:T(8,128)(2,1)}, u32[]{:S(2)}) copy-start(bf16[1,1024,512]{2,1,0:T(8,128)(2,1)} %param.29) | copy-start | bytes 3145732
  69.8 29.6 %copy-start.13 = (bf16[1,1024,512]{2,1,0:T(8,128)(2,1)S(1)}, bf16[1,1024,512]{2,1,0:T(8,128)(2,1)}, u32[]{:S(2)}) copy-start(bf16[1,1024,512]{2,1,0:T(8,128)(2,1)} %param.30) | copy-start | bytes 3145732
  70.2 1.1 copy-start.4
  71.2 0.7 copy-start.5
  74.1 8.7 %collective-permute-start = (bf16[1,128,128]{2,1,0:T(8,128)(2,1)S(1)}, bf16[1,128,128]{2,1,0:T(8,128)(2,1)S(1)}, u32[]{:S(2)}, u32[]{:S(2)}) collective-permute-start(bf16[1,128,128]{2,1,0:T(8,128)(2,1)S(1)} %fusion.42), channel_id=1, source_target_pairs={{0,64},{64,128},{128,192},{192,256},{256,320},{320,384},{384,448},... | collective-permute-start | bytes 98312 | tf_op jit(solution)/shard_map/ppermute | solution.py:23
  82.9 9.9 %collective-permute-start.1 = (bf16[1,128,128]{2,1,0:T(8,128)(2,1)S(1)}, bf16[1,128,128]{2,1,0:T(8,128)(2,1)S(1)}, u32[]{:S(2)}, u32[]{:S(2)}) collective-permute-start(bf16[1,128,128]{2,1,0:T(8,128)(2,1)S(1)} %fusion.41), channel_id=1, source_target_pairs={{0,64},{64,128},{128,192},{192,256},{256,320},{320,384},{384,448},... | collective-permute-start | bytes 98312 | tf_op jit(solution)/shard_map/ppermute | solution.py:23
  93.1 10.7 %collective-permute-start.2 = (bf16[1,128,128]{2,1,0:T(8,128)(2,1)S(1)}, bf16[1,128,128]{2,1,0:T(8,128)(2,1)S(1)}, u32[]{:S(2)}, u32[]{:S(2)}) collective-permute-start(bf16[1,128,128]{2,1,0:T(8,128)(2,1)S(1)} %fusion.40), channel_id=1, source_target_pairs={{0,64},{64,128},{128,192},{192,256},{256,320},{320,384},{384,448},... | collective-permute-start | bytes 98312 | tf_op jit(solution)/shard_map/ppermute | solution.py:23
  97.5 29.9 %collective-permute-start.7 = (bf16[1024,512]{1,0:T(8,128)(2,1)S(1)}, bf16[1024,512]{1,0:T(8,128)(2,1)}, u32[]{:S(2)}, u32[]{:S(2)}) collective-permute-start(bf16[1024,512]{1,0:T(8,128)(2,1)S(1)} %bitcast.242), channel_id=1, source_target_pairs={{0,64},{64,0},{128,192},{192,128},{256,320},{320,256},{384,448},{4... | collective-permute-start | bytes 3145736 | tf_op jit(solution)/shard_map/ppermute | solution.py:446
  99.4 28.0 %collective-permute-start.8 = (bf16[1024,512]{1,0:T(8,128)(2,1)S(1)}, bf16[1024,512]{1,0:T(8,128)(2,1)}, u32[]{:S(2)}, u32[]{:S(2)}) collective-permute-start(bf16[1024,512]{1,0:T(8,128)(2,1)S(1)} %bitcast.244), channel_id=1, source_target_pairs={{0,64},{64,0},{128,192},{192,128},{256,320},{320,256},{384,448},{4... | collective-permute-start | bytes 3145736 | tf_op jit(solution)/shard_map/ppermute | solution.py:446
  101.8 25.6 %collective-permute-start.9 = (bf16[512,1024]{1,0:T(8,128)(2,1)}, bf16[512,1024]{1,0:T(8,128)(2,1)}, u32[]{:S(2)}, u32[]{:S(2)}) collective-permute-start(bf16[512,1024]{1,0:T(8,128)(2,1)} %bitcast.245), channel_id=1, source_target_pairs={{0,64},{64,0},{128,192},{192,128},{256,320},{320,256},{384,448},{4... | collective-permute-start | bytes 3145736 | tf_op jit(solution)/shard_map/ppermute | solution.py:446
  104.0 7.2 %collective-permute-start.3 = (bf16[1,128,128]{2,1,0:T(8,128)(2,1)S(1)}, bf16[1,128,128]{2,1,0:T(8,128)(2,1)S(1)}, u32[]{:S(2)}, u32[]{:S(2)}) collective-permute-start(bf16[1,128,128]{2,1,0:T(8,128)(2,1)S(1)} %fusion.39), channel_id=1, source_target_pairs={{0,64},{64,128},{128,192},{192,256},{256,320},{320,384},{384,448},... | collective-permute-start | bytes 98312 | tf_op jit(solution)/shard_map/ppermute | solution.py:23
  111.4 5.2 %collective-permute-start.4 = (bf16[1,128,128]{2,1,0:T(8,128)(2,1)S(1)}, bf16[1,128,128]{2,1,0:T(8,128)(2,1)S(1)}, u32[]{:S(2)}, u32[]{:S(2)}) collective-permute-start(bf16[1,128,128]{2,1,0:T(8,128)(2,1)S(1)} %fusion.38), channel_id=1, source_target_pairs={{0,64},{64,128},{128,192},{192,256},{256,320},{320,384},{384,448},... | collective-permute-start | bytes 98312 | tf_op jit(solution)/shard_map/ppermute | solution.py:23
  116.8 5.2 %collective-permute-start.5 = (bf16[1,128,128]{2,1,0:T(8,128)(2,1)S(1)}, bf16[1,128,128]{2,1,0:T(8,128)(2,1)S(1)}, u32[]{:S(2)}, u32[]{:S(2)}) collective-permute-start(bf16[1,128,128]{2,1,0:T(8,128)(2,1)S(1)} %fusion.37), channel_id=1, source_target_pairs={{0,64},{64,128},{128,192},{192,256},{256,320},{320,384},{384,448},... | collective-permute-start | bytes 98312 | tf_op jit(solution)/shard_map/ppermute | solution.py:23
  122.2 5.2 %collective-permute-start.6 = (bf16[1,128,128]{2,1,0:T(8,128)(2,1)S(1)}, bf16[1,128,128]{2,1,0:T(8,128)(2,1)S(1)}, u32[]{:S(2)}, u32[]{:S(2)}) collective-permute-start(bf16[1,128,128]{2,1,0:T(8,128)(2,1)S(1)} %fusion.36), channel_id=1, source_target_pairs={{0,64},{64,128},{128,192},{192,256},{256,320},{320,384},{384,448},... | collective-permute-start | bytes 98312 | tf_op jit(solution)/shard_map/ppermute | solution.py:23
  139.2 54.2 %all-to-all-start.2 = ((bf16[32,48,1024]{2,1,0:T(8,128)(2,1)}), bf16[32,48,1024]{2,1,0:T(8,128)(2,1)S(1)}, u32[]{:S(2)}, u32[]{:S(2)}) async-start(bf16[32,48,1024]{2,1,0:T(8,128)(2,1)} %bitcast.230), calls=%async_computation.2 | async-start | bytes 6291456 | tf_op jit(solution)/shard_map/all_to_all | solution.py:146
  193.4 1.7 copy-start.2
  201.5 9.6 %copy-start.6 = (f32[4,1,64,128]{3,2,1,0:T(8,128)S(1)}, f32[4,1,64,128]{3,2,1,0:T(8,128)}, u32[]{:S(2)}) copy-start(f32[4,1,64,128]{3,2,1,0:T(8,128)} %custom-call) | copy-start | bytes 393220
  201.5 30.5 %copy-start.8 = (f32[1,256,128]{2,1,0:T(8,128)S(1)}, f32[1,256,128]{2,1,0:T(8,128)}, u32[]{:S(2)}) copy-start(f32[1,256,128]{2,1,0:T(8,128)} %param.21) | copy-start | bytes 393220
  201.5 30.5 %copy-start.11 = (f32[128]{0:T(128)S(1)}, f32[128]{0:T(128)}, u32[]{:S(2)}) copy-start(f32[128]{0:T(128)} %param.25) | copy-start | bytes 1540
  201.5 39.0 %all-to-all-start.3 = ((bf16[8,128,1024]{2,1,0:T(8,128)(2,1)}), bf16[8,128,1024]{2,1,0:T(8,128)(2,1)S(1)}, u32[]{:S(2)}, u32[]{:S(2)}) async-start(bf16[8,128,1024]{2,1,0:T(8,128)(2,1)} %combine_rows.1), calls=%async_computation.3 | async-start | bytes 4194304 | tf_op jit(solution)/shard_map/all_to_all | solution.py:146

commit v4 on v3

--- a/solution.py
+++ b/solution.py
@@ -14,13 +14,7 @@
 CORES = 2
 LANES = 128
 META_ROWS = 16
-VMEM_BYTES = 60 * 1024 * 1024
-
-
-def passed_along(block, axis, distance):
-    devices = range(lax.axis_size(axis))
-    route = [(i - distance, i) for i in devices if i - distance in devices]
-    return lax.ppermute(block, axis, route)
+VMEM_BYTES = 40 * 1024 * 1024
 
 
 def block_parts(queries, key_vectors, values, write_strength, log_fading_factor, block_inverse):
@@ -114,16 +108,17 @@
         (identity_map, jnp.zeros_like(identity_map)),
         (jnp.moveaxis(block_maps, 1, 0), jnp.moveaxis(block_adds, 1, 0)),
     )
-    incoming_state = jnp.zeros_like(section_addend)
-    for relay_turn in range(lax.axis_size("ctx") - 1):
-        departing_state = (
-            jnp.einsum("qfz,qze->qfe", section_mapping, incoming_state, precision=TOP_PRECISION)
-            + section_addend
-        )
-        incoming_state = passed_along(departing_state.astype(jnp.bfloat16), "ctx", 1).astype(
-            departing_state.dtype
-        )
-    return pieces, incoming_state
+    return pieces, jnp.concatenate([section_mapping, section_addend], axis=0)
+
+
+def entering_state(sections):
+    maps, addends = sections[:, 0], sections[:, 1]
+    mine = lax.axis_index("ctx")
+    state = addends[0]
+    for section in range(1, sections.shape[0] - 1):
+        later = jnp.dot(maps[section], state, precision=TOP_PRECISION) + addends[section]
+        state = jnp.where(section < mine, later, state)
+    return jnp.where(mine == 0, 0.0, state)[None]
 
 
 def device_of(x, core, y, z, side):
@@ -148,68 +143,50 @@
     )
 
 
-def head_kernel(experts, picks_ref, line_ref, place_ref, weights_ref, hidden_ref, out_ref, block_ref):
-    tokens = hidden_ref.shape[0]
-    top = picks_ref.shape[0]
-
-    @pl.when(pl.program_id(0) == 0)
-    def _():
-        picks = picks_ref[...]
-        row = lax.broadcasted_iota(jnp.int32, (experts, tokens), 0)
-        named = jnp.zeros((experts, tokens), jnp.bool_)
-        for pick in range(top):
-            named = jnp.logical_or(named, picks[pick : pick + 1, :] == row)
-        before = lax.broadcasted_iota(jnp.int32, (tokens, tokens), 0) < lax.broadcasted_iota(
-            jnp.int32, (tokens, tokens), 1
-        )
-        earlier = jnp.dot(
-            named.astype(jnp.float32).astype(jnp.bfloat16),
-            before.astype(jnp.float32).astype(jnp.bfloat16),
-            preferred_element_type=jnp.float32,
-        )
-        slot = jnp.concatenate(
-            [
-                jnp.sum(
-                    jnp.where(picks[pick : pick + 1, :] == row, earlier, 0.0), axis=0, keepdims=True
-                )
-                for pick in range(top)
-            ],
-            axis=0,
-        )
-        weights = weights_ref[...]
-        high = weights.astype(jnp.bfloat16).astype(jnp.float32)
-        block_ref[...] = jnp.zeros_like(block_ref)
-        block_ref[0:tokens, :] = hidden_ref[...].astype(jnp.float32)
-        for column, item in enumerate(
-            (line_ref[...], place_ref[0] + slot * place_ref[1], high, weights - high)
-        ):
-            block_ref[tokens : tokens + top, column * tokens : (column + 1) * tokens] = item
-
+def head_kernel(experts, picks_ref, line_ref, place_ref, weights_ref, out_ref, block_ref):
+    top, tokens = picks_ref.shape
+    picks = picks_ref[...]
+    row = lax.broadcasted_iota(jnp.int32, (experts, tokens), 0)
+    named = jnp.zeros((experts, tokens), jnp.bool_)
+    for pick in range(top):
+        named = jnp.logical_or(named, picks[pick : pick + 1, :] == row)
+    before = lax.broadcasted_iota(jnp.int32, (tokens, tokens), 0) < lax.broadcasted_iota(
+        jnp.int32, (tokens, tokens), 1
+    )
+    earlier = jnp.dot(
+        named.astype(jnp.float32).astype(jnp.bfloat16),
+        before.astype(jnp.float32).astype(jnp.bfloat16),
+        preferred_element_type=jnp.float32,
+    )
+    slot = jnp.concatenate(
+        [
+            jnp.sum(jnp.where(picks[pick : pick + 1, :] == row, earlier, 0.0), axis=0, keepdims=True)
+            for pick in range(top)
+        ],
+        axis=0,
+    )
+    weights = weights_ref[...]
+    high = weights.astype(jnp.bfloat16).astype(jnp.float32)
+    block_ref[...] = jnp.zeros_like(block_ref)
+    for column, item in enumerate(
+        (line_ref[...], place_ref[0] + slot * place_ref[1], high, weights - high)
+    ):
+        block_ref[0:top, column * tokens : (column + 1) * tokens] = item
     out_ref[...] = block_ref[...].astype(jnp.bfloat16)
 
 
-def head_rows(picks, line, place, weights, hidden, experts, copies):
-    tokens, width = hidden.shape
-    shape = (tokens + META_ROWS, width)
+def head_rows(picks, line, place, weights, experts):
+    shape = (META_ROWS, 4 * picks.shape[1])
     return pl.pallas_call(
         functools.partial(head_kernel, experts),
-        grid=(copies,),
-        out_shape=jax.ShapeDtypeStruct((copies * shape[0], width), jnp.bfloat16),
-        in_specs=[
-            pl.BlockSpec(picks.shape, lambda i: (0, 0)),
-            pl.BlockSpec(line.shape, lambda i: (0, 0)),
-            pl.BlockSpec(place.shape, lambda i: (0, 0, 0)),
-            pl.BlockSpec(weights.shape, lambda i: (0, 0)),
-            pl.BlockSpec(hidden.shape, lambda i: (0, 0)),
-        ],
-        out_specs=pl.BlockSpec(shape, lambda i: (i, 0)),
+        out_shape=jax.ShapeDtypeStruct(shape, jnp.bfloat16),
         scratch_shapes=[pltpu.VMEM(shape, jnp.float32)],
-        compiler_params=pltpu.CompilerParams(vmem_limit_bytes=VMEM_BYTES),
+        compiler_params=pltpu.CompilerParams(vmem_limit_bytes=16 * 1024 * 1024),
         cost_estimate=pl.CostEstimate(
-            flops=2 * experts * tokens * tokens, bytes_accessed=2 * copies * shape[0] * width, transcendentals=0
+            flops=60 * experts * picks.shape[1], bytes_accessed=65536, transcendentals=0
         ),
         name="head_rows",
-    )(picks, line, place, weights, hidden)
+    )(picks, line, place, weights)
 
 
 def table_at(meta, mine, count, value):
@@ -248,16 +225,16 @@
         out_ref[:, part * lanes : (part + 1) * lanes] = spread_ref[part].astype(jnp.bfloat16)
 
 
-def pack_rows(mine, gathered, tokens, top, near, columns):
-    sources, _, width = gathered.shape
+def pack_rows(mine, meta, data, top, near, columns):
+    sources, tokens, width = data.shape
     rows = near * CAPACITY * sources
     return pl.pallas_call(
         functools.partial(pack_kernel, top),
         grid=(width // columns,),
-        out_shape=jax.ShapeDtypeStruct((rows, width), jnp.bfloat16),
+        out_shape=pltpu.HBM((rows, width), jnp.bfloat16),
         in_specs=[
             pl.BlockSpec(memory_space=pltpu.SMEM),
-            pl.BlockSpec((sources, META_ROWS, 4 * tokens), lambda i: (0, tokens // META_ROWS, 0)),
+            pl.BlockSpec(meta.shape, lambda i: (0, 0, 0)),
             pl.BlockSpec((sources, tokens, columns), lambda i: (0, 0, i)),
         ],
         out_specs=pl.BlockSpec((rows, columns), lambda i: (0, i)),
@@ -270,7 +247,7 @@
             flops=2 * rows * tokens * width, bytes_accessed=4 * rows * width, transcendentals=0
         ),
         name="pack_rows",
-    )(mine, gathered, gathered)
+    )(mine, meta, data)
 
 
 def expert_kernel(received_ref, *refs):
@@ -316,7 +293,7 @@
     return pl.pallas_call(
         expert_kernel,
         grid=(steps,),
-        out_shape=jax.ShapeDtypeStruct(received.shape, jnp.bfloat16),
+        out_shape=pltpu.HBM(received.shape, jnp.bfloat16),
         in_specs=[block] + [whole] * len(weights),
         out_specs=block,
         scratch_shapes=[pltpu.VMEM(weight.shape, jnp.bfloat16) for weight in weights]
@@ -378,18 +355,18 @@
         out_ref[source] = total.astype(jnp.bfloat16)
 
 
-def combine_rows(mine, gathered, returned, tokens, top, columns):
-    sources = gathered.shape[0]
+def combine_rows(mine, meta, returned, tokens, top, columns):
+    sources = meta.shape[0]
     rows, width = returned.shape
     near = rows // CAPACITY // sources
     table = pltpu.VMEM((sources, near * CAPACITY, tokens), jnp.bfloat16)
     return pl.pallas_call(
         functools.partial(combine_kernel, top),
         grid=(width // columns,),
-        out_shape=jax.ShapeDtypeStruct((sources, tokens, width), jnp.bfloat16),
+        out_shape=pltpu.HBM((sources, tokens, width), jnp.bfloat16),
         in_specs=[
             pl.BlockSpec(memory_space=pltpu.SMEM),
-            pl.BlockSpec((sources, META_ROWS, 4 * tokens), lambda i: (0, tokens // META_ROWS, 0)),
+            pl.BlockSpec(meta.shape, lambda i: (0, 0, 0)),
             pl.BlockSpec((rows, columns), lambda i: (0, i)),
         ],
         out_specs=pl.BlockSpec((sources, tokens, columns), lambda i: (0, 0, i)),
@@ -399,7 +376,7 @@
             flops=4 * rows * tokens * width, bytes_accessed=4 * rows * width, transcendentals=0
         ),
         name="combine_rows",
-    )(mine, gathered, returned)
+    )(mine, meta, returned)
 
 
 def body(
@@ -441,24 +418,31 @@
     place = (pick_x * side + across) * CORES + (pick_core + core) % CORES
     place = jnp.stack([place.astype(jnp.float32), jnp.full(place.shape, near, jnp.float32)])
 
+    copies = jnp.broadcast_to(hidden[None], (side, tokens, width)).reshape(side * tokens, width)
+    copies, picks = lax.optimization_barrier((copies, picks))
+    data = exchange(copies, lines).reshape(side, tokens, width)
+    meta = lax.all_gather(
+        head_rows(picks, line, place, route_weights.T, experts),
+        ("ctx", "exp"),
+        axis_index_groups=lines,
+    )
     swap = [(i, i + 1 - 2 * (i % CORES)) for i in range(context_size)]
     own_weights = [gate_weights[0], up_weights[0], down_weights[0]]
     partner_weights = [lax.ppermute(weight, "ctx", swap) for weight in own_weights]
-
-    sent = head_rows(picks, line, place, route_weights.T, hidden, experts, side)
-    gathered = exchange(sent, lines).reshape(side, tokens + META_ROWS, width)
-    outgoing = pack_rows(mine, gathered, tokens, top, near, width // 4)
+    pieces, section = delta_front(
+        queries, key_vectors, values, write_strength, log_fading_factor, block_inverse
+    )
+    data, partner_weights = lax.optimization_barrier((data, partner_weights))
+    outgoing = pack_rows(mine, meta, data, top, near, width // 4)
+    outgoing, section = lax.optimization_barrier((outgoing, section))
     received = exchange(outgoing, planes)
-    pieces, incoming_state = delta_front(
-        queries, key_vectors, values, write_strength, log_fading_factor, block_inverse
-    )
-    received, incoming_state = lax.optimization_barrier((received, incoming_state))
+    sections = lax.all_gather(section, "ctx")
     produced = expert_rows(received, own_weights + partner_weights, chips * side, 4)
     returned = exchange(produced, planes)
-    partial = combine_rows(mine, gathered, returned, tokens, top, width // 4)
+    partial = combine_rows(mine, meta, returned, tokens, top, width // 4)
     partial = exchange(partial.reshape(side * tokens, width), lines).reshape(side, tokens, width)
     expert_output = jnp.sum(partial.astype(jnp.float32), axis=0).astype(jnp.bfloat16)
-    _, attended = run_blocks(pieces, incoming_state)
+    _, attended = run_blocks(pieces, entering_state(sections))
     mixer_output = gated_norm(attended.reshape(out_gate.shape), norm_gain, out_gate)
     return (mixer_output, expert_output)
 

time: 246 us -> 241 us (0.980)
  blocking collectives: 0 us -> 76.9 us
  starting transfers between devices: 81.4 us -> 31.6 us
  waiting for transfers between devices: 91.3 us -> 52.7 us
  between operations: 1.05 us -> 14.4 us
  Pallas kernels: 28.7 us -> 20.6 us
  matrix products: 25 us -> 30.3 us
    all_to_all x4 -> x3, waiting for transfers between devices: 78.7 us -> 7.71 us  [exchange(): lax.all_to_all(rows, ('ctx', 'exp'), split_axis=0, concat_axis=0, tiled=T...]
    all_to_all x0 -> x1, blocking collectives: none -> 48.7 us  [exchange(): lax.all_to_all(rows, ('ctx', 'exp'), split_axis=0, concat_axis=0, tiled=T...]
    all_gather x0 -> x1, waiting for transfers between devices: none -> 44.3 us  [body(): sections = lax.all_gather(section, 'ctx')]
    ppermute x7 -> x0, starting transfers between devices: 33.3 us -> none  [passed_along(): return lax.ppermute(block, axis, route)]
    all_gather x0 -> x1, blocking collectives: none -> 28.2 us  [body(): lax.all_gather(head_rows(picks, line, place, route_weights.T, experts), (...]
    all_to_all x4 -> x3, starting transfers between devices: 41.8 us -> 25.4 us  [exchange(): lax.all_to_all(rows, ('ctx', 'exp'), split_axis=0, concat_axis=0, tiled=T...]
    ppermute x7 -> x0, waiting for transfers between devices: 12.6 us -> none  [passed_along(): return lax.ppermute(block, axis, route)]
    pallas_call x2, Pallas kernels: 16.5 us -> 11.1 us  [the longest x1 10.5 us: expert_rows(): pl.pallas_call(expert_kernel, grid=(steps,), out_shape=pltpu.HBM(received...]
  transfers between devices with their start and end apart: 14 -> 7, of which waited for: 9 -> 2; matrix products, arithmetic and copies ran while one was open for 13% -> 16% of each run, Pallas kernels for 0% -> 0%
where the time goes in v4:
time: 241 us; the launch traced here: 239 us
  blocking collectives  76.9 us (32%)
  waiting for transfers between devices  52.7 us (22%)
  starting transfers between devices  31.6 us (13%)
  matrix products  30.3 us (13%)
  Pallas kernels  20.6 us (9%)
  between operations  14.4 us (6%)
  other arithmetic  6.1 us (3%)
  local copies, waits for them, and re-layouts  6.07 us (3%)
    all_to_all x1, blocking collectives, exchange(): lax.all_to_all(rows, ('ctx', 'exp'), split_axis=0, concat_axis=0, tiled=T...  48.7 us
    all_gather x1, waiting for transfers between devices, body(): sections = lax.all_gather(section, 'ctx')  44.3 us
    all_gather x1, blocking collectives, body(): lax.all_gather(head_rows(picks, line, place, route_weights.T, experts), (...  28.2 us
    all_to_all x3, starting transfers between devices, exchange(): lax.all_to_all(rows, ('ctx', 'exp'), split_axis=0, concat_axis=0, tiled=T...  25.4 us
    pallas_call x1, Pallas kernels, expert_rows(): pl.pallas_call(expert_kernel, grid=(steps,), out_shape=pltpu.HBM(received...  10.5 us
    all_to_all x3, waiting for transfers between devices, exchange(): lax.all_to_all(rows, ('ctx', 'exp'), split_axis=0, concat_axis=0, tiled=T...  7.71 us
    dot_general x4, matrix products, block_step(): jnp.einsum('sch,scv->shv', faded_keys, fresh_values, precision=TOP_PRECIS...  6.81 us
    dot_general x6, matrix products, entering_state(): jnp.dot(maps[section], state, precision=TOP_PRECISION) + addends[section]  6.53 us
  transfers between devices with their start and end apart: 7, of which 2 were waited for; matrix products, arithmetic and copies ran while one was open for 16% of the time, Pallas kernels for 0%

profile of v4, /device:TPU:1, one launch (start us, length us, event | category | flops | bytes accessed | tf_op | source)
XLA Modules:
  0.0 239.0 jit_solution(8297223153680018594)
XLA Ops:
  7.2 2.7 %broadcast_in_dim.22 = bf16[8,128,1024]{2,1,0:T(8,128)(2,1)} broadcast(bf16[128,1024]{1,0:T(8,128)(2,1)} %param.26), dimensions={1,2} | broadcast | bytes 2359296 | tf_op jit(solution)/shard_map/broadcast_in_dim | solution.py:421
  9.9 10.9 %all-to-all-start = ((bf16[8,128,1024]{2,1,0:T(8,128)(2,1)}), bf16[8,128,1024]{2,1,0:T(8,128)(2,1)S(1)}, u32[]{:S(2)}, u32[]{:S(2)}) async-start(bf16[8,128,1024]{2,1,0:T(8,128)(2,1)} %broadcast_in_dim.22), calls=%async_computation | async-start | bytes 4194304 | tf_op jit(solution)/shard_map/all_to_all | solution.py:141
  20.8 1.9 collective-permute-start
  22.7 2.4 %collective-permute-start.1 = (bf16[1024,512]{1,0:T(8,128)(2,1)}, bf16[1024,512]{1,0:T(8,128)(2,1)}, u32[]{:S(2)}, u32[]{:S(2)}) collective-permute-start(bf16[1024,512]{1,0:T(8,128)(2,1)} %bitcast.23.refs_1_), channel_id=1, source_target_pairs={{0,64},{64,0},{128,192},{192,128},{256,320},{320,256},{384,448},{4... | collective-permute-start | bytes 3145736 | tf_op jit(solution)/shard_map/ppermute | solution.py:431
  25.1 1.9 collective-permute-start.2
  27.6 0.7 reduce.16
  28.3 0.7 reduce.15
  30.7 0.7 convolution_bitcast_fusion.2
  31.7 0.7 fusion.27
  32.4 28.2 %all-gather = bf16[128,512]{1,0:T(8,128)(2,1)S(1)} all-gather(bf16[16,512]{1,0:T(8,128)(2,1)S(1)} %head_rows.1), channel_id=2, replica_groups={{0,8,16,24,32,40,48,56},{1,9,17,25,33,41,49,57},{2,10,18,26,34,42,50,58..., dimensions={0}, use_global_device_ids=true | all-gather | bytes 147456 | tf_op jit(solution)/shard_map/all_gather | solution.py:424
  60.6 1.9 while.24
  62.5 0.7 pad_maximum_fusion
  63.2 4.4 %pack_rows.1 = bf16[1536,1024]{1,0:T(8,128)(2,1)} custom-call(s32[1]{0:T(128)} %bitcast.15.mine_ref, bf16[8,16,512]{2,1,0:T(8,128)(2,1)S(1)} %bitcast.207, bf16[8,128,1024]{2,1,0:T(8,128)(2,1)S(1)} %all-to-all-done.data_ref), custom_call_target="tpu_custom_call" | custom-call | flops 402653184 | bytes 6291456 | tf_op jit(solution)/shard_map/pack_rows/pallas_call | solution.py:231
  67.6 48.7 %all_to_all.37 = bf16[32,48,1024]{2,1,0:T(8,128)(2,1)S(1)} all-to-all(bf16[32,48,1024]{2,1,0:T(8,128)(2,1)} %bitcast.211), channel_id=1, replica_groups={{0,1,2,3,4,5,6,7,128,129,130,131,132,133,134,135,256,257,258,259,260,26..., dimensions={0} | all-to-all | bytes 6291456 | tf_op jit(solution)/shard_map/all_to_all | solution.py:141
  116.2 10.5 %expert_rows.1 = bf16[1536,1024]{1,0:T(8,128)(2,1)} custom-call(bf16[1536,1024]{1,0:T(8,128)(2,1)S(1)} %bitcast.206, bf16[1024,512]{1,0:T(8,128)(2,1)} %bitcast.22.refs_0_, bf16[1024,512]{1,0:T(8,128)(2,1)} %bitcast.23.refs_1_, bf16[512,1024]{1,0:T(8,128)(2,1)} %bitcast.24.refs_2_, bf16[1024,512]{1,0:T(8,128)(2,1)} %collective-permute-done.refs_3_, ...), custom_call_target="tpu_custom_call" | custom-call | flops 4831838208 | bytes 12582912 | tf_op jit(solution)/shard_map/expert_rows/pallas_call | solution.py:293
  126.8 6.3 %all-to-all-start.2 = ((bf16[32,48,1024]{2,1,0:T(8,128)(2,1)}), bf16[32,48,1024]{2,1,0:T(8,128)(2,1)S(1)}, u32[]{:S(2)}, u32[]{:S(2)}) async-start(bf16[32,48,1024]{2,1,0:T(8,128)(2,1)} %bitcast.217), calls=%async_computation.2 | async-start | bytes 6291456 | tf_op jit(solution)/shard_map/all_to_all | solution.py:141
  133.1 0.7 all-gather.4.cloned.1.call-update
  133.8 1.9 fusion.28
  135.7 1.7 broadcast_multiply_fusion
  137.4 44.3 %all-gather.4.cloned.1.call-done = f32[16,128,128]{2,1,0:T(8,128)} async-done(((f32[2,128,128]{2,1,0:T(8,128)}), f32[16,128,128]{2,1,0:T(8,128)}) %all-gather.4.cloned.1.call-update) | async-done | bytes 1048592 | tf_op jit(solution)/shard_map/all_gather | solution.py:439
  181.8 1.1 fusion.36
  182.9 1.1 fusion.35
  184.0 1.1 fusion.34
  185.1 1.1 fusion.33
  186.2 1.1 fusion.32
  187.2 1.1 fusion.31
  188.3 5.1 %combine_rows.1 = bf16[8,128,1024]{2,1,0:T(8,128)(2,1)} custom-call(s32[1]{0:T(128)} %bitcast.15.mine_ref, bf16[8,16,512]{2,1,0:T(8,128)(2,1)S(1)} %bitcast.208, bf16[1536,1024]{1,0:T(8,128)(2,1)S(1)} %bitcast.205), custom_call_target="tpu_custom_call" | custom-call | flops 805306368 | bytes 6291456 | tf_op jit(solution)/shard_map/combine_rows/pallas_call | solution.py:363
  193.5 8.2 %all-to-all-start.3 = ((bf16[8,128,1024]{2,1,0:T(8,128)(2,1)}), bf16[8,128,1024]{2,1,0:T(8,128)(2,1)S(1)}, u32[]{:S(2)}, u32[]{:S(2)}) async-start(bf16[8,128,1024]{2,1,0:T(8,128)(2,1)} %combine_rows.1), calls=%async_computation.3 | async-start | bytes 4194304 | tf_op jit(solution)/shard_map/all_to_all | solution.py:141
  201.7 20.7 %while.25 = (s32[]{:T(128)}, f32[1,128,128]{2,1,0:T(8,128)S(1)}, f32[4,1,64,128]{3,2,1,0:T(8,128)S(1)}, f32[4,1,1]{0,2,1:T(1,128)S(1)}, f32[4,1,64,128]{3,2,1,0:...) while((s32[]{:T(128)}, f32[1,128,128]{2,1,0:T(8,128)S(1)}, ...), condition=%wide.region_4.5_spmd, body=%wide.region_3.4_spmd.sunk | while | flops 44089344 | bytes 625281 | solution.py:72
  201.7 0.9 fusion.107
  202.7 1.0 convolution_subtract_fusion.3
  204.3 1.7 fusion.106
  206.0 0.9 fusion.108
  206.9 0.9 fusion.107
  207.9 1.0 convolution_subtract_fusion.3
  209.4 1.7 fusion.106
  211.1 0.9 fusion.108
  212.1 0.9 fusion.107
  213.0 1.0 convolution_subtract_fusion.3
  214.6 1.7 fusion.106
  216.3 0.9 fusion.108
  217.2 0.9 fusion.107
  218.2 1.0 convolution_subtract_fusion.3
  219.8 1.7 fusion.106
  221.5 0.9 fusion.108
  222.6 0.8 multiply_multiply_fusion
  223.4 7.7 %all-to-all-done.3 = bf16[8,128,1024]{2,1,0:T(8,128)(2,1)S(1)} async-done(((bf16[8,128,1024]{2,1,0:T(8,128)(2,1)}), bf16[8,128,1024]{2,1,0:T(8,128)(2,1)S(1)}, u32[]{:S(2)}, u32[]{:S(2)}) %all-to-all-start.3) | async-done | bytes 2097184 | tf_op jit(solution)/shard_map/all_to_all | solution.py:141
  231.1 1.1 reduce_sum.22
  (69 shorter events, 6.9 us)
Async XLA Ops:
  7.2 23.1 %copy-start = (f32[1,4,64,64]{3,2,1,0:T(8,128)S(1)}, f32[1,4,64,64]{3,2,1,0:T(8,128)}, u32[]{:S(2)}) copy-start(f32[1,4,64,64]{3,2,1,0:T(8,128)} %param.24) | copy-start | bytes 196612
  7.2 21.9 %copy-start.1 = (s32[128,10]{0,1:T(8,128)S(1)}, s32[128,10]{0,1:T(8,128)}, u32[]{:S(2)}) copy-start(s32[128,10]{0,1:T(8,128)} %param.27) | copy-start | bytes 15364
  7.2 20.4 %copy-start.9 = (f32[1,256]{1,0:T(1,128)S(1)}, f32[1,256]{1,0:T(1,128)}, u32[]{:S(2)}) copy-start(f32[1,256]{1,0:T(1,128)} %param.23) | copy-start | bytes 3076
  7.2 21.1 %copy-start.10 = (f32[1,256]{1,0:T(1,128)S(1)}, f32[1,256]{1,0:T(1,128)}, u32[]{:S(2)}) copy-start(f32[1,256]{1,0:T(1,128)} %param.22) | copy-start | bytes 3076
  7.2 22.1 %copy-start.2 = (f32[128,10]{0,1:T(8,128)S(1)}, f32[128,10]{0,1:T(8,128)}, u32[]{:S(2)}) copy-start(f32[128,10]{0,1:T(8,128)} %param.28) | copy-start | bytes 15364
  7.2 23.1 %copy-start.7 = (f32[1,256,128]{2,1,0:T(8,128)S(1)}, f32[1,256,128]{2,1,0:T(8,128)}, u32[]{:S(2)}) copy-start(f32[1,256,128]{2,1,0:T(8,128)} %param.20) | copy-start | bytes 393220
  7.2 23.4 %copy-start.3 = (f32[1,256,128]{2,1,0:T(8,128)S(1)}, f32[1,256,128]{2,1,0:T(8,128)}, u32[]{:S(2)}) copy-start(f32[1,256,128]{2,1,0:T(8,128)} %param.19) | copy-start | bytes 393220
  9.9 53.3 %all-to-all-start = ((bf16[8,128,1024]{2,1,0:T(8,128)(2,1)}), bf16[8,128,1024]{2,1,0:T(8,128)(2,1)S(1)}, u32[]{:S(2)}, u32[]{:S(2)}) async-start(bf16[8,128,1024]{2,1,0:T(8,128)(2,1)} %broadcast_in_dim.22), calls=%async_computation | async-start | bytes 4194304 | tf_op jit(solution)/shard_map/all_to_all | solution.py:141
  20.8 42.4 %collective-permute-start = (bf16[1024,512]{1,0:T(8,128)(2,1)}, bf16[1024,512]{1,0:T(8,128)(2,1)}, u32[]{:S(2)}, u32[]{:S(2)}) collective-permute-start(bf16[1024,512]{1,0:T(8,128)(2,1)} %bitcast.22.refs_0_), channel_id=1, source_target_pairs={{0,64},{64,0},{128,192},{192,128},{256,320},{320,256},{384,448},{4... | collective-permute-start | bytes 3145736 | tf_op jit(solution)/shard_map/ppermute | solution.py:431
  22.7 40.5 %collective-permute-start.1 = (bf16[1024,512]{1,0:T(8,128)(2,1)}, bf16[1024,512]{1,0:T(8,128)(2,1)}, u32[]{:S(2)}, u32[]{:S(2)}) collective-permute-start(bf16[1024,512]{1,0:T(8,128)(2,1)} %bitcast.23.refs_1_), channel_id=1, source_target_pairs={{0,64},{64,0},{128,192},{192,128},{256,320},{320,256},{384,448},{4... | collective-permute-start | bytes 3145736 | tf_op jit(solution)/shard_map/ppermute | solution.py:431
  25.1 38.1 %collective-permute-start.2 = (bf16[512,1024]{1,0:T(8,128)(2,1)}, bf16[512,1024]{1,0:T(8,128)(2,1)}, u32[]{:S(2)}, u32[]{:S(2)}) collective-permute-start(bf16[512,1024]{1,0:T(8,128)(2,1)} %bitcast.24.refs_2_), channel_id=1, source_target_pairs={{0,64},{64,0},{128,192},{192,128},{256,320},{320,256},{384,448},{4... | collective-permute-start | bytes 3145736 | tf_op jit(solution)/shard_map/ppermute | solution.py:431
  30.6 1.0 copy-start.4
  31.7 35.9 %copy-start.5 = (f32[4,128,64]{1,2,0:T(8,128)}, f32[4,128,64]{1,2,0:T(8,128)S(1)}, u32[]{:S(2)}) copy-start(f32[4,128,64]{1,2,0:T(8,128)S(1)} %fusion.39) | copy-start | bytes 393220
  126.8 61.6 %all-to-all-start.2 = ((bf16[32,48,1024]{2,1,0:T(8,128)(2,1)}), bf16[32,48,1024]{2,1,0:T(8,128)(2,1)S(1)}, u32[]{:S(2)}, u32[]{:S(2)}) async-start(bf16[32,48,1024]{2,1,0:T(8,128)(2,1)} %bitcast.217), calls=%async_computation.2 | async-start | bytes 6291456 | tf_op jit(solution)/shard_map/all_to_all | solution.py:141
  133.0 48.7 %all-gather.4.cloned.1.call-start = ((), (), s32[]{:S(2)}) async-start(), calls=%async_computation.4 | async-start | bytes 1179648 | tf_op jit(solution)/shard_map/all_gather | solution.py:439
  193.5 8.2 %copy-start.6 = (f32[4,1,64,128]{3,2,1,0:T(8,128)S(1)}, f32[4,1,64,128]{3,2,1,0:T(8,128)}, u32[]{:S(2)}) copy-start(f32[4,1,64,128]{3,2,1,0:T(8,128)} %custom-call) | copy-start | bytes 393220
  193.5 29.1 %copy-start.8 = (f32[1,256,128]{2,1,0:T(8,128)S(1)}, f32[1,256,128]{2,1,0:T(8,128)}, u32[]{:S(2)}) copy-start(f32[1,256,128]{2,1,0:T(8,128)} %param.21) | copy-start | bytes 393220
  193.5 29.1 %copy-start.11 = (f32[128]{0:T(128)S(1)}, f32[128]{0:T(128)}, u32[]{:S(2)}) copy-start(f32[128]{0:T(128)} %param.25) | copy-start | bytes 1540
  193.5 37.6 %all-to-all-start.3 = ((bf16[8,128,1024]{2,1,0:T(8,128)(2,1)}), bf16[8,128,1024]{2,1,0:T(8,128)(2,1)S(1)}, u32[]{:S(2)}, u32[]{:S(2)}) async-start(bf16[8,128,1024]{2,1,0:T(8,128)(2,1)} %combine_rows.1), calls=%async_computation.3 | async-start | bytes 4194304 | tf_op jit(solution)/shard_map/all_to_all | solution.py:141
Sparse Core Ops, SparseCore 0:
  136.6 45.1 all-gather.3

commit v5 on v4

--- a/solution.py
+++ b/solution.py
@@ -111,14 +111,21 @@
     return pieces, jnp.concatenate([section_mapping, section_addend], axis=0)
 
 
+def earlier_sections(section):
+    size = lax.axis_size("ctx")
+    return tuple(
+        lax.ppermute(section, "ctx", [(i, i + back) for i in range(size - back)])
+        for back in range(size - 1, 0, -1)
+    )
+
+
 def entering_state(sections):
-    maps, addends = sections[:, 0], sections[:, 1]
-    mine = lax.axis_index("ctx")
-    state = addends[0]
-    for section in range(1, sections.shape[0] - 1):
-        later = jnp.dot(maps[section], state, precision=TOP_PRECISION) + addends[section]
-        state = jnp.where(section < mine, later, state)
-    return jnp.where(mine == 0, 0.0, state)[None]
+    state = sections[0][1:2]
+    for section in sections[1:]:
+        state = (
+            jnp.einsum("qfz,qze->qfe", section[0:1], state, precision=TOP_PRECISION) + section[1:2]
+        )
+    return state
 
 
 def device_of(x, core, y, z, side):
@@ -143,8 +150,17 @@
     )
 
 
-def head_kernel(experts, picks_ref, line_ref, place_ref, weights_ref, out_ref, block_ref):
+def head_kernel(
+    experts, copies, picks_ref, line_ref, place_ref, weights_ref, hidden_ref, out_ref, block_ref, meta_ref, sent
+):
     top, tokens = picks_ref.shape
+    each = out_ref.shape[0] // copies
+    moves = [
+        pltpu.make_async_copy(hidden_ref, out_ref.at[pl.ds(copy * each, tokens), :], sent.at[copy])
+        for copy in range(copies)
+    ]
+    for move in moves:
+        move.start()
     picks = picks_ref[...]
     row = lax.broadcasted_iota(jnp.int32, (experts, tokens), 0)
     named = jnp.zeros((experts, tokens), jnp.bool_)
@@ -172,21 +188,38 @@
         (line_ref[...], place_ref[0] + slot * place_ref[1], high, weights - high)
     ):
         block_ref[0:top, column * tokens : (column + 1) * tokens] = item
-    out_ref[...] = block_ref[...].astype(jnp.bfloat16)
-
-
-def head_rows(picks, line, place, weights, experts):
-    shape = (META_ROWS, 4 * picks.shape[1])
+    meta_ref[...] = block_ref[...].astype(jnp.bfloat16)
+    more = [
+        pltpu.make_async_copy(
+            meta_ref, out_ref.at[pl.ds(copy * each + tokens, META_ROWS), :], sent.at[copies + copy]
+        )
+        for copy in range(copies)
+    ]
+    for move in more:
+        move.start()
+    for move in moves + more:
+        move.wait()
+
+
+def head_rows(picks, line, place, weights, hidden, experts, copies):
+    tokens, width = hidden.shape
+    here = pl.BlockSpec(memory_space=pltpu.VMEM)
     return pl.pallas_call(
-        functools.partial(head_kernel, experts),
-        out_shape=jax.ShapeDtypeStruct(shape, jnp.bfloat16),
-        scratch_shapes=[pltpu.VMEM(shape, jnp.float32)],
+        functools.partial(head_kernel, experts, copies),
+        out_shape=pltpu.HBM((copies * (tokens + META_ROWS), width), jnp.bfloat16),
+        in_specs=[here] * 5,
+        out_specs=pl.BlockSpec(memory_space=pl.ANY),
+        scratch_shapes=[
+            pltpu.VMEM((META_ROWS, width), jnp.float32),
+            pltpu.VMEM((META_ROWS, width), jnp.bfloat16),
+            pltpu.SemaphoreType.DMA((2 * copies,)),
+        ],
         compiler_params=pltpu.CompilerParams(vmem_limit_bytes=16 * 1024 * 1024),
         cost_estimate=pl.CostEstimate(
-            flops=60 * experts * picks.shape[1], bytes_accessed=65536, transcendentals=0
+            flops=60 * experts * tokens, bytes_accessed=2 * copies * tokens * width, transcendentals=0
         ),
         name="head_rows",
-    )(picks, line, place, weights)
+    )(picks, line, place, weights, hidden)
 
 
 def table_at(meta, mine, count, value):
@@ -225,8 +258,8 @@
         out_ref[:, part * lanes : (part + 1) * lanes] = spread_ref[part].astype(jnp.bfloat16)
 
 
-def pack_rows(mine, meta, data, top, near, columns):
-    sources, tokens, width = data.shape
+def pack_rows(mine, gathered, tokens, top, near, columns):
+    sources, _, width = gathered.shape
     rows = near * CAPACITY * sources
     return pl.pallas_call(
         functools.partial(pack_kernel, top),
@@ -234,7 +267,7 @@
         out_shape=pltpu.HBM((rows, width), jnp.bfloat16),
         in_specs=[
             pl.BlockSpec(memory_space=pltpu.SMEM),
-            pl.BlockSpec(meta.shape, lambda i: (0, 0, 0)),
+            pl.BlockSpec((sources, META_ROWS, 4 * tokens), lambda i: (0, tokens // META_ROWS, 0)),
             pl.BlockSpec((sources, tokens, columns), lambda i: (0, 0, i)),
         ],
         out_specs=pl.BlockSpec((rows, columns), lambda i: (0, i)),
@@ -247,7 +280,7 @@
             flops=2 * rows * tokens * width, bytes_accessed=4 * rows * width, transcendentals=0
         ),
         name="pack_rows",
-    )(mine, meta, data)
+    )(mine, gathered, gathered)
 
 
 def expert_kernel(received_ref, *refs):
@@ -311,9 +344,9 @@
     )(received, *weights)
 
 
-def combine_kernel(top, mine_ref, meta_ref, returned_ref, out_ref, high_ref, low_ref, spread_ref):
+def combine_kernel(top, mine_ref, meta_ref, returned_ref, out_ref, table_ref, spread_ref):
     sources, tokens, _ = out_ref.shape
-    count = high_ref.shape[1]
+    count = table_ref.shape[1]
     near = count // CAPACITY
     lanes = spread_ref.shape[2]
 
@@ -322,9 +355,11 @@
         mine = mine_ref[0].astype(jnp.float32)
         for source in range(sources):
             meta = meta_ref[source].astype(jnp.float32)[0:top]
-            for column, table in ((2, high_ref), (3, low_ref)):
-                value = meta[:, column * tokens : (column + 1) * tokens]
-                table[source] = table_at(meta, mine, count, value).astype(jnp.bfloat16)
+            for half in range(2):
+                value = meta[:, (2 + half) * tokens : (3 + half) * tokens]
+                table_ref[source, :, half * tokens : (half + 1) * tokens] = table_at(
+                    meta, mine, count, value
+                ).astype(jnp.bfloat16)
 
     for part in range(spread_ref.shape[0]):
         spread_ref[part] = returned_ref[:, part * lanes : (part + 1) * lanes].astype(jnp.float32)
@@ -346,37 +381,36 @@
             ],
             axis=0,
         ).astype(jnp.bfloat16)
-        total = sum(
-            lax.dot_general(
-                table[source], rows, (((0,), (0,)), ((), ())), preferred_element_type=jnp.float32
-            )
-            for table in (high_ref, low_ref)
+        total = lax.dot_general(
+            table_ref[source], rows, (((0,), (0,)), ((), ())), preferred_element_type=jnp.float32
         )
-        out_ref[source] = total.astype(jnp.bfloat16)
-
-
-def combine_rows(mine, meta, returned, tokens, top, columns):
-    sources = meta.shape[0]
+        out_ref[source] = (total[:tokens] + total[tokens:]).astype(jnp.bfloat16)
+
+
+def combine_rows(mine, gathered, returned, tokens, top, columns):
+    sources = gathered.shape[0]
     rows, width = returned.shape
     near = rows // CAPACITY // sources
-    table = pltpu.VMEM((sources, near * CAPACITY, tokens), jnp.bfloat16)
     return pl.pallas_call(
         functools.partial(combine_kernel, top),
         grid=(width // columns,),
         out_shape=pltpu.HBM((sources, tokens, width), jnp.bfloat16),
         in_specs=[
             pl.BlockSpec(memory_space=pltpu.SMEM),
-            pl.BlockSpec(meta.shape, lambda i: (0, 0, 0)),
+            pl.BlockSpec((sources, META_ROWS, 4 * tokens), lambda i: (0, tokens // META_ROWS, 0)),
             pl.BlockSpec((rows, columns), lambda i: (0, i)),
         ],
         out_specs=pl.BlockSpec((sources, tokens, columns), lambda i: (0, 0, i)),
-        scratch_shapes=[table, table, pltpu.VMEM((columns // LANES, rows, LANES), jnp.float32)],
+        scratch_shapes=[
+            pltpu.VMEM((sources, near * CAPACITY, 2 * tokens), jnp.bfloat16),
+            pltpu.VMEM((columns // LANES, rows, LANES), jnp.float32),
+        ],
         compiler_params=pltpu.CompilerParams(vmem_limit_bytes=VMEM_BYTES),
         cost_estimate=pl.CostEstimate(
             flops=4 * rows * tokens * width, bytes_accessed=4 * rows * width, transcendentals=0
         ),
         name="combine_rows",
-    )(mine, meta, returned)
+    )(mine, gathered, returned)
 
 
 def body(
@@ -418,28 +452,23 @@
     place = (pick_x * side + across) * CORES + (pick_core + core) % CORES
     place = jnp.stack([place.astype(jnp.float32), jnp.full(place.shape, near, jnp.float32)])
 
-    copies = jnp.broadcast_to(hidden[None], (side, tokens, width)).reshape(side * tokens, width)
-    copies, picks = lax.optimization_barrier((copies, picks))
-    data = exchange(copies, lines).reshape(side, tokens, width)
-    meta = lax.all_gather(
-        head_rows(picks, line, place, route_weights.T, experts),
-        ("ctx", "exp"),
-        axis_index_groups=lines,
-    )
+    sent = head_rows(picks, line, place, route_weights.T, hidden, experts, side)
+    gathered = exchange(sent, lines).reshape(side, tokens + META_ROWS, width)
     swap = [(i, i + 1 - 2 * (i % CORES)) for i in range(context_size)]
     own_weights = [gate_weights[0], up_weights[0], down_weights[0]]
     partner_weights = [lax.ppermute(weight, "ctx", swap) for weight in own_weights]
     pieces, section = delta_front(
         queries, key_vectors, values, write_strength, log_fading_factor, block_inverse
     )
-    data, partner_weights = lax.optimization_barrier((data, partner_weights))
-    outgoing = pack_rows(mine, meta, data, top, near, width // 4)
-    outgoing, section = lax.optimization_barrier((outgoing, section))
+    gathered, partner_weights, section = lax.optimization_barrier(
+        (gathered, partner_weights, section)
+    )
+    outgoing = pack_rows(mine, gathered, tokens, top, near, width // 4)
     received = exchange(outgoing, planes)
-    sections = lax.all_gather(section, "ctx")
-    produced = expert_rows(received, own_weights + partner_weights, chips * side, 4)
+    received, sections = lax.optimization_barrier((received, earlier_sections(section)))
+    produced = expert_rows(received, own_weights + partner_weights, chips * side, 2)
     returned = exchange(produced, planes)
-    partial = combine_rows(mine, meta, returned, tokens, top, width // 4)
+    partial = combine_rows(mine, gathered, returned, tokens, top, width // 4)
     partial = exchange(partial.reshape(side * tokens, width), lines).reshape(side, tokens, width)
     expert_output = jnp.sum(partial.astype(jnp.float32), axis=0).astype(jnp.bfloat16)
     _, attended = run_blocks(pieces, entering_state(sections))

time: 241 us -> 237 us (0.983)
  the two profiles are of different devices: /device:TPU:1 before, /device:TPU:64 now
where the time goes in v5:
time: 237 us; the launch traced here: 235 us
  waiting for transfers between devices  84.6 us (36%)
  starting transfers between devices  67.3 us (28%)
  matrix products  36.4 us (15%)
  Pallas kernels  21.8 us (9%)
  local copies, waits for them, and re-layouts  16.8 us (7%)
  other arithmetic  6.71 us (3%)
    all_to_all x4, waiting for transfers between devices, exchange(): lax.all_to_all(rows, ('ctx', 'exp'), split_axis=0, concat_axis=0, tiled=T...  52.6 us
    all_to_all x4, starting transfers between devices, exchange(): lax.all_to_all(rows, ('ctx', 'exp'), split_axis=0, concat_axis=0, tiled=T...  42.7 us
    ppermute x7, waiting for transfers between devices, earlier_sections(): lax.ppermute(section, 'ctx', [(i, i + back) for i in range(size - back)])  31.9 us
    ppermute x7, starting transfers between devices, earlier_sections(): lax.ppermute(section, 'ctx', [(i, i + back) for i in range(size - back)])  16.3 us
    pallas_call x1, Pallas kernels, expert_rows(): pl.pallas_call(expert_kernel, grid=(steps,), out_shape=pltpu.HBM(received...  9.59 us
    ppermute x3, starting transfers between devices, body(): lax.ppermute(weight, 'ctx', swap)  8.37 us
    dot_general x4, matrix products, compose(): jnp.einsum('qfz,qze->qfe', segment_mapping, current_addend, precision=TOP...  6.85 us
    while x8, local copies, waits for them, and re-layouts  6.72 us
  transfers between devices with their start and end apart: 14, of which 5 were waited for; matrix products, arithmetic and copies ran while one was open for 22% of the time, Pallas kernels for 0%

profile of v5, /device:TPU:64, one launch (start us, length us, event | category | flops | bytes accessed | tf_op | source)
XLA Modules:
  0.0 234.7 jit_solution(6374620245365830910)
XLA Ops:
  3.8 1.6 head_rows.1
  5.4 7.1 %all-to-all-start = ((bf16[8,144,1024]{2,1,0:T(8,128)(2,1)}), bf16[8,144,1024]{2,1,0:T(8,128)(2,1)S(1)}, u32[]{:S(2)}, u32[]{:S(2)}) async-start(bf16[8,144,1024]{2,1,0:T(8,128)(2,1)} %bitcast.238), calls=%async_computation | async-start | bytes 4718592 | tf_op jit(solution)/shard_map/all_to_all | solution.py:148
  12.5 4.0 %collective-permute-start = (bf16[1024,512]{1,0:T(8,128)(2,1)S(1)}, bf16[1024,512]{1,0:T(8,128)(2,1)}, u32[]{:S(2)}, u32[]{:S(2)}) collective-permute-start(bf16[1024,512]{1,0:T(8,128)(2,1)S(1)} %bitcast.231), channel_id=1, source_target_pairs={{0,64},{64,0},{128,192},{192,128},{256,320},{320,256},{384,448},{4... | collective-permute-start | bytes 3145736 | tf_op jit(solution)/shard_map/ppermute | solution.py:459
  16.5 1.9 collective-permute-start.1
  18.5 2.4 %collective-permute-start.2 = (bf16[512,1024]{1,0:T(8,128)(2,1)}, bf16[512,1024]{1,0:T(8,128)(2,1)}, u32[]{:S(2)}, u32[]{:S(2)}) collective-permute-start(bf16[512,1024]{1,0:T(8,128)(2,1)} %bitcast.235), channel_id=1, source_target_pairs={{0,64},{64,0},{128,192},{192,128},{256,320},{320,256},{384,448},{4... | collective-permute-start | bytes 3145736 | tf_op jit(solution)/shard_map/ppermute | solution.py:459
  23.4 1.3 fusion.29
  25.4 2.3 convolution_bitcast_fusion.2
  27.6 1.2 fusion.31
  29.5 2.3 fusion.27
  33.1 20.2 %while.24 = (s32[]{:T(128)}, f32[1,128,128]{2,1,0:T(8,128)}, f32[1,128,128]{2,1,0:T(8,128)}, f32[4,1,128,128]{3,2,1,0:T(8,128)}, f32[4,1,128,128]{3,2,1,0:T(8,128)}, /*index=5*/s32[]{:T(128)}) while((s32[]{:T(128)}, f32[1,128,128]{2,1,0:T(8,128)}, f32[1,128,128]{2,1,0:T(8,128)}, f32[4,1,128,128]{3,2,1,0:T(8,128)}, ...), condition=%wide.region_2.3_spmd, body=%wide.region_1.2_spmd.sunk | while | flops 50348032 | bytes 722001 | solution.py:106
  33.9 1.7 convolution_bitcast_fusion.10
  36.4 1.7 fusion.131
  39.0 1.7 convolution_bitcast_fusion.10
  41.5 1.7 fusion.131
  44.0 1.7 convolution_bitcast_fusion.10
  46.5 1.7 fusion.131
  49.1 1.7 convolution_bitcast_fusion.10
  51.6 1.7 fusion.131
  53.3 1.5 pad_maximum_fusion
  54.8 4.4 %pack_rows.1 = bf16[1536,1024]{1,0:T(8,128)(2,1)} custom-call(s32[1]{0:T(128)} %bitcast.15.mine_ref, bf16[8,144,1024]{2,1,0:T(8,128)(2,1)S(1)} %all-to-all-done.meta_ref.data_ref, bf16[8,144,1024]{2,1,0:T(8,128)(2,1)S(1)} %all-to-all-done.meta_ref.data_ref), custom_call_target="tpu_custom_call" | custom-call | flops 402653184 | bytes 6291456 | tf_op jit(solution)/shard_map/pack_rows/pallas_call | solution.py:264
  59.2 10.5 %all-to-all-start.1 = ((bf16[32,48,1024]{2,1,0:T(8,128)(2,1)}), bf16[32,48,1024]{2,1,0:T(8,128)(2,1)}, u32[]{:S(2)}, u32[]{:S(2)}) async-start(bf16[32,48,1024]{2,1,0:T(8,128)(2,1)} %bitcast.237), calls=%async_computation.1 | async-start | bytes 6291456 | tf_op jit(solution)/shard_map/all_to_all | solution.py:148
  69.7 4.2 %collective-permute-start.3 = (f32[2,128,128]{2,1,0:T(8,128)}, f32[2,128,128]{2,1,0:T(8,128)}, u32[]{:S(2)}, u32[]{:S(2)}) collective-permute-start(f32[2,128,128]{2,1,0:T(8,128)} %pad_maximum_fusion), channel_id=1, source_target_pairs={{0,448},{1,449},{2,450},{3,451},{4,452},{5,453},{6,454},{7,455},{8... | collective-permute-start | bytes 393224 | tf_op jit(solution)/shard_map/ppermute | solution.py:117
  73.9 2.4 %collective-permute-start.4 = (f32[2,128,128]{2,1,0:T(8,128)}, f32[2,128,128]{2,1,0:T(8,128)}, u32[]{:S(2)}, u32[]{:S(2)}) collective-permute-start(f32[2,128,128]{2,1,0:T(8,128)} %pad_maximum_fusion), channel_id=1, source_target_pairs={{0,384},{64,448},{1,385},{65,449},{2,386},{66,450},{3,387},{67,451... | collective-permute-start | bytes 393224 | tf_op jit(solution)/shard_map/ppermute | solution.py:117
  76.3 1.9 collective-permute-start.5
  78.3 1.9 collective-permute-start.6
  80.2 1.9 collective-permute-start.7
  82.1 28.3 %collective-permute-done.3 = f32[2,128,128]{2,1,0:T(8,128)} collective-permute-done((f32[2,128,128]{2,1,0:T(8,128)}, f32[2,128,128]{2,1,0:T(8,128)}, u32[]{:S(2)}, u32[]{:S(2)}) %collective-permute-start.3) | collective-permute-done | bytes 131104 | tf_op jit(solution)/shard_map/ppermute | solution.py:117
  110.5 1.9 collective-permute-start.8
  112.4 2.9 %collective-permute-done.4 = f32[2,128,128]{2,1,0:T(8,128)} collective-permute-done((f32[2,128,128]{2,1,0:T(8,128)}, f32[2,128,128]{2,1,0:T(8,128)}, u32[]{:S(2)}, u32[]{:S(2)}) %collective-permute-start.4) | collective-permute-done | bytes 131104 | tf_op jit(solution)/shard_map/ppermute | solution.py:117
  115.3 1.9 collective-permute-start.9
  117.9 1.2 copy-done.5
  119.2 1.2 copy-done.6
  120.4 9.6 %expert_rows.1 = bf16[1536,1024]{1,0:T(8,128)(2,1)} custom-call(bf16[1536,1024]{1,0:T(8,128)(2,1)} %bitcast.32.received_ref, bf16[1024,512]{1,0:T(8,128)(2,1)S(1)} %bitcast.232, bf16[1024,512]{1,0:T(8,128)(2,1)S(1)} %bitcast.234, bf16[512,1024]{1,0:T(8,128)(2,1)S(1)} %bitcast.236, bf16[1024,512]{1,0:T(8,128)(2,1)} %collective-permute-done.refs_3_, ...), custom_call_target="tpu_custom_call" | custom-call | flops 4831838208 | bytes 12582912 | tf_op jit(solution)/shard_map/expert_rows/pallas_call | solution.py:326
  130.0 15.8 %all-to-all-start.2 = ((bf16[32,48,1024]{2,1,0:T(8,128)(2,1)}), bf16[32,48,1024]{2,1,0:T(8,128)(2,1)}, u32[]{:S(2)}, u32[]{:S(2)}) async-start(bf16[32,48,1024]{2,1,0:T(8,128)(2,1)} %bitcast.244), calls=%async_computation.2 | async-start | bytes 6291456 | tf_op jit(solution)/shard_map/all_to_all | solution.py:148
  146.4 1.1 fusion.43
  147.5 1.1 fusion.48
  148.6 1.1 fusion.54
  149.7 1.1 fusion.60
  150.8 1.1 fusion.66
  151.8 1.1 fusion.72
  152.9 34.9 %all-to-all-done.2 = bf16[32,48,1024]{2,1,0:T(8,128)(2,1)} async-done(((bf16[32,48,1024]{2,1,0:T(8,128)(2,1)}), bf16[32,48,1024]{2,1,0:T(8,128)(2,1)}, u32[]{:S(2)}, u32[]{:S(2)}) %all-to-all-start.2) | async-done | bytes 3145760 | tf_op jit(solution)/shard_map/all_to_all | solution.py:148
  187.8 6.3 %combine_rows.1 = bf16[8,128,1024]{2,1,0:T(8,128)(2,1)} custom-call(s32[1]{0:T(128)} %bitcast.15.mine_ref, bf16[8,144,1024]{2,1,0:T(8,128)(2,1)S(1)} %all-to-all-done.meta_ref.data_ref, bf16[1536,1024]{1,0:T(8,128)(2,1)} %bitcast.64.returned_ref), custom_call_target="tpu_custom_call" | custom-call | flops 805306368 | bytes 6291456 | tf_op jit(solution)/shard_map/combine_rows/pallas_call | solution.py:394
  194.1 9.2 %all-to-all-start.3 = ((bf16[8,128,1024]{2,1,0:T(8,128)(2,1)}), bf16[8,128,1024]{2,1,0:T(8,128)(2,1)S(1)}, u32[]{:S(2)}, u32[]{:S(2)}) async-start(bf16[8,128,1024]{2,1,0:T(8,128)(2,1)} %combine_rows.1), calls=%async_computation.3 | async-start | bytes 4194304 | tf_op jit(solution)/shard_map/all_to_all | solution.py:148
  203.4 11.6 %while.25 = (s32[]{:T(128)}, f32[1,128,128]{2,1,0:T(8,128)S(1)}, f32[4,1,64,128]{3,2,1,0:T(8,128)S(1)}, f32[4,1,1]{0,2,1:T(1,128)S(1)}, f32[4,1,64,128]{3,2,1,0:...) while((s32[]{:T(128)}, f32[1,128,128]{2,1,0:T(8,128)S(1)}, ...), condition=%wide.region_4.5_spmd, body=%wide.region_3.4_spmd.sunk | while | flops 44089344 | bytes 624773 | solution.py:72
  203.6 1.0 convolution_subtract_fusion.3
  206.4 1.0 convolution_subtract_fusion.3
  215.9 17.7 %all-to-all-done.3 = bf16[8,128,1024]{2,1,0:T(8,128)(2,1)S(1)} async-done(((bf16[8,128,1024]{2,1,0:T(8,128)(2,1)}), bf16[8,128,1024]{2,1,0:T(8,128)(2,1)S(1)}, u32[]{:S(2)}, u32[]{:S(2)}) %all-to-all-start.3) | async-done | bytes 2097184 | tf_op jit(solution)/shard_map/all_to_all | solution.py:148
  233.6 1.1 reduce_sum.22
  (89 shorter events, 26.5 us)
Async XLA Ops:
  0.6 22.8 %copy-start = (f32[1,4,64,64]{3,2,1,0:T(8,128)S(1)}, f32[1,4,64,64]{3,2,1,0:T(8,128)}, u32[]{:S(2)}) copy-start(f32[1,4,64,64]{3,2,1,0:T(8,128)} %param.24) | copy-start | bytes 196612
  1.4 1.0 copy-start.1
  2.4 0.7 copy-start.2
  3.1 0.7 copy-start.3
  3.8 8.7 %copy-start.4 = (bf16[1,1024,512]{2,1,0:T(8,128)(2,1)S(1)}, bf16[1,1024,512]{2,1,0:T(8,128)(2,1)}, u32[]{:S(2)}) copy-start(bf16[1,1024,512]{2,1,0:T(8,128)(2,1)} %param.29) | copy-start | bytes 3145732
  3.8 17.6 %copy-start.14 = (f32[1,256]{1,0:T(1,128)S(1)}, f32[1,256]{1,0:T(1,128)}, u32[]{:S(2)}) copy-start(f32[1,256]{1,0:T(1,128)} %param.23) | copy-start | bytes 3076
  3.8 18.4 %copy-start.15 = (f32[1,256]{1,0:T(1,128)S(1)}, f32[1,256]{1,0:T(1,128)}, u32[]{:S(2)}) copy-start(f32[1,256]{1,0:T(1,128)} %param.22) | copy-start | bytes 3076
  5.4 49.5 %all-to-all-start = ((bf16[8,144,1024]{2,1,0:T(8,128)(2,1)}), bf16[8,144,1024]{2,1,0:T(8,128)(2,1)S(1)}, u32[]{:S(2)}, u32[]{:S(2)}) async-start(bf16[8,144,1024]{2,1,0:T(8,128)(2,1)} %bitcast.238), calls=%async_computation | async-start | bytes 4718592 | tf_op jit(solution)/shard_map/all_to_all | solution.py:148
  12.5 42.3 %collective-permute-start = (bf16[1024,512]{1,0:T(8,128)(2,1)S(1)}, bf16[1024,512]{1,0:T(8,128)(2,1)}, u32[]{:S(2)}, u32[]{:S(2)}) collective-permute-start(bf16[1024,512]{1,0:T(8,128)(2,1)S(1)} %bitcast.231), channel_id=1, source_target_pairs={{0,64},{64,0},{128,192},{192,128},{256,320},{320,256},{384,448},{4... | collective-permute-start | bytes 3145736 | tf_op jit(solution)/shard_map/ppermute | solution.py:459
  16.5 38.3 %collective-permute-start.1 = (bf16[1024,512]{1,0:T(8,128)(2,1)}, bf16[1024,512]{1,0:T(8,128)(2,1)}, u32[]{:S(2)}, u32[]{:S(2)}) collective-permute-start(bf16[1024,512]{1,0:T(8,128)(2,1)} %bitcast.233), channel_id=1, source_target_pairs={{0,64},{64,0},{128,192},{192,128},{256,320},{320,256},{384,448},{4... | collective-permute-start | bytes 3145736 | tf_op jit(solution)/shard_map/ppermute | solution.py:459
  18.5 36.4 %collective-permute-start.2 = (bf16[512,1024]{1,0:T(8,128)(2,1)}, bf16[512,1024]{1,0:T(8,128)(2,1)}, u32[]{:S(2)}, u32[]{:S(2)}) collective-permute-start(bf16[512,1024]{1,0:T(8,128)(2,1)} %bitcast.235), channel_id=1, source_target_pairs={{0,64},{64,0},{128,192},{192,128},{256,320},{320,256},{384,448},{4... | collective-permute-start | bytes 3145736 | tf_op jit(solution)/shard_map/ppermute | solution.py:459
  23.3 8.5 %copy-start.12 = (f32[4]{0:T(128)}, f32[4]{0:T(128)S(1)}, u32[]{:S(2)}) copy-start(f32[4]{0:T(128)S(1)} %get-tuple-element.135) | copy-start | bytes 52
  24.7 0.7 copy-start.8
  28.9 0.7 copy-start.9
  59.2 58.7 %all-to-all-start.1 = ((bf16[32,48,1024]{2,1,0:T(8,128)(2,1)}), bf16[32,48,1024]{2,1,0:T(8,128)(2,1)}, u32[]{:S(2)}, u32[]{:S(2)}) async-start(bf16[32,48,1024]{2,1,0:T(8,128)(2,1)} %bitcast.237), calls=%async_computation.1 | async-start | bytes 6291456 | tf_op jit(solution)/shard_map/all_to_all | solution.py:148
  69.7 40.7 %collective-permute-start.3 = (f32[2,128,128]{2,1,0:T(8,128)}, f32[2,128,128]{2,1,0:T(8,128)}, u32[]{:S(2)}, u32[]{:S(2)}) collective-permute-start(f32[2,128,128]{2,1,0:T(8,128)} %pad_maximum_fusion), channel_id=1, source_target_pairs={{0,448},{1,449},{2,450},{3,451},{4,452},{5,453},{6,454},{7,455},{8... | collective-permute-start | bytes 393224 | tf_op jit(solution)/shard_map/ppermute | solution.py:117
  73.9 41.4 %collective-permute-start.4 = (f32[2,128,128]{2,1,0:T(8,128)}, f32[2,128,128]{2,1,0:T(8,128)}, u32[]{:S(2)}, u32[]{:S(2)}) collective-permute-start(f32[2,128,128]{2,1,0:T(8,128)} %pad_maximum_fusion), channel_id=1, source_target_pairs={{0,384},{64,448},{1,385},{65,449},{2,386},{66,450},{3,387},{67,451... | collective-permute-start | bytes 393224 | tf_op jit(solution)/shard_map/ppermute | solution.py:117
  76.3 41.0 %collective-permute-start.5 = (f32[2,128,128]{2,1,0:T(8,128)}, f32[2,128,128]{2,1,0:T(8,128)}, u32[]{:S(2)}, u32[]{:S(2)}) collective-permute-start(f32[2,128,128]{2,1,0:T(8,128)} %pad_maximum_fusion), channel_id=1, source_target_pairs={{0,320},{64,384},{128,448},{1,321},{65,385},{129,449},{2,322},{66,... | collective-permute-start | bytes 393224 | tf_op jit(solution)/shard_map/ppermute | solution.py:117
  78.3 39.0 %collective-permute-start.6 = (f32[2,128,128]{2,1,0:T(8,128)}, f32[2,128,128]{2,1,0:T(8,128)}, u32[]{:S(2)}, u32[]{:S(2)}) collective-permute-start(f32[2,128,128]{2,1,0:T(8,128)} %pad_maximum_fusion), channel_id=1, source_target_pairs={{0,256},{64,320},{128,384},{192,448},{1,257},{65,321},{129,385},{1... | collective-permute-start | bytes 393224 | tf_op jit(solution)/shard_map/ppermute | solution.py:117
  80.2 37.1 %collective-permute-start.7 = (f32[2,128,128]{2,1,0:T(8,128)}, f32[2,128,128]{2,1,0:T(8,128)}, u32[]{:S(2)}, u32[]{:S(2)}) collective-permute-start(f32[2,128,128]{2,1,0:T(8,128)} %pad_maximum_fusion), channel_id=1, source_target_pairs={{0,192},{64,256},{128,320},{192,384},{256,448},{1,193},{65,257},{1... | collective-permute-start | bytes 393224 | tf_op jit(solution)/shard_map/ppermute | solution.py:117
  110.5 6.8 %collective-permute-start.8 = (f32[2,128,128]{2,1,0:T(8,128)}, f32[2,128,128]{2,1,0:T(8,128)}, u32[]{:S(2)}, u32[]{:S(2)}) collective-permute-start(f32[2,128,128]{2,1,0:T(8,128)} %pad_maximum_fusion), channel_id=1, source_target_pairs={{0,128},{64,192},{128,256},{192,320},{256,384},{320,448},{1,129},{... | collective-permute-start | bytes 393224 | tf_op jit(solution)/shard_map/ppermute | solution.py:117
  115.3 2.6 %collective-permute-start.9 = (f32[2,128,128]{2,1,0:T(8,128)}, f32[2,128,128]{2,1,0:T(8,128)}, u32[]{:S(2)}, u32[]{:S(2)}) collective-permute-start(f32[2,128,128]{2,1,0:T(8,128)} %pad_maximum_fusion), channel_id=1, source_target_pairs={{0,64},{64,128},{128,192},{192,256},{256,320},{320,384},{384,448},... | collective-permute-start | bytes 393224 | tf_op jit(solution)/shard_map/ppermute | solution.py:117
  117.9 1.2 copy-start.5
  119.2 1.2 copy-start.6
  130.0 15.9 %copy-start.7 = (f32[1,256,128]{2,1,0:T(8,128)S(1)}, f32[1,256,128]{2,1,0:T(8,128)}, u32[]{:S(2)}) copy-start(f32[1,256,128]{2,1,0:T(8,128)} %param.19) | copy-start | bytes 393220
  130.0 15.9 %copy-start.10 = (f32[1,256,128]{2,1,0:T(8,128)S(1)}, f32[1,256,128]{2,1,0:T(8,128)}, u32[]{:S(2)}) copy-start(f32[1,256,128]{2,1,0:T(8,128)} %param.18) | copy-start | bytes 393220
  130.0 57.8 %all-to-all-start.2 = ((bf16[32,48,1024]{2,1,0:T(8,128)(2,1)}), bf16[32,48,1024]{2,1,0:T(8,128)(2,1)}, u32[]{:S(2)}, u32[]{:S(2)}) async-start(bf16[32,48,1024]{2,1,0:T(8,128)(2,1)} %bitcast.244), calls=%async_computation.2 | async-start | bytes 6291456 | tf_op jit(solution)/shard_map/all_to_all | solution.py:148
  194.1 9.2 %copy-start.13 = (f32[4]{0:T(128)S(1)}, f32[4]{0:T(128)}, u32[]{:S(2)}) copy-start(f32[4]{0:T(128)} %copy-done.12) | copy-start | bytes 52
  194.1 21.0 %copy-start.11 = (f32[1,256,128]{2,1,0:T(8,128)S(1)}, f32[1,256,128]{2,1,0:T(8,128)}, u32[]{:S(2)}) copy-start(f32[1,256,128]{2,1,0:T(8,128)} %param.21) | copy-start | bytes 393220
  194.1 21.0 %copy-start.16 = (f32[128]{0:T(128)S(1)}, f32[128]{0:T(128)}, u32[]{:S(2)}) copy-start(f32[128]{0:T(128)} %param.25) | copy-start | bytes 1540
  194.1 39.5 %all-to-all-start.3 = ((bf16[8,128,1024]{2,1,0:T(8,128)(2,1)}), bf16[8,128,1024]{2,1,0:T(8,128)(2,1)S(1)}, u32[]{:S(2)}, u32[]{:S(2)}) async-start(bf16[8,128,1024]{2,1,0:T(8,128)(2,1)} %combine_rows.1), calls=%async_computation.3 | async-start | bytes 4194304 | tf_op jit(solution)/shard_map/all_to_all | solution.py:148

commit v6 on v2

--- a/solution.py
+++ b/solution.py
@@ -11,7 +11,7 @@
 NORM_EPSILON = 1e-06
 CAPACITY = 3
 LANES = 128
-VMEM_BYTES = 60 * 1024 * 1024
+VMEM_BYTES = 36 * 1024 * 1024
 
 
 def passed_along(block, axis, distance):
@@ -139,50 +139,44 @@
     return named, earlier
 
 
-def pack_kernel(owner_count, context_size, routes_ref, hidden_ref, out_ref, spread_ref):
+def ranks_of(picks, owner_count, context_size):
+    context = jnp.floor(picks.astype(jnp.float32) * (1.0 / owner_count)).astype(jnp.int32)
+    return (picks - context * owner_count) * context_size + context
+
+
+def pack_kernel(owner_count, context_size, picks_ref, hidden_ref, out_ref, spread_ref):
     tokens, width = hidden_ref.shape
     parts = width // LANES
     per = CAPACITY * parts
     count = out_ref.shape[0] // per
-    routes = routes_ref[...].astype(jnp.float32)
-    context = jnp.floor(routes * (1.0 / owner_count))
-    pieces = (context, routes - context * owner_count)
-    diagonal = (
-        lax.broadcasted_iota(jnp.int32, (tokens, tokens), 0)
-        == lax.broadcasted_iota(jnp.int32, (tokens, tokens), 1)
-    )
-    unit = diagonal.astype(jnp.float32).astype(jnp.bfloat16)
-    context, owner = (
-        lax.dot_general(
-            piece.astype(jnp.bfloat16),
-            unit,
-            (((0,), (0,)), ((), ())),
-            preferred_element_type=jnp.float32,
-        )
-        for piece in pieces
-    )
-    ranks = (owner * context_size + context).astype(jnp.int32)
+    ranks = ranks_of(picks_ref[...], owner_count, context_size)
     named, earlier = named_and_rank(ranks, pl.program_id(0) * count, count, tokens)
+    chosen = jnp.concatenate(
+        [
+            jnp.where(jnp.logical_and(named, earlier == slot), 1.0, 0.0)
+            for slot in range(CAPACITY)
+        ],
+        axis=0,
+    ).astype(jnp.bfloat16)
+    rows = jnp.dot(chosen, hidden_ref[...], preferred_element_type=jnp.float32)
     for slot in range(CAPACITY):
-        chosen = jnp.where(jnp.logical_and(named, earlier == slot), 1.0, 0.0).astype(jnp.bfloat16)
-        rows = jnp.dot(chosen, hidden_ref[...], preferred_element_type=jnp.float32)
         for part in range(parts):
             spread_ref[pl.ds(slot * parts + part, count, stride=per), :] = rows[
-                :, part * LANES : (part + 1) * LANES
+                slot * count : (slot + 1) * count, part * LANES : (part + 1) * LANES
             ]
     out_ref[...] = spread_ref[...].astype(jnp.bfloat16)
 
 
-def pack_rows(routes, hidden, owner_count, context_size, steps):
+def pack_rows(picks, hidden, owner_count, context_size, steps):
     tokens, width = hidden.shape
     experts = owner_count * context_size
     rows = experts * CAPACITY * width // LANES
     return pl.pallas_call(
         functools.partial(pack_kernel, owner_count, context_size),
         grid=(steps,),
-        out_shape=jax.ShapeDtypeStruct((rows, LANES), jnp.bfloat16),
+        out_shape=pltpu.HBM((rows, LANES), jnp.bfloat16),
         in_specs=[
-            pl.BlockSpec(routes.shape, lambda i: (0, 0)),
+            pl.BlockSpec(picks.shape, lambda i: (0, 0)),
             pl.BlockSpec(hidden.shape, lambda i: (0, 0)),
         ],
         out_specs=pl.BlockSpec((rows // steps, LANES), lambda i: (i, 0)),
@@ -192,38 +186,10 @@
             flops=2 * experts * CAPACITY * tokens * width, bytes_accessed=rows * 256, transcendentals=0
         ),
         name="pack_rows",
-    )(routes, hidden)
-
-
-def weight_kernel(ranks_ref, weights_ref, high_ref, low_ref):
-    tokens = ranks_ref.shape[1]
-    experts = high_ref.shape[1]
-    ranks = ranks_ref[...]
-    named, earlier = named_and_rank(ranks, 0, experts, tokens)
-    row = lax.broadcasted_iota(jnp.int32, (experts, tokens), 0)
-    scale = jnp.zeros((experts, tokens), jnp.float32)
-    for pick in range(ranks.shape[0]):
-        scale = jnp.where(ranks[pick : pick + 1, :] == row, weights_ref[pick : pick + 1, :], scale)
-    high = scale.astype(jnp.bfloat16).astype(jnp.float32)
-    low = scale - high
-    for slot in range(CAPACITY):
-        here = jnp.logical_and(named, earlier == slot)
-        high_ref[slot] = jnp.where(here, high, 0.0).astype(jnp.bfloat16)
-        low_ref[slot] = jnp.where(here, low, 0.0).astype(jnp.bfloat16)
-
-
-def weight_table(ranks, weights, experts):
-    tokens = ranks.shape[1]
-    shape = jax.ShapeDtypeStruct((CAPACITY, experts, tokens), jnp.bfloat16)
-    return pl.pallas_call(
-        weight_kernel,
-        out_shape=(shape, shape),
-        compiler_params=pltpu.CompilerParams(vmem_limit_bytes=32 * 1024 * 1024),
-        cost_estimate=pl.CostEstimate(
-            flops=40 * experts * tokens, bytes_accessed=4 * CAPACITY * experts * tokens, transcendentals=0
-        ),
-        name="weight_table",
-    )(ranks, weights)
+    )(
+        pltpu.with_memory_space_constraint(picks, pltpu.HBM),
+        pltpu.with_memory_space_constraint(hidden, pltpu.HBM),
+    )
 
 
 def expert_kernel(
@@ -263,12 +229,17 @@
 
     @pl.when(first)
     def _():
-        for load in loads:
-            load.wait()
+        loads[0].wait()
+        loads[1].wait()
 
     gate = jnp.dot(rows, gate_here[...], preferred_element_type=jnp.float32)
     up = jnp.dot(rows, up_here[...], preferred_element_type=jnp.float32)
     active = (gate / (1.0 + jnp.exp(-gate)) * up).astype(jnp.bfloat16)
+
+    @pl.when(first)
+    def _():
+        loads[2].wait()
+
     produced = jnp.dot(active, down_here[...], preferred_element_type=jnp.float32)
     for slot in range(CAPACITY):
         for part in range(parts):
@@ -284,10 +255,14 @@
     slots = rows * LANES // width
     block = pl.BlockSpec((rows // steps, LANES), lambda i: (i, 0))
     whole = pl.BlockSpec(memory_space=pl.ANY)
+    weights = [
+        pltpu.with_memory_space_constraint(weight, pltpu.HBM)
+        for weight in (gate_weights, up_weights, down_weights)
+    ]
     return pl.pallas_call(
         expert_kernel,
         grid=(steps,),
-        out_shape=jax.ShapeDtypeStruct(received.shape, jnp.bfloat16),
+        out_shape=pltpu.HBM(received.shape, jnp.bfloat16),
         in_specs=[block, whole, whole, whole],
         out_specs=block,
         scratch_shapes=[
@@ -304,10 +279,10 @@
             transcendentals=slots * units,
         ),
         name="expert_rows",
-    )(received, gate_weights, up_weights, down_weights)
-
-
-def combine_kernel(returned_ref, high_ref, low_ref, out_ref, spread_ref, total_ref):
+    )(received, *weights)
+
+
+def combine_kernel(owner_count, context_size, picks_ref, weights_ref, returned_ref, out_ref, spread_ref, total_ref):
     tokens, width = out_ref.shape
     parts = width // LANES
     per = CAPACITY * parts
@@ -319,19 +294,35 @@
         total_ref[...] = jnp.zeros_like(total_ref)
 
     spread_ref[...] = returned_ref[...].astype(jnp.float32)
-    total = total_ref[...]
-    for slot in range(CAPACITY):
-        rows = jnp.concatenate(
-            [
-                spread_ref[pl.ds(slot * parts + part, count, stride=per), :].astype(jnp.bfloat16)
-                for part in range(parts)
-            ],
-            axis=1,
-        )
-        for table in (high_ref, low_ref):
-            total = total + lax.dot_general(
-                table[slot], rows, (((0,), (0,)), ((), ())), preferred_element_type=jnp.float32
+    ranks = ranks_of(picks_ref[...], owner_count, context_size)
+    named, earlier = named_and_rank(ranks, step * count, count, tokens)
+    row = lax.broadcasted_iota(jnp.int32, (count, tokens), 0) + step * count
+    scale = jnp.zeros((count, tokens), jnp.float32)
+    for pick in range(ranks.shape[0]):
+        scale = jnp.where(ranks[pick : pick + 1, :] == row, weights_ref[pick : pick + 1, :], scale)
+    high = scale.astype(jnp.bfloat16).astype(jnp.float32)
+    halves = jnp.concatenate([high, scale - high], axis=1)
+    at = jnp.concatenate([jnp.where(named, earlier, -1.0)] * 2, axis=1)
+    table = jnp.concatenate(
+        [jnp.where(at == slot, halves, 0.0) for slot in range(CAPACITY)], axis=0
+    ).astype(jnp.bfloat16)
+    rows = jnp.concatenate(
+        [
+            jnp.concatenate(
+                [
+                    spread_ref[pl.ds(slot * parts + part, count, stride=per), :].astype(jnp.bfloat16)
+                    for part in range(parts)
+                ],
+                axis=1,
             )
+            for slot in range(CAPACITY)
+        ],
+        axis=0,
+    )
+    both = lax.dot_general(
+        table, rows, (((0,), (0,)), ((), ())), preferred_element_type=jnp.float32
+    )
+    total = total_ref[...] + (both[:tokens] + both[tokens:])
     total_ref[...] = total
 
     @pl.when(step == pl.num_programs(0) - 1)
@@ -339,15 +330,18 @@
         out_ref[...] = total.astype(jnp.bfloat16)
 
 
-def combine_rows(returned, high, low, tokens, width, steps):
+def combine_rows(picks, weights, returned, owner_count, context_size, width, steps):
+    tokens = picks.shape[1]
     rows = returned.shape[0]
-    experts = high.shape[1]
-    table = pl.BlockSpec((CAPACITY, experts // steps, tokens), lambda i: (0, i, 0))
     return pl.pallas_call(
-        combine_kernel,
+        functools.partial(combine_kernel, owner_count, context_size),
         grid=(steps,),
         out_shape=jax.ShapeDtypeStruct((tokens, width), jnp.bfloat16),
-        in_specs=[pl.BlockSpec((rows // steps, LANES), lambda i: (i, 0)), table, table],
+        in_specs=[
+            pl.BlockSpec(picks.shape, lambda i: (0, 0)),
+            pl.BlockSpec(weights.shape, lambda i: (0, 0)),
+            pl.BlockSpec((rows // steps, LANES), lambda i: (i, 0)),
+        ],
         out_specs=pl.BlockSpec((tokens, width), lambda i: (0, 0)),
         scratch_shapes=[
             pltpu.VMEM((rows // steps, LANES), jnp.float32),
@@ -358,7 +352,7 @@
             flops=4 * rows * LANES * tokens, bytes_accessed=2 * rows * LANES, transcendentals=0
         ),
         name="combine_rows",
-    )(returned, high, low)
+    )(picks, weights, returned)
 
 
 def exchange(rows):
@@ -381,11 +375,11 @@
     up_weights,
     down_weights,
 ):
-    tokens, width = hidden.shape
+    width = hidden.shape[1]
     context_size = lax.axis_size("ctx")
     owner_count = lax.axis_size("exp")
-    experts = context_size * owner_count
-    outgoing = pack_rows(routes, hidden, owner_count, context_size, 4)
+    picks = routes.T
+    outgoing = pack_rows(picks, hidden, owner_count, context_size, 4)
     received = exchange(outgoing)
     pieces, incoming_state = delta_front(
         queries, key_vectors, values, write_strength, log_fading_factor, block_inverse
@@ -393,9 +387,9 @@
     received, incoming_state = lax.optimization_barrier((received, incoming_state))
     produced = expert_rows(received, gate_weights[0], up_weights[0], down_weights[0], 4)
     returned = exchange(produced)
-    ranks = (routes % owner_count * context_size + routes // owner_count).T
-    high, low = weight_table(ranks, route_weights.T, experts)
-    expert_output = combine_rows(returned, high, low, tokens, width, 4)
+    expert_output = combine_rows(
+        picks, route_weights.T, returned, owner_count, context_size, width, 4
+    )
     _, attended = run_blocks(pieces, incoming_state)
     mixer_output = gated_norm(attended.reshape(out_gate.shape), norm_gain, out_gate)
     return (mixer_output, expert_output)

time: 213 us -> 207 us (0.972)
  matrix products: 27.6 us -> 36.5 us
  local copies, waits for them, and re-layouts: 8.33 us -> 3.43 us
  waiting for transfers between devices: 79.7 us -> 75.8 us
  Pallas kernels: 22.4 us -> 18.9 us
  starting transfers between devices: 64.9 us -> 62.2 us
    all_to_all x2, waiting for transfers between devices: 70.6 us -> 65.7 us  [exchange(): lax.all_to_all(rows, ('exp', 'ctx'), split_axis=0, concat_axis=0, tiled=T...]
    unnamed x28 -> x19, local copies, waits for them, and re-layouts: 5.16 us -> 0.56 us
    dot_general x4, matrix products: 0.83 us -> 4.33 us  [compose(): jnp.einsum('qfz,qze->qfe', segment_mapping, current_addend, precision=TOP...]
    dot_general x4, matrix products: 0.82 us -> 4.19 us  [compose(): jnp.einsum('qfz,qze->qfe', segment_mapping, current_mapping, precision=TO...]
    pallas_call x3 -> x2, Pallas kernels: 17.2 us -> 14.2 us  [the longest x1 10.3 us: expert_rows(): pl.pallas_call(expert_kernel, grid=(steps,), out_shape=pltpu.HBM(received...]
  transfers between devices with their start and end apart: 9 -> 9, of which waited for: 9 -> 9; matrix products, arithmetic and copies ran while one was open for 18% -> 23% of each run, Pallas kernels for 0% -> 0%
where the time goes in v6:
time: 207 us; the launch traced here: 204 us
  waiting for transfers between devices  75.8 us (37%)
  starting transfers between devices  62.2 us (30%)
  matrix products  36.5 us (18%)
  Pallas kernels  18.9 us (9%)
  other arithmetic  6.17 us (3%)
  local copies, waits for them, and re-layouts  3.43 us (2%)
    all_to_all x2, waiting for transfers between devices, exchange(): lax.all_to_all(rows, ('exp', 'ctx'), split_axis=0, concat_axis=0, tiled=T...  65.7 us
    all_to_all x2, starting transfers between devices, exchange(): lax.all_to_all(rows, ('exp', 'ctx'), split_axis=0, concat_axis=0, tiled=T...  33.4 us
    ppermute x7, starting transfers between devices, passed_along(): return lax.ppermute(block, axis, route)  28.8 us
    pallas_call x1, Pallas kernels, expert_rows(): pl.pallas_call(expert_kernel, grid=(steps,), out_shape=pltpu.HBM(received...  10.3 us
    ppermute x7, waiting for transfers between devices, passed_along(): return lax.ppermute(block, axis, route)  10.1 us
    dot_general x4, matrix products, block_step(): jnp.einsum('sch,scv->shv', faded_keys, fresh_values, precision=TOP_PRECIS...  6.69 us
    dot_general x4, matrix products, block_step(): jnp.einsum('sij,sjv->siv', causal, fresh_values, precision=TOP_PRECISION)  6.18 us
    pallas_call x1, Pallas kernels, pack_rows(): pl.pallas_call(functools.partial(pack_kernel, owner_count, context_size),...  4.76 us
  transfers between devices with their start and end apart: 9, of which 9 were waited for; matrix products, arithmetic and copies ran while one was open for 23% of the time, Pallas kernels for 0%

profile of v6, /device:TPU:1, one launch (start us, length us, event | category | flops | bytes accessed | tf_op | source)
XLA Modules:
  0.0 204.3 jit_solution(8136834931774477480)
XLA Ops:
  0.6 4.8 %pack_rows.1 = bf16[12288,128]{1,0:T(8,128)(2,1)} custom-call(s32[10,128]{1,0:T(8,128)} %bitcast.214, bf16[128,1024]{1,0:T(8,128)(2,1)} %hidden_ref.1), custom_call_target="tpu_custom_call" | custom-call | flops 402653184 | bytes 3145728 | tf_op jit(solution)/shard_map/pack_rows/pallas_call | solution.py:174
  5.4 22.2 %all-to-all-start = ((bf16[512,24,128]{2,1,0:T(8,128)(2,1)}), bf16[512,24,128]{2,1,0:T(8,128)(2,1)S(1)}, u32[]{:S(2)}, u32[]{:S(2)}) async-start(bf16[512,24,128]{2,1,0:T(8,128)(2,1)} %bitcast.217), calls=%async_computation | async-start | bytes 6291456 | tf_op jit(solution)/shard_map/all_to_all | solution.py:359
  30.1 1.3 fusion.43
  31.4 1.4 convolution_bitcast_fusion.2
  33.2 1.4 fusion.27
  34.6 8.8 %while.24 = (s32[]{:T(128)}, f32[1,128,128]{2,1,0:T(8,128)S(1)}, f32[1,128,128]{2,1,0:T(8,128)S(1)}, f32[4,1,128,128]{3,2,1,0:T(8,128)}, f32[4,1,128,128]{3,2,1,0:T(8,128)}, /*index=5*/s32[]{:T(128)}) while((s32[]{:T(128)}, f32[1,128,128]{2,1,0:T(8,128)S(1)}, f32[1,128,128]{2,1,0:T(8,128)S(1)}, f32[4,1,128,128]{3,2,1,0:T(8,128)}, ...), condition=%wide.region_2.3_spmd, body=%wide.region_1.2_spmd.sunk | while | flops 50348032 | bytes 722001 | solution.py:109
  34.6 1.0 convolution_bitcast_fusion.11
  35.7 1.1 fusion.99
  36.8 1.0 convolution_bitcast_fusion.11
  37.8 1.1 fusion.99
  39.0 1.0 convolution_bitcast_fusion.11
  40.0 1.1 fusion.99
  41.2 1.0 convolution_bitcast_fusion.11
  42.2 1.1 fusion.99
  43.5 3.5 %collective-permute-start = (bf16[1,128,128]{2,1,0:T(8,128)(2,1)S(1)}, bf16[1,128,128]{2,1,0:T(8,128)(2,1)S(1)}, u32[]{:S(2)}, u32[]{:S(2)}) collective-permute-start(bf16[1,128,128]{2,1,0:T(8,128)(2,1)S(1)} %fusion.42), channel_id=1, source_target_pairs={{0,64},{64,128},{128,192},{192,256},{256,320},{320,384},{384,448},... | collective-permute-start | bytes 98312 | tf_op jit(solution)/shard_map/ppermute | solution.py:20
  47.1 2.7 %collective-permute-done = bf16[1,128,128]{2,1,0:T(8,128)(2,1)S(1)} collective-permute-done((bf16[1,128,128]{2,1,0:T(8,128)(2,1)S(1)}, bf16[1,128,128]{2,1,0:T(8,128)(2,1)S(1)}, u32[]{:S(2)}, u32[]{:S(2)}) %collective-permute-start) | collective-permute-done | bytes 32800 | tf_op jit(solution)/shard_map/ppermute | solution.py:20
  50.0 2.6 %collective-permute-start.1 = (bf16[1,128,128]{2,1,0:T(8,128)(2,1)S(1)}, bf16[1,128,128]{2,1,0:T(8,128)(2,1)S(1)}, u32[]{:S(2)}, u32[]{:S(2)}) collective-permute-start(bf16[1,128,128]{2,1,0:T(8,128)(2,1)S(1)} %fusion.41), channel_id=1, source_target_pairs={{0,64},{64,128},{128,192},{192,256},{256,320},{320,384},{384,448},... | collective-permute-start | bytes 98312 | tf_op jit(solution)/shard_map/ppermute | solution.py:20
  52.6 1.3 collective-permute-done.1
  54.0 4.5 %collective-permute-start.2 = (bf16[1,128,128]{2,1,0:T(8,128)(2,1)S(1)}, bf16[1,128,128]{2,1,0:T(8,128)(2,1)S(1)}, u32[]{:S(2)}, u32[]{:S(2)}) collective-permute-start(bf16[1,128,128]{2,1,0:T(8,128)(2,1)S(1)} %fusion.40), channel_id=1, source_target_pairs={{0,64},{64,128},{128,192},{192,256},{256,320},{320,384},{384,448},... | collective-permute-start | bytes 98312 | tf_op jit(solution)/shard_map/ppermute | solution.py:20
  58.5 1.4 collective-permute-done.2
  60.1 4.5 %collective-permute-start.3 = (bf16[1,128,128]{2,1,0:T(8,128)(2,1)S(1)}, bf16[1,128,128]{2,1,0:T(8,128)(2,1)S(1)}, u32[]{:S(2)}, u32[]{:S(2)}) collective-permute-start(bf16[1,128,128]{2,1,0:T(8,128)(2,1)S(1)} %fusion.39), channel_id=1, source_target_pairs={{0,64},{64,128},{128,192},{192,256},{256,320},{320,384},{384,448},... | collective-permute-start | bytes 98312 | tf_op jit(solution)/shard_map/ppermute | solution.py:20
  64.6 1.0 collective-permute-done.3
  65.8 4.4 %collective-permute-start.4 = (bf16[1,128,128]{2,1,0:T(8,128)(2,1)S(1)}, bf16[1,128,128]{2,1,0:T(8,128)(2,1)S(1)}, u32[]{:S(2)}, u32[]{:S(2)}) collective-permute-start(bf16[1,128,128]{2,1,0:T(8,128)(2,1)S(1)} %fusion.38), channel_id=1, source_target_pairs={{0,64},{64,128},{128,192},{192,256},{256,320},{320,384},{384,448},... | collective-permute-start | bytes 98312 | tf_op jit(solution)/shard_map/ppermute | solution.py:20
  70.2 1.7 collective-permute-done.4
  72.1 4.6 %collective-permute-start.5 = (bf16[1,128,128]{2,1,0:T(8,128)(2,1)S(1)}, bf16[1,128,128]{2,1,0:T(8,128)(2,1)S(1)}, u32[]{:S(2)}, u32[]{:S(2)}) collective-permute-start(bf16[1,128,128]{2,1,0:T(8,128)(2,1)S(1)} %fusion.37), channel_id=1, source_target_pairs={{0,64},{64,128},{128,192},{192,256},{256,320},{320,384},{384,448},... | collective-permute-start | bytes 98312 | tf_op jit(solution)/shard_map/ppermute | solution.py:20
  76.7 1.0 collective-permute-done.5
  77.9 4.7 %collective-permute-start.6 = (bf16[1,128,128]{2,1,0:T(8,128)(2,1)S(1)}, bf16[1,128,128]{2,1,0:T(8,128)(2,1)S(1)}, u32[]{:S(2)}, u32[]{:S(2)}) collective-permute-start(bf16[1,128,128]{2,1,0:T(8,128)(2,1)S(1)} %fusion.36), channel_id=1, source_target_pairs={{0,64},{64,128},{128,192},{192,256},{256,320},{320,384},{384,448},... | collective-permute-start | bytes 98312 | tf_op jit(solution)/shard_map/ppermute | solution.py:20
  82.5 1.1 collective-permute-done.6
  83.6 19.6 %all-to-all-done = bf16[512,24,128]{2,1,0:T(8,128)(2,1)S(1)} async-done(((bf16[512,24,128]{2,1,0:T(8,128)(2,1)}), bf16[512,24,128]{2,1,0:T(8,128)(2,1)S(1)}, u32[]{:S(2)}, u32[]{:S(2)}) %all-to-all-start) | async-done | bytes 3145760 | tf_op jit(solution)/shard_map/all_to_all | solution.py:359
  103.2 10.3 %expert_rows.1 = bf16[12288,128]{1,0:T(8,128)(2,1)} custom-call(bf16[12288,128]{1,0:T(8,128)(2,1)S(1)} %bitcast.213, bf16[1024,512]{1,0:T(8,128)(2,1)} %bitcast.232, bf16[1024,512]{1,0:T(8,128)(2,1)} %bitcast.233, bf16[512,1024]{1,0:T(8,128)(2,1)} %bitcast.234), custom_call_target="tpu_custom_call" | custom-call | flops 4831838208 | bytes 9437184 | tf_op jit(solution)/shard_map/expert_rows/pallas_call | solution.py:262
  113.5 11.3 %all-to-all-start.1 = ((bf16[512,24,128]{2,1,0:T(8,128)(2,1)}), bf16[512,24,128]{2,1,0:T(8,128)(2,1)S(1)}, u32[]{:S(2)}, u32[]{:S(2)}) async-start(bf16[512,24,128]{2,1,0:T(8,128)(2,1)} %bitcast.223), calls=%async_computation.1 | async-start | bytes 6291456 | tf_op jit(solution)/shard_map/all_to_all | solution.py:359
  124.8 1.9 fusion.28
  126.7 1.7 broadcast_multiply_fusion
  128.4 22.9 %while.25 = (s32[]{:T(128)}, f32[1,128,128]{2,1,0:T(8,128)S(1)}, f32[4,1,64,128]{3,2,1,0:T(8,128)}, f32[4,1,1]{0,2,1:T(1,128)S(1)}, f32[4,1,64,128]{3,2,1,0:T(8,...) while((s32[]{:T(128)}, f32[1,128,128]{2,1,0:T(8,128)S(1)}, ...), condition=%wide.region_4.5_spmd, body=%wide.region_3.4_spmd.sunk | while | flops 44089344 | bytes 625281 | solution.py:75
  131.0 1.7 fusion.108
  132.6 1.5 fusion.110
  135.1 1.0 convolution_subtract_fusion.3
  136.7 1.7 fusion.108
  138.4 1.5 fusion.110
  140.9 1.0 convolution_subtract_fusion.3
  142.4 1.7 fusion.108
  144.1 1.5 fusion.110
  148.2 1.7 fusion.108
  149.8 1.5 fusion.110
  151.4 1.0 multiply_reduce_fusion
  152.5 1.7 multiply_multiply_fusion
  154.2 46.1 %all-to-all-done.1 = bf16[512,24,128]{2,1,0:T(8,128)(2,1)S(1)} async-done(((bf16[512,24,128]{2,1,0:T(8,128)(2,1)}), bf16[512,24,128]{2,1,0:T(8,128)(2,1)S(1)}, u32[]{:S(2)}, u32[]{:S(2)}) %all-to-all-start.1) | async-done | bytes 3145760 | tf_op jit(solution)/shard_map/all_to_all | solution.py:359
  200.4 3.9 %combine_rows.1 = bf16[128,1024]{1,0:T(8,128)(2,1)} custom-call(s32[10,128]{1,0:T(8,128)S(1)} %bitcast.215, f32[10,128]{1,0:T(8,128)S(1)} %bitcast.216, bf16[12288,128]{1,0:T(8,128)(2,1)S(1)} %bitcast.212), custom_call_target="tpu_custom_call" | custom-call | flops 805306368 | bytes 3145728 | tf_op jit(solution)/shard_map/combine_rows/pallas_call | solution.py:336
  (60 shorter events, 12.4 us)
Async XLA Ops:
  0.6 29.5 %copy-start = (f32[1,4,64,64]{3,2,1,0:T(8,128)S(1)}, f32[1,4,64,64]{3,2,1,0:T(8,128)}, u32[]{:S(2)}) copy-start(f32[1,4,64,64]{3,2,1,0:T(8,128)} %param.24) | copy-start | bytes 196612
  5.4 22.7 %copy-start.6 = (f32[1,256]{1,0:T(1,128)S(1)}, f32[1,256]{1,0:T(1,128)}, u32[]{:S(2)}) copy-start(f32[1,256]{1,0:T(1,128)} %param.23) | copy-start | bytes 3076
  5.4 23.4 %copy-start.7 = (f32[1,256]{1,0:T(1,128)S(1)}, f32[1,256]{1,0:T(1,128)}, u32[]{:S(2)}) copy-start(f32[1,256]{1,0:T(1,128)} %param.22) | copy-start | bytes 3076
  5.4 26.0 %copy-start.3 = (f32[1,256,128]{2,1,0:T(8,128)S(1)}, f32[1,256,128]{2,1,0:T(8,128)}, u32[]{:S(2)}) copy-start(f32[1,256,128]{2,1,0:T(8,128)} %param.19) | copy-start | bytes 393220
  5.4 97.8 %all-to-all-start = ((bf16[512,24,128]{2,1,0:T(8,128)(2,1)}), bf16[512,24,128]{2,1,0:T(8,128)(2,1)S(1)}, u32[]{:S(2)}, u32[]{:S(2)}) async-start(bf16[512,24,128]{2,1,0:T(8,128)(2,1)} %bitcast.217), calls=%async_computation | async-start | bytes 6291456 | tf_op jit(solution)/shard_map/all_to_all | solution.py:359
  31.4 1.8 copy-start.4
  33.2 1.4 copy-start.5
  43.5 6.3 %collective-permute-start = (bf16[1,128,128]{2,1,0:T(8,128)(2,1)S(1)}, bf16[1,128,128]{2,1,0:T(8,128)(2,1)S(1)}, u32[]{:S(2)}, u32[]{:S(2)}) collective-permute-start(bf16[1,128,128]{2,1,0:T(8,128)(2,1)S(1)} %fusion.42), channel_id=1, source_target_pairs={{0,64},{64,128},{128,192},{192,256},{256,320},{320,384},{384,448},... | collective-permute-start | bytes 98312 | tf_op jit(solution)/shard_map/ppermute | solution.py:20
  50.0 3.9 %collective-permute-start.1 = (bf16[1,128,128]{2,1,0:T(8,128)(2,1)S(1)}, bf16[1,128,128]{2,1,0:T(8,128)(2,1)S(1)}, u32[]{:S(2)}, u32[]{:S(2)}) collective-permute-start(bf16[1,128,128]{2,1,0:T(8,128)(2,1)S(1)} %fusion.41), channel_id=1, source_target_pairs={{0,64},{64,128},{128,192},{192,256},{256,320},{320,384},{384,448},... | collective-permute-start | bytes 98312 | tf_op jit(solution)/shard_map/ppermute | solution.py:20
  54.0 5.8 %collective-permute-start.2 = (bf16[1,128,128]{2,1,0:T(8,128)(2,1)S(1)}, bf16[1,128,128]{2,1,0:T(8,128)(2,1)S(1)}, u32[]{:S(2)}, u32[]{:S(2)}) collective-permute-start(bf16[1,128,128]{2,1,0:T(8,128)(2,1)S(1)} %fusion.40), channel_id=1, source_target_pairs={{0,64},{64,128},{128,192},{192,256},{256,320},{320,384},{384,448},... | collective-permute-start | bytes 98312 | tf_op jit(solution)/shard_map/ppermute | solution.py:20
  60.1 5.5 %collective-permute-start.3 = (bf16[1,128,128]{2,1,0:T(8,128)(2,1)S(1)}, bf16[1,128,128]{2,1,0:T(8,128)(2,1)S(1)}, u32[]{:S(2)}, u32[]{:S(2)}) collective-permute-start(bf16[1,128,128]{2,1,0:T(8,128)(2,1)S(1)} %fusion.39), channel_id=1, source_target_pairs={{0,64},{64,128},{128,192},{192,256},{256,320},{320,384},{384,448},... | collective-permute-start | bytes 98312 | tf_op jit(solution)/shard_map/ppermute | solution.py:20
  65.8 6.1 %collective-permute-start.4 = (bf16[1,128,128]{2,1,0:T(8,128)(2,1)S(1)}, bf16[1,128,128]{2,1,0:T(8,128)(2,1)S(1)}, u32[]{:S(2)}, u32[]{:S(2)}) collective-permute-start(bf16[1,128,128]{2,1,0:T(8,128)(2,1)S(1)} %fusion.38), channel_id=1, source_target_pairs={{0,64},{64,128},{128,192},{192,256},{256,320},{320,384},{384,448},... | collective-permute-start | bytes 98312 | tf_op jit(solution)/shard_map/ppermute | solution.py:20
  72.1 5.6 %collective-permute-start.5 = (bf16[1,128,128]{2,1,0:T(8,128)(2,1)S(1)}, bf16[1,128,128]{2,1,0:T(8,128)(2,1)S(1)}, u32[]{:S(2)}, u32[]{:S(2)}) collective-permute-start(bf16[1,128,128]{2,1,0:T(8,128)(2,1)S(1)} %fusion.37), channel_id=1, source_target_pairs={{0,64},{64,128},{128,192},{192,256},{256,320},{320,384},{384,448},... | collective-permute-start | bytes 98312 | tf_op jit(solution)/shard_map/ppermute | solution.py:20
  77.9 5.8 %collective-permute-start.6 = (bf16[1,128,128]{2,1,0:T(8,128)(2,1)S(1)}, bf16[1,128,128]{2,1,0:T(8,128)(2,1)S(1)}, u32[]{:S(2)}, u32[]{:S(2)}) collective-permute-start(bf16[1,128,128]{2,1,0:T(8,128)(2,1)S(1)} %fusion.36), channel_id=1, source_target_pairs={{0,64},{64,128},{128,192},{192,256},{256,320},{320,384},{384,448},... | collective-permute-start | bytes 98312 | tf_op jit(solution)/shard_map/ppermute | solution.py:20
  113.5 86.9 %all-to-all-start.1 = ((bf16[512,24,128]{2,1,0:T(8,128)(2,1)}), bf16[512,24,128]{2,1,0:T(8,128)(2,1)S(1)}, u32[]{:S(2)}, u32[]{:S(2)}) async-start(bf16[512,24,128]{2,1,0:T(8,128)(2,1)} %bitcast.223), calls=%async_computation.1 | async-start | bytes 6291456 | tf_op jit(solution)/shard_map/all_to_all | solution.py:359
  124.7 27.7 %copy-start.8 = (f32[128]{0:T(128)S(1)}, f32[128]{0:T(128)}, u32[]{:S(2)}) copy-start(f32[128]{0:T(128)} %param.25) | copy-start | bytes 1540
  124.8 75.6 %copy-start.1 = (s32[128,10]{0,1:T(8,128)S(1)}, s32[128,10]{0,1:T(8,128)}, u32[]{:S(2)}) copy-start(s32[128,10]{0,1:T(8,128)} %param.27) | copy-start | bytes 15364
  124.8 75.6 %copy-start.2 = (f32[128,10]{0,1:T(8,128)S(1)}, f32[128,10]{0,1:T(8,128)}, u32[]{:S(2)}) copy-start(f32[128,10]{0,1:T(8,128)} %param.28) | copy-start | bytes 15364

commit v7 on v6

--- a/solution.py
+++ b/solution.py
@@ -144,43 +144,56 @@
     return (picks - context * owner_count) * context_size + context
 
 
-def pack_kernel(owner_count, context_size, picks_ref, hidden_ref, out_ref, spread_ref):
+def pack_kernel(
+    owner_count, context_size, blocks, picks_ref, hidden_ref, out_ref, spread_ref, result_ref, sent
+):
     tokens, width = hidden_ref.shape
     parts = width // LANES
     per = CAPACITY * parts
-    count = out_ref.shape[0] // per
+    block = out_ref.shape[0] // blocks
+    count = block // per
     ranks = ranks_of(picks_ref[...], owner_count, context_size)
-    named, earlier = named_and_rank(ranks, pl.program_id(0) * count, count, tokens)
-    chosen = jnp.concatenate(
-        [
-            jnp.where(jnp.logical_and(named, earlier == slot), 1.0, 0.0)
-            for slot in range(CAPACITY)
-        ],
-        axis=0,
-    ).astype(jnp.bfloat16)
-    rows = jnp.dot(chosen, hidden_ref[...], preferred_element_type=jnp.float32)
-    for slot in range(CAPACITY):
-        for part in range(parts):
-            spread_ref[pl.ds(slot * parts + part, count, stride=per), :] = rows[
-                slot * count : (slot + 1) * count, part * LANES : (part + 1) * LANES
-            ]
-    out_ref[...] = spread_ref[...].astype(jnp.bfloat16)
-
-
-def pack_rows(picks, hidden, owner_count, context_size, steps):
+    moves = []
+    for i in range(blocks):
+        named, earlier = named_and_rank(ranks, i * count, count, tokens)
+        chosen = jnp.concatenate(
+            [
+                jnp.where(jnp.logical_and(named, earlier == slot), 1.0, 0.0)
+                for slot in range(CAPACITY)
+            ],
+            axis=0,
+        ).astype(jnp.bfloat16)
+        rows = jnp.dot(chosen, hidden_ref[...], preferred_element_type=jnp.float32)
+        for slot in range(CAPACITY):
+            for part in range(parts):
+                spread_ref[i, pl.ds(slot * parts + part, count, stride=per), :] = rows[
+                    slot * count : (slot + 1) * count, part * LANES : (part + 1) * LANES
+                ]
+        result_ref[i] = spread_ref[i].astype(jnp.bfloat16)
+        move = pltpu.make_async_copy(
+            result_ref.at[i], out_ref.at[pl.ds(i * block, block), :], sent.at[i]
+        )
+        move.start()
+        moves.append(move)
+    for move in moves:
+        move.wait()
+
+
+def pack_rows(picks, hidden, owner_count, context_size, blocks):
     tokens, width = hidden.shape
     experts = owner_count * context_size
     rows = experts * CAPACITY * width // LANES
+    here = pl.BlockSpec(memory_space=pltpu.VMEM)
     return pl.pallas_call(
-        functools.partial(pack_kernel, owner_count, context_size),
-        grid=(steps,),
+        functools.partial(pack_kernel, owner_count, context_size, blocks),
         out_shape=pltpu.HBM((rows, LANES), jnp.bfloat16),
-        in_specs=[
-            pl.BlockSpec(picks.shape, lambda i: (0, 0)),
-            pl.BlockSpec(hidden.shape, lambda i: (0, 0)),
+        in_specs=[here, here],
+        out_specs=pl.BlockSpec(memory_space=pl.ANY),
+        scratch_shapes=[
+            pltpu.VMEM((blocks, rows // blocks, LANES), jnp.float32),
+            pltpu.VMEM((blocks, rows // blocks, LANES), jnp.bfloat16),
+            pltpu.SemaphoreType.DMA((blocks,)),
         ],
-        out_specs=pl.BlockSpec((rows // steps, LANES), lambda i: (i, 0)),
-        scratch_shapes=[pltpu.VMEM((rows // steps, LANES), jnp.float32)],
         compiler_params=pltpu.CompilerParams(vmem_limit_bytes=VMEM_BYTES),
         cost_estimate=pl.CostEstimate(
             flops=2 * experts * CAPACITY * tokens * width, bytes_accessed=rows * 256, transcendentals=0
@@ -193,84 +206,107 @@
 
 
 def expert_kernel(
-    received_ref, gate_ref, up_ref, down_ref, out_ref, spread_ref, gate_here, up_here, down_here, ready
+    blocks,
+    received_ref,
+    gate_ref,
+    up_ref,
+    down_ref,
+    out_ref,
+    spread_ref,
+    result_ref,
+    gate_here,
+    up_here,
+    down_here,
+    ready,
+    sent,
 ):
     width = gate_here.shape[0]
     parts = width // LANES
     per = CAPACITY * parts
-    count = received_ref.shape[0] // per
+    block = received_ref.shape[0] // blocks
+    count = block // per
     loads = [
         pltpu.make_async_copy(there, here, ready.at[i])
         for i, (there, here) in enumerate(
             ((gate_ref, gate_here), (up_ref, up_here), (down_ref, down_here))
         )
     ]
-    first = pl.program_id(0) == 0
-
-    @pl.when(first)
-    def _():
-        for load in loads:
-            load.start()
-
-    spread_ref[...] = received_ref[...].astype(jnp.float32)
-    rows = jnp.concatenate(
-        [
-            jnp.concatenate(
-                [
-                    spread_ref[pl.ds(slot * parts + part, count, stride=per), :].astype(jnp.bfloat16)
-                    for part in range(parts)
-                ],
-                axis=1,
+    for load in loads:
+        load.start()
+
+    def unpacked(i):
+        spread_ref[i] = received_ref[pl.ds(i * block, block), :].astype(jnp.float32)
+        return jnp.concatenate(
+            [
+                jnp.concatenate(
+                    [
+                        spread_ref[i, pl.ds(slot * parts + part, count, stride=per), :].astype(
+                            jnp.bfloat16
+                        )
+                        for part in range(parts)
+                    ],
+                    axis=1,
+                )
+                for slot in range(CAPACITY)
+            ],
+            axis=0,
+        )
+
+    rows = unpacked(0)
+    moves = []
+    for i in range(blocks):
+        if i == 0:
+            loads[0].wait()
+        gate = jnp.dot(rows, gate_here[...], preferred_element_type=jnp.float32)
+        if i == 0:
+            loads[1].wait()
+            loads[2].wait()
+        up = jnp.dot(rows, up_here[...], preferred_element_type=jnp.float32)
+        if i + 1 < blocks:
+            rows = unpacked(i + 1)
+        active = (gate / (1.0 + jnp.exp(-gate)) * up).astype(jnp.bfloat16)
+        produced = jnp.dot(active, down_here[...], preferred_element_type=jnp.float32)
+        for slot in range(CAPACITY):
+            for part in range(parts):
+                spread_ref[i, pl.ds(slot * parts + part, count, stride=per), :] = produced[
+                    slot * count : (slot + 1) * count, part * LANES : (part + 1) * LANES
+                ]
+        for half in range(2):
+            at = pl.ds(half * (block // 2), block // 2)
+            result_ref[i, at, :] = spread_ref[i, at, :].astype(jnp.bfloat16)
+            move = pltpu.make_async_copy(
+                result_ref.at[i, at, :],
+                out_ref.at[pl.ds(i * block + half * (block // 2), block // 2), :],
+                sent.at[2 * i + half],
             )
-            for slot in range(CAPACITY)
-        ],
-        axis=0,
-    )
-
-    @pl.when(first)
-    def _():
-        loads[0].wait()
-        loads[1].wait()
-
-    gate = jnp.dot(rows, gate_here[...], preferred_element_type=jnp.float32)
-    up = jnp.dot(rows, up_here[...], preferred_element_type=jnp.float32)
-    active = (gate / (1.0 + jnp.exp(-gate)) * up).astype(jnp.bfloat16)
-
-    @pl.when(first)
-    def _():
-        loads[2].wait()
-
-    produced = jnp.dot(active, down_here[...], preferred_element_type=jnp.float32)
-    for slot in range(CAPACITY):
-        for part in range(parts):
-            spread_ref[pl.ds(slot * parts + part, count, stride=per), :] = produced[
-                slot * count : (slot + 1) * count, part * LANES : (part + 1) * LANES
-            ]
-    out_ref[...] = spread_ref[...].astype(jnp.bfloat16)
-
-
-def expert_rows(received, gate_weights, up_weights, down_weights, steps):
+            move.start()
+            moves.append(move)
+    for move in moves:
+        move.wait()
+
+
+def expert_rows(received, gate_weights, up_weights, down_weights, blocks):
     rows = received.shape[0]
     width, units = gate_weights.shape
     slots = rows * LANES // width
-    block = pl.BlockSpec((rows // steps, LANES), lambda i: (i, 0))
     whole = pl.BlockSpec(memory_space=pl.ANY)
     weights = [
         pltpu.with_memory_space_constraint(weight, pltpu.HBM)
         for weight in (gate_weights, up_weights, down_weights)
     ]
     return pl.pallas_call(
-        expert_kernel,
-        grid=(steps,),
+        functools.partial(expert_kernel, blocks),
         out_shape=pltpu.HBM(received.shape, jnp.bfloat16),
-        in_specs=[block, whole, whole, whole],
-        out_specs=block,
+        in_specs=[pl.BlockSpec(memory_space=pltpu.VMEM), whole, whole, whole],
+        out_specs=whole,
         scratch_shapes=[
-            pltpu.VMEM((rows // steps, LANES), jnp.float32),
+            pltpu.VMEM((blocks, rows // blocks, LANES), jnp.float32),
+            pltpu.VMEM((blocks, rows // blocks, LANES), jnp.bfloat16),
             pltpu.VMEM(gate_weights.shape, jnp.bfloat16),
             pltpu.VMEM(up_weights.shape, jnp.bfloat16),
             pltpu.VMEM(down_weights.shape, jnp.bfloat16),
             pltpu.SemaphoreType.DMA((3,)),
+            pltpu.SemaphoreType.DMA((2 * blocks,)),
         ],
         compiler_params=pltpu.CompilerParams(vmem_limit_bytes=VMEM_BYTES),
         cost_estimate=pl.CostEstimate(
@@ -388,7 +424,7 @@
     produced = expert_rows(received, gate_weights[0], up_weights[0], down_weights[0], 4)
     returned = exchange(produced)
     expert_output = combine_rows(
-        picks, route_weights.T, returned, owner_count, context_size, width, 4
+        picks, route_weights.T, returned, owner_count, context_size, width, 1
     )
     _, attended = run_blocks(pieces, incoming_state)
     mixer_output = gated_norm(attended.reshape(out_gate.shape), norm_gain, out_gate)

time: 207 us -> 204 us (0.986)
  Pallas kernels: 18.9 us -> 15.5 us
    pallas_call x2, Pallas kernels: 15 us -> 12.5 us  [the longest x1 8.53 us: expert_rows(): pl.pallas_call(functools.partial(expert_kernel, blocks), out_shape=pltpu....]
where the time goes in v7:
time: 204 us; the launch traced here: 201 us
  waiting for transfers between devices  75.6 us (37%)
  starting transfers between devices  62.4 us (31%)
  matrix products  36.5 us (18%)
  Pallas kernels  15.5 us (8%)
  other arithmetic  6.17 us (3%)
  local copies, waits for them, and re-layouts  3.44 us (2%)
    all_to_all x2, waiting for transfers between devices, exchange(): lax.all_to_all(rows, ('exp', 'ctx'), split_axis=0, concat_axis=0, tiled=T...  65.7 us
    all_to_all x2, starting transfers between devices, exchange(): lax.all_to_all(rows, ('exp', 'ctx'), split_axis=0, concat_axis=0, tiled=T...  33.4 us
    ppermute x7, starting transfers between devices, passed_along(): return lax.ppermute(block, axis, route)  29 us
    ppermute x7, waiting for transfers between devices, passed_along(): return lax.ppermute(block, axis, route)  9.95 us
    pallas_call x1, Pallas kernels, expert_rows(): pl.pallas_call(functools.partial(expert_kernel, blocks), out_shape=pltpu....  8.53 us
    dot_general x4, matrix products, block_step(): jnp.einsum('sch,scv->shv', faded_keys, fresh_values, precision=TOP_PRECIS...  6.69 us
    dot_general x4, matrix products, block_step(): jnp.einsum('sij,sjv->siv', causal, fresh_values, precision=TOP_PRECISION)  6.18 us
    dot_general x4, matrix products, compose(): jnp.einsum('qfz,qze->qfe', segment_mapping, current_addend, precision=TOP...  4.33 us
  transfers between devices with their start and end apart: 9, of which 9 were waited for; matrix products, arithmetic and copies ran while one was open for 23% of the time, Pallas kernels for 0%

profile of v7, /device:TPU:1, one launch (start us, length us, event | category | flops | bytes accessed | tf_op | source)
XLA Modules:
  0.0 200.9 jit_solution(2341812344680641111)
XLA Ops:
  0.6 4.0 %pack_rows.1 = bf16[12288,128]{1,0:T(8,128)(2,1)} custom-call(s32[10,128]{1,0:T(8,128)} %bitcast.214, bf16[128,1024]{1,0:T(8,128)(2,1)} %hidden_ref.1), custom_call_target="tpu_custom_call" | custom-call | flops 402653184 | bytes 3145728 | tf_op jit(solution)/shard_map/pack_rows/pallas_call | solution.py:187
  4.7 22.2 %all-to-all-start = ((bf16[512,24,128]{2,1,0:T(8,128)(2,1)}), bf16[512,24,128]{2,1,0:T(8,128)(2,1)S(1)}, u32[]{:S(2)}, u32[]{:S(2)}) async-start(bf16[512,24,128]{2,1,0:T(8,128)(2,1)} %bitcast.217), calls=%async_computation | async-start | bytes 6291456 | tf_op jit(solution)/shard_map/all_to_all | solution.py:395
  29.4 1.3 fusion.43
  30.7 1.4 convolution_bitcast_fusion.2
  32.5 1.4 fusion.27
  33.9 8.8 %while.24 = (s32[]{:T(128)}, f32[1,128,128]{2,1,0:T(8,128)S(1)}, f32[1,128,128]{2,1,0:T(8,128)S(1)}, f32[4,1,128,128]{3,2,1,0:T(8,128)}, f32[4,1,128,128]{3,2,1,0:T(8,128)}, /*index=5*/s32[]{:T(128)}) while((s32[]{:T(128)}, f32[1,128,128]{2,1,0:T(8,128)S(1)}, f32[1,128,128]{2,1,0:T(8,128)S(1)}, f32[4,1,128,128]{3,2,1,0:T(8,128)}, ...), condition=%wide.region_2.3_spmd, body=%wide.region_1.2_spmd.sunk | while | flops 50348032 | bytes 722001 | solution.py:109
  33.9 1.0 convolution_bitcast_fusion.11
  34.9 1.1 fusion.99
  36.1 1.0 convolution_bitcast_fusion.11
  37.1 1.1 fusion.99
  38.3 1.0 convolution_bitcast_fusion.11
  39.3 1.1 fusion.99
  40.5 1.0 convolution_bitcast_fusion.11
  41.5 1.1 fusion.99
  42.8 3.5 %collective-permute-start = (bf16[1,128,128]{2,1,0:T(8,128)(2,1)S(1)}, bf16[1,128,128]{2,1,0:T(8,128)(2,1)S(1)}, u32[]{:S(2)}, u32[]{:S(2)}) collective-permute-start(bf16[1,128,128]{2,1,0:T(8,128)(2,1)S(1)} %fusion.42), channel_id=1, source_target_pairs={{0,64},{64,128},{128,192},{192,256},{256,320},{320,384},{384,448},... | collective-permute-start | bytes 98312 | tf_op jit(solution)/shard_map/ppermute | solution.py:20
  46.4 2.7 %collective-permute-done = bf16[1,128,128]{2,1,0:T(8,128)(2,1)S(1)} collective-permute-done((bf16[1,128,128]{2,1,0:T(8,128)(2,1)S(1)}, bf16[1,128,128]{2,1,0:T(8,128)(2,1)S(1)}, u32[]{:S(2)}, u32[]{:S(2)}) %collective-permute-start) | collective-permute-done | bytes 32800 | tf_op jit(solution)/shard_map/ppermute | solution.py:20
  49.3 2.6 %collective-permute-start.1 = (bf16[1,128,128]{2,1,0:T(8,128)(2,1)S(1)}, bf16[1,128,128]{2,1,0:T(8,128)(2,1)S(1)}, u32[]{:S(2)}, u32[]{:S(2)}) collective-permute-start(bf16[1,128,128]{2,1,0:T(8,128)(2,1)S(1)} %fusion.41), channel_id=1, source_target_pairs={{0,64},{64,128},{128,192},{192,256},{256,320},{320,384},{384,448},... | collective-permute-start | bytes 98312 | tf_op jit(solution)/shard_map/ppermute | solution.py:20
  51.9 1.3 collective-permute-done.1
  53.3 4.5 %collective-permute-start.2 = (bf16[1,128,128]{2,1,0:T(8,128)(2,1)S(1)}, bf16[1,128,128]{2,1,0:T(8,128)(2,1)S(1)}, u32[]{:S(2)}, u32[]{:S(2)}) collective-permute-start(bf16[1,128,128]{2,1,0:T(8,128)(2,1)S(1)} %fusion.40), channel_id=1, source_target_pairs={{0,64},{64,128},{128,192},{192,256},{256,320},{320,384},{384,448},... | collective-permute-start | bytes 98312 | tf_op jit(solution)/shard_map/ppermute | solution.py:20
  57.8 1.4 collective-permute-done.2
  59.3 4.5 %collective-permute-start.3 = (bf16[1,128,128]{2,1,0:T(8,128)(2,1)S(1)}, bf16[1,128,128]{2,1,0:T(8,128)(2,1)S(1)}, u32[]{:S(2)}, u32[]{:S(2)}) collective-permute-start(bf16[1,128,128]{2,1,0:T(8,128)(2,1)S(1)} %fusion.39), channel_id=1, source_target_pairs={{0,64},{64,128},{128,192},{192,256},{256,320},{320,384},{384,448},... | collective-permute-start | bytes 98312 | tf_op jit(solution)/shard_map/ppermute | solution.py:20
  63.9 1.0 collective-permute-done.3
  65.1 4.4 %collective-permute-start.4 = (bf16[1,128,128]{2,1,0:T(8,128)(2,1)S(1)}, bf16[1,128,128]{2,1,0:T(8,128)(2,1)S(1)}, u32[]{:S(2)}, u32[]{:S(2)}) collective-permute-start(bf16[1,128,128]{2,1,0:T(8,128)(2,1)S(1)} %fusion.38), channel_id=1, source_target_pairs={{0,64},{64,128},{128,192},{192,256},{256,320},{320,384},{384,448},... | collective-permute-start | bytes 98312 | tf_op jit(solution)/shard_map/ppermute | solution.py:20
  69.5 1.7 collective-permute-done.4
  71.4 4.6 %collective-permute-start.5 = (bf16[1,128,128]{2,1,0:T(8,128)(2,1)S(1)}, bf16[1,128,128]{2,1,0:T(8,128)(2,1)S(1)}, u32[]{:S(2)}, u32[]{:S(2)}) collective-permute-start(bf16[1,128,128]{2,1,0:T(8,128)(2,1)S(1)} %fusion.37), channel_id=1, source_target_pairs={{0,64},{64,128},{128,192},{192,256},{256,320},{320,384},{384,448},... | collective-permute-start | bytes 98312 | tf_op jit(solution)/shard_map/ppermute | solution.py:20
  76.0 1.0 collective-permute-done.5
  77.1 4.8 %collective-permute-start.6 = (bf16[1,128,128]{2,1,0:T(8,128)(2,1)S(1)}, bf16[1,128,128]{2,1,0:T(8,128)(2,1)S(1)}, u32[]{:S(2)}, u32[]{:S(2)}) collective-permute-start(bf16[1,128,128]{2,1,0:T(8,128)(2,1)S(1)} %fusion.36), channel_id=1, source_target_pairs={{0,64},{64,128},{128,192},{192,256},{256,320},{320,384},{384,448},... | collective-permute-start | bytes 98312 | tf_op jit(solution)/shard_map/ppermute | solution.py:20
  82.9 19.6 %all-to-all-done = bf16[512,24,128]{2,1,0:T(8,128)(2,1)S(1)} async-done(((bf16[512,24,128]{2,1,0:T(8,128)(2,1)}), bf16[512,24,128]{2,1,0:T(8,128)(2,1)S(1)}, u32[]{:S(2)}, u32[]{:S(2)}) %all-to-all-start) | async-done | bytes 3145760 | tf_op jit(solution)/shard_map/all_to_all | solution.py:395
  102.5 8.5 %expert_rows.1 = bf16[12288,128]{1,0:T(8,128)(2,1)} custom-call(bf16[12288,128]{1,0:T(8,128)(2,1)S(1)} %bitcast.213, bf16[1024,512]{1,0:T(8,128)(2,1)} %bitcast.232, bf16[1024,512]{1,0:T(8,128)(2,1)} %bitcast.233, bf16[512,1024]{1,0:T(8,128)(2,1)} %bitcast.234), custom_call_target="tpu_custom_call" | custom-call | flops 4831838208 | bytes 9437184 | tf_op jit(solution)/shard_map/expert_rows/pallas_call | solution.py:297
  111.0 11.3 %all-to-all-start.1 = ((bf16[512,24,128]{2,1,0:T(8,128)(2,1)}), bf16[512,24,128]{2,1,0:T(8,128)(2,1)S(1)}, u32[]{:S(2)}, u32[]{:S(2)}) async-start(bf16[512,24,128]{2,1,0:T(8,128)(2,1)} %bitcast.223), calls=%async_computation.1 | async-start | bytes 6291456 | tf_op jit(solution)/shard_map/all_to_all | solution.py:395
  122.4 1.9 fusion.28
  124.3 1.7 broadcast_multiply_fusion
  126.0 22.9 %while.25 = (s32[]{:T(128)}, f32[1,128,128]{2,1,0:T(8,128)S(1)}, f32[4,1,64,128]{3,2,1,0:T(8,128)}, f32[4,1,1]{0,2,1:T(1,128)S(1)}, f32[4,1,64,128]{3,2,1,0:T(8,...) while((s32[]{:T(128)}, f32[1,128,128]{2,1,0:T(8,128)S(1)}, ...), condition=%wide.region_4.5_spmd, body=%wide.region_3.4_spmd.sunk | while | flops 44089344 | bytes 625281 | solution.py:75
  126.9 1.0 convolution_subtract_fusion.3
  128.5 1.7 fusion.108
  130.2 1.5 fusion.110
  132.7 1.0 convolution_subtract_fusion.3
  134.2 1.7 fusion.108
  135.9 1.5 fusion.110
  140.0 1.7 fusion.108
  141.7 1.5 fusion.110
  144.1 1.0 convolution_subtract_fusion.3
  145.7 1.7 fusion.108
  147.4 1.5 fusion.110
  148.9 1.0 multiply_reduce_fusion
  150.1 1.7 multiply_multiply_fusion
  151.8 46.1 %all-to-all-done.1 = bf16[512,24,128]{2,1,0:T(8,128)(2,1)S(1)} async-done(((bf16[512,24,128]{2,1,0:T(8,128)(2,1)}), bf16[512,24,128]{2,1,0:T(8,128)(2,1)S(1)}, u32[]{:S(2)}, u32[]{:S(2)}) %all-to-all-start.1) | async-done | bytes 3145760 | tf_op jit(solution)/shard_map/all_to_all | solution.py:395
  197.9 3.0 %combine_rows.1 = bf16[128,1024]{1,0:T(8,128)(2,1)} custom-call(s32[10,128]{1,0:T(8,128)S(1)} %bitcast.215, f32[10,128]{1,0:T(8,128)S(1)} %bitcast.216, bf16[12288,128]{1,0:T(8,128)(2,1)S(1)} %bitcast.212), custom_call_target="tpu_custom_call" | custom-call | flops 805306368 | bytes 3145728 | tf_op jit(solution)/shard_map/combine_rows/pallas_call | solution.py:372
  (60 shorter events, 12.3 us)
Async XLA Ops:
  0.6 28.8 %copy-start = (f32[1,4,64,64]{3,2,1,0:T(8,128)S(1)}, f32[1,4,64,64]{3,2,1,0:T(8,128)}, u32[]{:S(2)}) copy-start(f32[1,4,64,64]{3,2,1,0:T(8,128)} %param.24) | copy-start | bytes 196612
  4.7 22.7 %copy-start.6 = (f32[1,256]{1,0:T(1,128)S(1)}, f32[1,256]{1,0:T(1,128)}, u32[]{:S(2)}) copy-start(f32[1,256]{1,0:T(1,128)} %param.23) | copy-start | bytes 3076
  4.7 23.5 %copy-start.7 = (f32[1,256]{1,0:T(1,128)S(1)}, f32[1,256]{1,0:T(1,128)}, u32[]{:S(2)}) copy-start(f32[1,256]{1,0:T(1,128)} %param.22) | copy-start | bytes 3076
  4.7 26.0 %copy-start.3 = (f32[1,256,128]{2,1,0:T(8,128)S(1)}, f32[1,256,128]{2,1,0:T(8,128)}, u32[]{:S(2)}) copy-start(f32[1,256,128]{2,1,0:T(8,128)} %param.19) | copy-start | bytes 393220
  4.7 97.8 %all-to-all-start = ((bf16[512,24,128]{2,1,0:T(8,128)(2,1)}), bf16[512,24,128]{2,1,0:T(8,128)(2,1)S(1)}, u32[]{:S(2)}, u32[]{:S(2)}) async-start(bf16[512,24,128]{2,1,0:T(8,128)(2,1)} %bitcast.217), calls=%async_computation | async-start | bytes 6291456 | tf_op jit(solution)/shard_map/all_to_all | solution.py:395
  30.7 1.8 copy-start.4
  32.4 1.4 copy-start.5
  42.8 6.3 %collective-permute-start = (bf16[1,128,128]{2,1,0:T(8,128)(2,1)S(1)}, bf16[1,128,128]{2,1,0:T(8,128)(2,1)S(1)}, u32[]{:S(2)}, u32[]{:S(2)}) collective-permute-start(bf16[1,128,128]{2,1,0:T(8,128)(2,1)S(1)} %fusion.42), channel_id=1, source_target_pairs={{0,64},{64,128},{128,192},{192,256},{256,320},{320,384},{384,448},... | collective-permute-start | bytes 98312 | tf_op jit(solution)/shard_map/ppermute | solution.py:20
  49.3 3.9 %collective-permute-start.1 = (bf16[1,128,128]{2,1,0:T(8,128)(2,1)S(1)}, bf16[1,128,128]{2,1,0:T(8,128)(2,1)S(1)}, u32[]{:S(2)}, u32[]{:S(2)}) collective-permute-start(bf16[1,128,128]{2,1,0:T(8,128)(2,1)S(1)} %fusion.41), channel_id=1, source_target_pairs={{0,64},{64,128},{128,192},{192,256},{256,320},{320,384},{384,448},... | collective-permute-start | bytes 98312 | tf_op jit(solution)/shard_map/ppermute | solution.py:20
  53.3 5.8 %collective-permute-start.2 = (bf16[1,128,128]{2,1,0:T(8,128)(2,1)S(1)}, bf16[1,128,128]{2,1,0:T(8,128)(2,1)S(1)}, u32[]{:S(2)}, u32[]{:S(2)}) collective-permute-start(bf16[1,128,128]{2,1,0:T(8,128)(2,1)S(1)} %fusion.40), channel_id=1, source_target_pairs={{0,64},{64,128},{128,192},{192,256},{256,320},{320,384},{384,448},... | collective-permute-start | bytes 98312 | tf_op jit(solution)/shard_map/ppermute | solution.py:20
  59.3 5.5 %collective-permute-start.3 = (bf16[1,128,128]{2,1,0:T(8,128)(2,1)S(1)}, bf16[1,128,128]{2,1,0:T(8,128)(2,1)S(1)}, u32[]{:S(2)}, u32[]{:S(2)}) collective-permute-start(bf16[1,128,128]{2,1,0:T(8,128)(2,1)S(1)} %fusion.39), channel_id=1, source_target_pairs={{0,64},{64,128},{128,192},{192,256},{256,320},{320,384},{384,448},... | collective-permute-start | bytes 98312 | tf_op jit(solution)/shard_map/ppermute | solution.py:20
  65.1 6.1 %collective-permute-start.4 = (bf16[1,128,128]{2,1,0:T(8,128)(2,1)S(1)}, bf16[1,128,128]{2,1,0:T(8,128)(2,1)S(1)}, u32[]{:S(2)}, u32[]{:S(2)}) collective-permute-start(bf16[1,128,128]{2,1,0:T(8,128)(2,1)S(1)} %fusion.38), channel_id=1, source_target_pairs={{0,64},{64,128},{128,192},{192,256},{256,320},{320,384},{384,448},... | collective-permute-start | bytes 98312 | tf_op jit(solution)/shard_map/ppermute | solution.py:20
  71.4 5.6 %collective-permute-start.5 = (bf16[1,128,128]{2,1,0:T(8,128)(2,1)S(1)}, bf16[1,128,128]{2,1,0:T(8,128)(2,1)S(1)}, u32[]{:S(2)}, u32[]{:S(2)}) collective-permute-start(bf16[1,128,128]{2,1,0:T(8,128)(2,1)S(1)} %fusion.37), channel_id=1, source_target_pairs={{0,64},{64,128},{128,192},{192,256},{256,320},{320,384},{384,448},... | collective-permute-start | bytes 98312 | tf_op jit(solution)/shard_map/ppermute | solution.py:20
  77.1 5.8 %collective-permute-start.6 = (bf16[1,128,128]{2,1,0:T(8,128)(2,1)S(1)}, bf16[1,128,128]{2,1,0:T(8,128)(2,1)S(1)}, u32[]{:S(2)}, u32[]{:S(2)}) collective-permute-start(bf16[1,128,128]{2,1,0:T(8,128)(2,1)S(1)} %fusion.36), channel_id=1, source_target_pairs={{0,64},{64,128},{128,192},{192,256},{256,320},{320,384},{384,448},... | collective-permute-start | bytes 98312 | tf_op jit(solution)/shard_map/ppermute | solution.py:20
  111.0 86.9 %all-to-all-start.1 = ((bf16[512,24,128]{2,1,0:T(8,128)(2,1)}), bf16[512,24,128]{2,1,0:T(8,128)(2,1)S(1)}, u32[]{:S(2)}, u32[]{:S(2)}) async-start(bf16[512,24,128]{2,1,0:T(8,128)(2,1)} %bitcast.223), calls=%async_computation.1 | async-start | bytes 6291456 | tf_op jit(solution)/shard_map/all_to_all | solution.py:395
  122.3 27.7 %copy-start.8 = (f32[128]{0:T(128)S(1)}, f32[128]{0:T(128)}, u32[]{:S(2)}) copy-start(f32[128]{0:T(128)} %param.25) | copy-start | bytes 1540
  122.3 75.6 %copy-start.1 = (s32[128,10]{0,1:T(8,128)S(1)}, s32[128,10]{0,1:T(8,128)}, u32[]{:S(2)}) copy-start(s32[128,10]{0,1:T(8,128)} %param.27) | copy-start | bytes 15364
  122.3 75.6 %copy-start.2 = (f32[128,10]{0,1:T(8,128)S(1)}, f32[128,10]{0,1:T(8,128)}, u32[]{:S(2)}) copy-start(f32[128,10]{0,1:T(8,128)} %param.28) | copy-start | bytes 15364

commit v8 on v7

--- a/solution.py
+++ b/solution.py
@@ -205,19 +205,43 @@
     )
 
 
+def staging_kernel(*refs):
+    count = len(refs) // 2
+    ready = refs[-1]
+    moves = [
+        pltpu.make_async_copy(refs[i], refs[count + i], ready.at[i]) for i in range(count)
+    ]
+    for move in moves:
+        move.start()
+    for move in moves:
+        move.wait()
+
+
+def staged(arrays):
+    there = pl.BlockSpec(memory_space=pl.ANY)
+    here = pl.BlockSpec(memory_space=pltpu.VMEM)
+    return pl.pallas_call(
+        staging_kernel,
+        out_shape=[pltpu.VMEM(array.shape, array.dtype) for array in arrays],
+        in_specs=[there] * len(arrays),
+        out_specs=[here] * len(arrays),
+        scratch_shapes=[pltpu.SemaphoreType.DMA((len(arrays),))],
+        cost_estimate=pl.CostEstimate(
+            flops=0, bytes_accessed=4 * sum(array.size for array in arrays), transcendentals=0
+        ),
+        name="staged_weights",
+    )(*[pltpu.with_memory_space_constraint(array, pltpu.HBM) for array in arrays])
+
+
 def expert_kernel(
     blocks,
     received_ref,
-    gate_ref,
-    up_ref,
-    down_ref,
+    gate_here,
+    up_here,
+    down_here,
     out_ref,
     spread_ref,
     result_ref,
-    gate_here,
-    up_here,
-    down_here,
-    ready,
     sent,
 ):
     width = gate_here.shape[0]
@@ -225,15 +249,6 @@
     per = CAPACITY * parts
     block = received_ref.shape[0] // blocks
     count = block // per
-    loads = [
-        pltpu.make_async_copy(there, here, ready.at[i])
-        for i, (there, here) in enumerate(
-            ((gate_ref, gate_here), (up_ref, up_here), (down_ref, down_here))
-        )
-    ]
-    for load in loads:
-        load.start()
-
     def unpacked(i):
         spread_ref[i] = received_ref[pl.ds(i * block, block), :].astype(jnp.float32)
         return jnp.concatenate(
@@ -255,12 +270,7 @@
     rows = unpacked(0)
     moves = []
     for i in range(blocks):
-        if i == 0:
-            loads[0].wait()
         gate = jnp.dot(rows, gate_here[...], preferred_element_type=jnp.float32)
-        if i == 0:
-            loads[1].wait()
-            loads[2].wait()
         up = jnp.dot(rows, up_here[...], preferred_element_type=jnp.float32)
         if i + 1 < blocks:
             rows = unpacked(i + 1)
@@ -290,22 +300,15 @@
     width, units = gate_weights.shape
     slots = rows * LANES // width
     whole = pl.BlockSpec(memory_space=pl.ANY)
-    weights = [
-        pltpu.with_memory_space_constraint(weight, pltpu.HBM)
-        for weight in (gate_weights, up_weights, down_weights)
-    ]
+    here = pl.BlockSpec(memory_space=pltpu.VMEM)
     return pl.pallas_call(
         functools.partial(expert_kernel, blocks),
         out_shape=pltpu.HBM(received.shape, jnp.bfloat16),
-        in_specs=[pl.BlockSpec(memory_space=pltpu.VMEM), whole, whole, whole],
+        in_specs=[here] * 4,
         out_specs=whole,
         scratch_shapes=[
             pltpu.VMEM((blocks, rows // blocks, LANES), jnp.float32),
             pltpu.VMEM((blocks, rows // blocks, LANES), jnp.bfloat16),
-            pltpu.VMEM(gate_weights.shape, jnp.bfloat16),
-            pltpu.VMEM(up_weights.shape, jnp.bfloat16),
-            pltpu.VMEM(down_weights.shape, jnp.bfloat16),
-            pltpu.SemaphoreType.DMA((3,)),
             pltpu.SemaphoreType.DMA((2 * blocks,)),
         ],
         compiler_params=pltpu.CompilerParams(vmem_limit_bytes=VMEM_BYTES),
@@ -315,7 +318,7 @@
             transcendentals=slots * units,
         ),
         name="expert_rows",
-    )(received, *weights)
+    )(received, gate_weights, up_weights, down_weights)
 
 
 def combine_kernel(owner_count, context_size, picks_ref, weights_ref, returned_ref, out_ref, spread_ref, total_ref):
@@ -420,8 +423,11 @@
     pieces, incoming_state = delta_front(
         queries, key_vectors, values, write_strength, log_fading_factor, block_inverse
     )
-    received, incoming_state = lax.optimization_barrier((received, incoming_state))
-    produced = expert_rows(received, gate_weights[0], up_weights[0], down_weights[0], 4)
+    weights = staged([gate_weights[0], up_weights[0], down_weights[0]])
+    received, incoming_state, weights = lax.optimization_barrier(
+        (received, incoming_state, weights)
+    )
+    produced = expert_rows(received, *weights, 4)
     returned = exchange(produced)
     expert_output = combine_rows(
         picks, route_weights.T, returned, owner_count, context_size, width, 1

time: 204 us -> 204 us (level)
  matrix products: 36.5 us -> 27 us
  waiting for transfers between devices: 75.6 us -> 80.9 us
  starting transfers between devices: 62.4 us -> 65 us
  Pallas kernels: 15.5 us -> 17.9 us
    all_to_all x2, waiting for transfers between devices: 65.7 us -> 72.7 us  [exchange(): lax.all_to_all(rows, ('exp', 'ctx'), split_axis=0, concat_axis=0, tiled=T...]
    dot_general x4, matrix products: 4.33 us -> 0.83 us  [compose(): jnp.einsum('qfz,qze->qfe', segment_mapping, current_addend, precision=TOP...]
    dot_general x4, matrix products: 4.19 us -> 0.82 us  [compose(): jnp.einsum('qfz,qze->qfe', segment_mapping, current_mapping, precision=TO...]
  transfers between devices with their start and end apart: 9 -> 9, of which waited for: 9 -> 8; matrix products, arithmetic and copies ran while one was open for 23% -> 18% of each run, Pallas kernels for 0% -> 1%
where the time goes in v8:
time: 204 us; the launch traced here: 202 us
  waiting for transfers between devices  80.9 us (40%)
  starting transfers between devices  65 us (32%)
  matrix products  27 us (13%)
  Pallas kernels  17.9 us (9%)
  other arithmetic  6.18 us (3%)
  local copies, waits for them, and re-layouts  3.25 us (2%)
    all_to_all x2, waiting for transfers between devices, exchange(): lax.all_to_all(rows, ('exp', 'ctx'), split_axis=0, concat_axis=0, tiled=T...  72.7 us
    all_to_all x2, starting transfers between devices, exchange(): lax.all_to_all(rows, ('exp', 'ctx'), split_axis=0, concat_axis=0, tiled=T...  35.2 us
    ppermute x7, starting transfers between devices, passed_along(): return lax.ppermute(block, axis, route)  29.8 us
    pallas_call x1, Pallas kernels, expert_rows(): pl.pallas_call(functools.partial(expert_kernel, blocks), out_shape=pltpu....  9.07 us
    ppermute x7, waiting for transfers between devices, passed_along(): return lax.ppermute(block, axis, route)  8.12 us
    dot_general x4, matrix products, block_step(): jnp.einsum('sch,scv->shv', faded_keys, fresh_values, precision=TOP_PRECIS...  6.41 us
    dot_general x4, matrix products, block_step(): jnp.einsum('sij,sjv->siv', causal, fresh_values, precision=TOP_PRECISION)  6.18 us
  transfers between devices with their start and end apart: 9, of which 8 were waited for; matrix products, arithmetic and copies ran while one was open for 18% of the time, Pallas kernels for 1%

profile of v8, /device:TPU:1, one launch (start us, length us, event | category | flops | bytes accessed | tf_op | source)
XLA Modules:
  0.0 201.5 jit_solution(14616138402899435773)
XLA Ops:
  0.6 4.0 %pack_rows.1 = bf16[12288,128]{1,0:T(8,128)(2,1)} custom-call(s32[10,128]{1,0:T(8,128)} %bitcast.213, bf16[128,1024]{1,0:T(8,128)(2,1)} %hidden_ref.1), custom_call_target="tpu_custom_call" | custom-call | flops 402653184 | bytes 3145728 | tf_op jit(solution)/shard_map/pack_rows/pallas_call | solution.py:187
  4.7 24.0 %all-to-all-start = ((bf16[512,24,128]{2,1,0:T(8,128)(2,1)}), bf16[512,24,128]{2,1,0:T(8,128)(2,1)}, u32[]{:S(2)}, u32[]{:S(2)}) async-start(bf16[512,24,128]{2,1,0:T(8,128)(2,1)} %bitcast.216), calls=%async_computation | async-start | bytes 6291456 | tf_op jit(solution)/shard_map/all_to_all | solution.py:398
  29.2 0.7 reduce.13
  29.9 0.7 reduce.14
  31.6 0.7 convolution_bitcast_fusion.2
  32.7 0.7 fusion.27
  33.4 1.9 while.24
  35.5 3.5 %collective-permute-start = (bf16[1,128,128]{2,1,0:T(8,128)(2,1)S(1)}, bf16[1,128,128]{2,1,0:T(8,128)(2,1)S(1)}, u32[]{:S(2)}, u32[]{:S(2)}) collective-permute-start(bf16[1,128,128]{2,1,0:T(8,128)(2,1)S(1)} %fusion.42), channel_id=1, source_target_pairs={{0,64},{64,128},{128,192},{192,256},{256,320},{320,384},{384,448},... | collective-permute-start | bytes 98312 | tf_op jit(solution)/shard_map/ppermute | solution.py:20
  39.0 2.8 %collective-permute-done = bf16[1,128,128]{2,1,0:T(8,128)(2,1)S(1)} collective-permute-done((bf16[1,128,128]{2,1,0:T(8,128)(2,1)S(1)}, bf16[1,128,128]{2,1,0:T(8,128)(2,1)S(1)}, u32[]{:S(2)}, u32[]{:S(2)}) %collective-permute-start) | collective-permute-done | bytes 32800 | tf_op jit(solution)/shard_map/ppermute | solution.py:20
  42.0 3.1 %collective-permute-start.1 = (bf16[1,128,128]{2,1,0:T(8,128)(2,1)S(1)}, bf16[1,128,128]{2,1,0:T(8,128)(2,1)S(1)}, u32[]{:S(2)}, u32[]{:S(2)}) collective-permute-start(bf16[1,128,128]{2,1,0:T(8,128)(2,1)S(1)} %fusion.41), channel_id=1, source_target_pairs={{0,64},{64,128},{128,192},{192,256},{256,320},{320,384},{384,448},... | collective-permute-start | bytes 98312 | tf_op jit(solution)/shard_map/ppermute | solution.py:20
  45.1 1.0 collective-permute-done.1
  46.3 4.8 %collective-permute-start.2 = (bf16[1,128,128]{2,1,0:T(8,128)(2,1)S(1)}, bf16[1,128,128]{2,1,0:T(8,128)(2,1)S(1)}, u32[]{:S(2)}, u32[]{:S(2)}) collective-permute-start(bf16[1,128,128]{2,1,0:T(8,128)(2,1)S(1)} %fusion.40), channel_id=1, source_target_pairs={{0,64},{64,128},{128,192},{192,256},{256,320},{320,384},{384,448},... | collective-permute-start | bytes 98312 | tf_op jit(solution)/shard_map/ppermute | solution.py:20
  51.1 1.1 collective-permute-done.2
  52.3 4.4 %collective-permute-start.3 = (bf16[1,128,128]{2,1,0:T(8,128)(2,1)S(1)}, bf16[1,128,128]{2,1,0:T(8,128)(2,1)S(1)}, u32[]{:S(2)}, u32[]{:S(2)}) collective-permute-start(bf16[1,128,128]{2,1,0:T(8,128)(2,1)S(1)} %fusion.39), channel_id=1, source_target_pairs={{0,64},{64,128},{128,192},{192,256},{256,320},{320,384},{384,448},... | collective-permute-start | bytes 98312 | tf_op jit(solution)/shard_map/ppermute | solution.py:20
  56.8 1.0 collective-permute-done.3
  58.0 4.5 %collective-permute-start.4 = (bf16[1,128,128]{2,1,0:T(8,128)(2,1)S(1)}, bf16[1,128,128]{2,1,0:T(8,128)(2,1)S(1)}, u32[]{:S(2)}, u32[]{:S(2)}) collective-permute-start(bf16[1,128,128]{2,1,0:T(8,128)(2,1)S(1)} %fusion.38), channel_id=1, source_target_pairs={{0,64},{64,128},{128,192},{192,256},{256,320},{320,384},{384,448},... | collective-permute-start | bytes 98312 | tf_op jit(solution)/shard_map/ppermute | solution.py:20
  62.5 1.3 collective-permute-done.4
  63.9 4.4 %collective-permute-start.5 = (bf16[1,128,128]{2,1,0:T(8,128)(2,1)S(1)}, bf16[1,128,128]{2,1,0:T(8,128)(2,1)S(1)}, u32[]{:S(2)}, u32[]{:S(2)}) collective-permute-start(bf16[1,128,128]{2,1,0:T(8,128)(2,1)S(1)} %fusion.37), channel_id=1, source_target_pairs={{0,64},{64,128},{128,192},{192,256},{256,320},{320,384},{384,448},... | collective-permute-start | bytes 98312 | tf_op jit(solution)/shard_map/ppermute | solution.py:20
  68.4 1.0 collective-permute-done.5
  69.5 4.9 %collective-permute-start.6 = (bf16[1,128,128]{2,1,0:T(8,128)(2,1)S(1)}, bf16[1,128,128]{2,1,0:T(8,128)(2,1)S(1)}, u32[]{:S(2)}, u32[]{:S(2)}) collective-permute-start(bf16[1,128,128]{2,1,0:T(8,128)(2,1)S(1)} %fusion.36), channel_id=1, source_target_pairs={{0,64},{64,128},{128,192},{192,256},{256,320},{320,384},{384,448},... | collective-permute-start | bytes 98312 | tf_op jit(solution)/shard_map/ppermute | solution.py:20
  74.5 1.9 staged_weights.1
  76.4 26.2 %all-to-all-done = bf16[512,24,128]{2,1,0:T(8,128)(2,1)} async-done(((bf16[512,24,128]{2,1,0:T(8,128)(2,1)}), bf16[512,24,128]{2,1,0:T(8,128)(2,1)}, u32[]{:S(2)}, u32[]{:S(2)}) %all-to-all-start) | async-done | bytes 3145760 | tf_op jit(solution)/shard_map/all_to_all | solution.py:398
  102.6 9.1 %expert_rows.1 = bf16[12288,128]{1,0:T(8,128)(2,1)} custom-call(bf16[12288,128]{1,0:T(8,128)(2,1)} %bitcast.17.received_ref, bf16[1024,512]{1,0:T(8,128)(2,1)S(1)} %get-tuple-element.93.gate_here, bf16[1024,512]{1,0:T(8,128)(2,1)S(1)} %get-tuple-element.94.up_here, bf16[512,1024]{1,0:T(8,128)(2,1)S(1)} %get-tuple-element.95.down_here), custom_call_target="tpu_custom_call" | custom-call | flops 4831838208 | bytes 9437184 | tf_op jit(solution)/shard_map/expert_rows/pallas_call | solution.py:304
  111.7 11.3 %all-to-all-start.1 = ((bf16[512,24,128]{2,1,0:T(8,128)(2,1)}), bf16[512,24,128]{2,1,0:T(8,128)(2,1)S(1)}, u32[]{:S(2)}, u32[]{:S(2)}) async-start(bf16[512,24,128]{2,1,0:T(8,128)(2,1)} %bitcast.222), calls=%async_computation.1 | async-start | bytes 6291456 | tf_op jit(solution)/shard_map/all_to_all | solution.py:398
  123.0 1.9 fusion.28
  124.9 1.7 broadcast_multiply_fusion
  126.6 22.5 %while.25 = (s32[]{:T(128)}, f32[1,128,128]{2,1,0:T(8,128)S(1)}, f32[4,1,64,128]{3,2,1,0:T(8,128)}, f32[4,1,1]{0,2,1:T(1,128)S(1)}, f32[4,1,64,128]{3,2,1,0:T(8,...) while((s32[]{:T(128)}, f32[1,128,128]{2,1,0:T(8,128)S(1)}, ...), condition=%wide.region_4.5_spmd, body=%wide.region_3.4_spmd.sunk | while | flops 44089344 | bytes 625281 | solution.py:75
  127.2 1.0 convolution_subtract_fusion.3
  128.2 0.9 fusion.109
  129.1 1.6 fusion.108
  130.7 1.5 fusion.110
  132.8 1.0 convolution_subtract_fusion.3
  133.8 0.9 fusion.109
  134.7 1.6 fusion.108
  136.3 1.5 fusion.110
  138.4 1.0 convolution_subtract_fusion.3
  139.4 0.9 fusion.109
  140.3 1.6 fusion.108
  142.0 1.5 fusion.110
  143.5 0.5 constant_dynamic-slice_fusion.2
  144.0 1.0 convolution_subtract_fusion.3
  145.0 0.9 fusion.109
  146.0 1.6 fusion.108
  147.6 1.5 fusion.110
  149.1 1.0 multiply_reduce_fusion
  150.2 1.7 multiply_multiply_fusion
  152.0 46.6 %all-to-all-done.1 = bf16[512,24,128]{2,1,0:T(8,128)(2,1)S(1)} async-done(((bf16[512,24,128]{2,1,0:T(8,128)(2,1)}), bf16[512,24,128]{2,1,0:T(8,128)(2,1)S(1)}, u32[]{:S(2)}, u32[]{:S(2)}) %all-to-all-start.1) | async-done | bytes 3145760 | tf_op jit(solution)/shard_map/all_to_all | solution.py:398
  198.6 3.0 %combine_rows.1 = bf16[128,1024]{1,0:T(8,128)(2,1)} custom-call(s32[10,128]{1,0:T(8,128)S(1)} %bitcast.214, f32[10,128]{1,0:T(8,128)S(1)} %bitcast.215, bf16[12288,128]{1,0:T(8,128)(2,1)S(1)} %bitcast.212), custom_call_target="tpu_custom_call" | custom-call | flops 805306368 | bytes 3145728 | tf_op jit(solution)/shard_map/combine_rows/pallas_call | solution.py:375
  (63 shorter events, 6.7 us)
Async XLA Ops:
  0.6 30.6 %copy-start = (f32[1,4,64,64]{3,2,1,0:T(8,128)S(1)}, f32[1,4,64,64]{3,2,1,0:T(8,128)}, u32[]{:S(2)}) copy-start(f32[1,4,64,64]{3,2,1,0:T(8,128)} %param.24) | copy-start | bytes 196612
  4.7 24.6 %copy-start.7 = (f32[1,256]{1,0:T(1,128)S(1)}, f32[1,256]{1,0:T(1,128)}, u32[]{:S(2)}) copy-start(f32[1,256]{1,0:T(1,128)} %param.22) | copy-start | bytes 3076
  4.7 25.2 %copy-start.8 = (f32[1,256]{1,0:T(1,128)S(1)}, f32[1,256]{1,0:T(1,128)}, u32[]{:S(2)}) copy-start(f32[1,256]{1,0:T(1,128)} %param.23) | copy-start | bytes 3076
  4.7 26.6 %copy-start.6 = (f32[1,256,128]{2,1,0:T(8,128)S(1)}, f32[1,256,128]{2,1,0:T(8,128)}, u32[]{:S(2)}) copy-start(f32[1,256,128]{2,1,0:T(8,128)} %param.20) | copy-start | bytes 393220
  4.7 26.9 %copy-start.3 = (f32[1,256,128]{2,1,0:T(8,128)S(1)}, f32[1,256,128]{2,1,0:T(8,128)}, u32[]{:S(2)}) copy-start(f32[1,256,128]{2,1,0:T(8,128)} %param.19) | copy-start | bytes 393220
  4.7 97.9 %all-to-all-start = ((bf16[512,24,128]{2,1,0:T(8,128)(2,1)}), bf16[512,24,128]{2,1,0:T(8,128)(2,1)}, u32[]{:S(2)}, u32[]{:S(2)}) async-start(bf16[512,24,128]{2,1,0:T(8,128)(2,1)} %bitcast.216), calls=%async_computation | async-start | bytes 6291456 | tf_op jit(solution)/shard_map/all_to_all | solution.py:398
  31.6 1.1 copy-start.4
  32.7 0.7 copy-start.5
  35.5 6.3 %collective-permute-start = (bf16[1,128,128]{2,1,0:T(8,128)(2,1)S(1)}, bf16[1,128,128]{2,1,0:T(8,128)(2,1)S(1)}, u32[]{:S(2)}, u32[]{:S(2)}) collective-permute-start(bf16[1,128,128]{2,1,0:T(8,128)(2,1)S(1)} %fusion.42), channel_id=1, source_target_pairs={{0,64},{64,128},{128,192},{192,256},{256,320},{320,384},{384,448},... | collective-permute-start | bytes 98312 | tf_op jit(solution)/shard_map/ppermute | solution.py:20
  42.0 4.1 %collective-permute-start.1 = (bf16[1,128,128]{2,1,0:T(8,128)(2,1)S(1)}, bf16[1,128,128]{2,1,0:T(8,128)(2,1)S(1)}, u32[]{:S(2)}, u32[]{:S(2)}) collective-permute-start(bf16[1,128,128]{2,1,0:T(8,128)(2,1)S(1)} %fusion.41), channel_id=1, source_target_pairs={{0,64},{64,128},{128,192},{192,256},{256,320},{320,384},{384,448},... | collective-permute-start | bytes 98312 | tf_op jit(solution)/shard_map/ppermute | solution.py:20
  46.3 5.9 %collective-permute-start.2 = (bf16[1,128,128]{2,1,0:T(8,128)(2,1)S(1)}, bf16[1,128,128]{2,1,0:T(8,128)(2,1)S(1)}, u32[]{:S(2)}, u32[]{:S(2)}) collective-permute-start(bf16[1,128,128]{2,1,0:T(8,128)(2,1)S(1)} %fusion.40), channel_id=1, source_target_pairs={{0,64},{64,128},{128,192},{192,256},{256,320},{320,384},{384,448},... | collective-permute-start | bytes 98312 | tf_op jit(solution)/shard_map/ppermute | solution.py:20
  52.3 5.4 %collective-permute-start.3 = (bf16[1,128,128]{2,1,0:T(8,128)(2,1)S(1)}, bf16[1,128,128]{2,1,0:T(8,128)(2,1)S(1)}, u32[]{:S(2)}, u32[]{:S(2)}) collective-permute-start(bf16[1,128,128]{2,1,0:T(8,128)(2,1)S(1)} %fusion.39), channel_id=1, source_target_pairs={{0,64},{64,128},{128,192},{192,256},{256,320},{320,384},{384,448},... | collective-permute-start | bytes 98312 | tf_op jit(solution)/shard_map/ppermute | solution.py:20
  58.0 5.8 %collective-permute-start.4 = (bf16[1,128,128]{2,1,0:T(8,128)(2,1)S(1)}, bf16[1,128,128]{2,1,0:T(8,128)(2,1)S(1)}, u32[]{:S(2)}, u32[]{:S(2)}) collective-permute-start(bf16[1,128,128]{2,1,0:T(8,128)(2,1)S(1)} %fusion.38), channel_id=1, source_target_pairs={{0,64},{64,128},{128,192},{192,256},{256,320},{320,384},{384,448},... | collective-permute-start | bytes 98312 | tf_op jit(solution)/shard_map/ppermute | solution.py:20
  63.9 5.5 %collective-permute-start.5 = (bf16[1,128,128]{2,1,0:T(8,128)(2,1)S(1)}, bf16[1,128,128]{2,1,0:T(8,128)(2,1)S(1)}, u32[]{:S(2)}, u32[]{:S(2)}) collective-permute-start(bf16[1,128,128]{2,1,0:T(8,128)(2,1)S(1)} %fusion.37), channel_id=1, source_target_pairs={{0,64},{64,128},{128,192},{192,256},{256,320},{320,384},{384,448},... | collective-permute-start | bytes 98312 | tf_op jit(solution)/shard_map/ppermute | solution.py:20
  69.5 6.9 %collective-permute-start.6 = (bf16[1,128,128]{2,1,0:T(8,128)(2,1)S(1)}, bf16[1,128,128]{2,1,0:T(8,128)(2,1)S(1)}, u32[]{:S(2)}, u32[]{:S(2)}) collective-permute-start(bf16[1,128,128]{2,1,0:T(8,128)(2,1)S(1)} %fusion.36), channel_id=1, source_target_pairs={{0,64},{64,128},{128,192},{192,256},{256,320},{320,384},{384,448},... | collective-permute-start | bytes 98312 | tf_op jit(solution)/shard_map/ppermute | solution.py:20
  111.7 86.9 %all-to-all-start.1 = ((bf16[512,24,128]{2,1,0:T(8,128)(2,1)}), bf16[512,24,128]{2,1,0:T(8,128)(2,1)S(1)}, u32[]{:S(2)}, u32[]{:S(2)}) async-start(bf16[512,24,128]{2,1,0:T(8,128)(2,1)} %bitcast.222), calls=%async_computation.1 | async-start | bytes 6291456 | tf_op jit(solution)/shard_map/all_to_all | solution.py:398
  122.9 27.3 %copy-start.9 = (f32[128]{0:T(128)S(1)}, f32[128]{0:T(128)}, u32[]{:S(2)}) copy-start(f32[128]{0:T(128)} %param.25) | copy-start | bytes 1540
  123.0 75.6 %copy-start.1 = (s32[128,10]{0,1:T(8,128)S(1)}, s32[128,10]{0,1:T(8,128)}, u32[]{:S(2)}) copy-start(s32[128,10]{0,1:T(8,128)} %param.27) | copy-start | bytes 15364
  123.0 75.6 %copy-start.2 = (f32[128,10]{0,1:T(8,128)S(1)}, f32[128,10]{0,1:T(8,128)}, u32[]{:S(2)}) copy-start(f32[128,10]{0,1:T(8,128)} %param.28) | copy-start | bytes 15364

commit v9 on v8

--- a/solution.py
+++ b/solution.py
@@ -235,22 +235,33 @@
 
 def expert_kernel(
     blocks,
-    received_ref,
+    received_there,
     gate_here,
     up_here,
     down_here,
     out_ref,
+    received_ref,
     spread_ref,
     result_ref,
+    ready,
     sent,
 ):
     width = gate_here.shape[0]
     parts = width // LANES
     per = CAPACITY * parts
-    block = received_ref.shape[0] // blocks
+    block = received_ref.shape[1]
     count = block // per
+    loads = [
+        pltpu.make_async_copy(
+            received_there.at[pl.ds(i * block, block), :], received_ref.at[i], ready.at[i]
+        )
+        for i in range(blocks)
+    ]
+    for load in loads:
+        load.start()
     def unpacked(i):
-        spread_ref[i] = received_ref[pl.ds(i * block, block), :].astype(jnp.float32)
+        loads[i].wait()
+        spread_ref[i] = received_ref[i].astype(jnp.float32)
         return jnp.concatenate(
             [
                 jnp.concatenate(
@@ -304,11 +315,13 @@
     return pl.pallas_call(
         functools.partial(expert_kernel, blocks),
         out_shape=pltpu.HBM(received.shape, jnp.bfloat16),
-        in_specs=[here] * 4,
+        in_specs=[whole, here, here, here],
         out_specs=whole,
         scratch_shapes=[
+            pltpu.VMEM((blocks, rows // blocks, LANES), jnp.bfloat16),
             pltpu.VMEM((blocks, rows // blocks, LANES), jnp.float32),
             pltpu.VMEM((blocks, rows // blocks, LANES), jnp.bfloat16),
+            pltpu.SemaphoreType.DMA((blocks,)),
             pltpu.SemaphoreType.DMA((2 * blocks,)),
         ],
         compiler_params=pltpu.CompilerParams(vmem_limit_bytes=VMEM_BYTES),

time: 204 us -> 204 us (level)
  no operation moved by 1% of the time
where the time goes in v9:
time: 204 us; the launch traced here: 201 us
  waiting for transfers between devices  80.9 us (40%)
  starting transfers between devices  65 us (32%)
  matrix products  27 us (13%)
  Pallas kernels  17.6 us (9%)
  other arithmetic  6.18 us (3%)
  local copies, waits for them, and re-layouts  3.25 us (2%)
    all_to_all x2, waiting for transfers between devices, exchange(): lax.all_to_all(rows, ('exp', 'ctx'), split_axis=0, concat_axis=0, tiled=T...  72.7 us
    all_to_all x2, starting transfers between devices, exchange(): lax.all_to_all(rows, ('exp', 'ctx'), split_axis=0, concat_axis=0, tiled=T...  35.3 us
    ppermute x7, starting transfers between devices, passed_along(): return lax.ppermute(block, axis, route)  29.8 us
    pallas_call x1, Pallas kernels, expert_rows(): pl.pallas_call(functools.partial(expert_kernel, blocks), out_shape=pltpu....  8.7 us
    ppermute x7, waiting for transfers between devices, passed_along(): return lax.ppermute(block, axis, route)  8.12 us
    dot_general x4, matrix products, block_step(): jnp.einsum('sch,scv->shv', faded_keys, fresh_values, precision=TOP_PRECIS...  6.41 us
    dot_general x4, matrix products, block_step(): jnp.einsum('sij,sjv->siv', causal, fresh_values, precision=TOP_PRECISION)  6.17 us
  transfers between devices with their start and end apart: 9, of which 8 were waited for; matrix products, arithmetic and copies ran while one was open for 18% of the time, Pallas kernels for 1%

profile of v9, /device:TPU:1, one launch (start us, length us, event | category | flops | bytes accessed | tf_op | source)
XLA Modules:
  0.0 201.2 jit_solution(11458961037214338233)
XLA Ops:
  0.6 4.0 %pack_rows.1 = bf16[12288,128]{1,0:T(8,128)(2,1)} custom-call(s32[10,128]{1,0:T(8,128)} %bitcast.213, bf16[128,1024]{1,0:T(8,128)(2,1)} %hidden_ref.1), custom_call_target="tpu_custom_call" | custom-call | flops 402653184 | bytes 3145728 | tf_op jit(solution)/shard_map/pack_rows/pallas_call | solution.py:187
  4.7 24.0 %all-to-all-start = ((bf16[512,24,128]{2,1,0:T(8,128)(2,1)}), bf16[512,24,128]{2,1,0:T(8,128)(2,1)}, u32[]{:S(2)}, u32[]{:S(2)}) async-start(bf16[512,24,128]{2,1,0:T(8,128)(2,1)} %bitcast.216), calls=%async_computation | async-start | bytes 6291456 | tf_op jit(solution)/shard_map/all_to_all | solution.py:411
  29.2 0.7 reduce.13
  29.9 0.7 reduce.14
  31.6 0.7 convolution_bitcast_fusion.2
  32.7 0.7 fusion.27
  33.4 1.9 while.24
  35.5 3.5 %collective-permute-start = (bf16[1,128,128]{2,1,0:T(8,128)(2,1)S(1)}, bf16[1,128,128]{2,1,0:T(8,128)(2,1)S(1)}, u32[]{:S(2)}, u32[]{:S(2)}) collective-permute-start(bf16[1,128,128]{2,1,0:T(8,128)(2,1)S(1)} %fusion.42), channel_id=1, source_target_pairs={{0,64},{64,128},{128,192},{192,256},{256,320},{320,384},{384,448},... | collective-permute-start | bytes 98312 | tf_op jit(solution)/shard_map/ppermute | solution.py:20
  39.0 2.8 %collective-permute-done = bf16[1,128,128]{2,1,0:T(8,128)(2,1)S(1)} collective-permute-done((bf16[1,128,128]{2,1,0:T(8,128)(2,1)S(1)}, bf16[1,128,128]{2,1,0:T(8,128)(2,1)S(1)}, u32[]{:S(2)}, u32[]{:S(2)}) %collective-permute-start) | collective-permute-done | bytes 32800 | tf_op jit(solution)/shard_map/ppermute | solution.py:20
  42.0 3.1 %collective-permute-start.1 = (bf16[1,128,128]{2,1,0:T(8,128)(2,1)S(1)}, bf16[1,128,128]{2,1,0:T(8,128)(2,1)S(1)}, u32[]{:S(2)}, u32[]{:S(2)}) collective-permute-start(bf16[1,128,128]{2,1,0:T(8,128)(2,1)S(1)} %fusion.41), channel_id=1, source_target_pairs={{0,64},{64,128},{128,192},{192,256},{256,320},{320,384},{384,448},... | collective-permute-start | bytes 98312 | tf_op jit(solution)/shard_map/ppermute | solution.py:20
  45.1 1.0 collective-permute-done.1
  46.3 4.8 %collective-permute-start.2 = (bf16[1,128,128]{2,1,0:T(8,128)(2,1)S(1)}, bf16[1,128,128]{2,1,0:T(8,128)(2,1)S(1)}, u32[]{:S(2)}, u32[]{:S(2)}) collective-permute-start(bf16[1,128,128]{2,1,0:T(8,128)(2,1)S(1)} %fusion.40), channel_id=1, source_target_pairs={{0,64},{64,128},{128,192},{192,256},{256,320},{320,384},{384,448},... | collective-permute-start | bytes 98312 | tf_op jit(solution)/shard_map/ppermute | solution.py:20
  51.1 1.1 collective-permute-done.2
  52.3 4.4 %collective-permute-start.3 = (bf16[1,128,128]{2,1,0:T(8,128)(2,1)S(1)}, bf16[1,128,128]{2,1,0:T(8,128)(2,1)S(1)}, u32[]{:S(2)}, u32[]{:S(2)}) collective-permute-start(bf16[1,128,128]{2,1,0:T(8,128)(2,1)S(1)} %fusion.39), channel_id=1, source_target_pairs={{0,64},{64,128},{128,192},{192,256},{256,320},{320,384},{384,448},... | collective-permute-start | bytes 98312 | tf_op jit(solution)/shard_map/ppermute | solution.py:20
  56.8 1.0 collective-permute-done.3
  58.0 4.5 %collective-permute-start.4 = (bf16[1,128,128]{2,1,0:T(8,128)(2,1)S(1)}, bf16[1,128,128]{2,1,0:T(8,128)(2,1)S(1)}, u32[]{:S(2)}, u32[]{:S(2)}) collective-permute-start(bf16[1,128,128]{2,1,0:T(8,128)(2,1)S(1)} %fusion.38), channel_id=1, source_target_pairs={{0,64},{64,128},{128,192},{192,256},{256,320},{320,384},{384,448},... | collective-permute-start | bytes 98312 | tf_op jit(solution)/shard_map/ppermute | solution.py:20
  62.5 1.3 collective-permute-done.4
  63.9 4.4 %collective-permute-start.5 = (bf16[1,128,128]{2,1,0:T(8,128)(2,1)S(1)}, bf16[1,128,128]{2,1,0:T(8,128)(2,1)S(1)}, u32[]{:S(2)}, u32[]{:S(2)}) collective-permute-start(bf16[1,128,128]{2,1,0:T(8,128)(2,1)S(1)} %fusion.37), channel_id=1, source_target_pairs={{0,64},{64,128},{128,192},{192,256},{256,320},{320,384},{384,448},... | collective-permute-start | bytes 98312 | tf_op jit(solution)/shard_map/ppermute | solution.py:20
  68.4 1.0 collective-permute-done.5
  69.5 4.9 %collective-permute-start.6 = (bf16[1,128,128]{2,1,0:T(8,128)(2,1)S(1)}, bf16[1,128,128]{2,1,0:T(8,128)(2,1)S(1)}, u32[]{:S(2)}, u32[]{:S(2)}) collective-permute-start(bf16[1,128,128]{2,1,0:T(8,128)(2,1)S(1)} %fusion.36), channel_id=1, source_target_pairs={{0,64},{64,128},{128,192},{192,256},{256,320},{320,384},{384,448},... | collective-permute-start | bytes 98312 | tf_op jit(solution)/shard_map/ppermute | solution.py:20
  74.5 1.9 staged_weights.1
  76.4 26.2 %all-to-all-done = bf16[512,24,128]{2,1,0:T(8,128)(2,1)} async-done(((bf16[512,24,128]{2,1,0:T(8,128)(2,1)}), bf16[512,24,128]{2,1,0:T(8,128)(2,1)}, u32[]{:S(2)}, u32[]{:S(2)}) %all-to-all-start) | async-done | bytes 3145760 | tf_op jit(solution)/shard_map/all_to_all | solution.py:411
  102.6 8.7 %expert_rows.1 = bf16[12288,128]{1,0:T(8,128)(2,1)} custom-call(bf16[12288,128]{1,0:T(8,128)(2,1)} %bitcast.17.received_there, bf16[1024,512]{1,0:T(8,128)(2,1)S(1)} %get-tuple-element.93.gate_here, bf16[1024,512]{1,0:T(8,128)(2,1)S(1)} %get-tuple-element.94.up_here, bf16[512,1024]{1,0:T(8,128)(2,1)S(1)} %get-tuple-element.95.down_here), custom_call_target="tpu_custom_call" | custom-call | flops 4831838208 | bytes 9437184 | tf_op jit(solution)/shard_map/expert_rows/pallas_call | solution.py:315
  111.3 11.3 %all-to-all-start.1 = ((bf16[512,24,128]{2,1,0:T(8,128)(2,1)}), bf16[512,24,128]{2,1,0:T(8,128)(2,1)S(1)}, u32[]{:S(2)}, u32[]{:S(2)}) async-start(bf16[512,24,128]{2,1,0:T(8,128)(2,1)} %bitcast.222), calls=%async_computation.1 | async-start | bytes 6291456 | tf_op jit(solution)/shard_map/all_to_all | solution.py:411
  122.6 1.9 fusion.28
  124.6 1.7 broadcast_multiply_fusion
  126.3 22.5 %while.25 = (s32[]{:T(128)}, f32[1,128,128]{2,1,0:T(8,128)S(1)}, f32[4,1,64,128]{3,2,1,0:T(8,128)}, f32[4,1,1]{0,2,1:T(1,128)S(1)}, f32[4,1,64,128]{3,2,1,0:T(8,...) while((s32[]{:T(128)}, f32[1,128,128]{2,1,0:T(8,128)S(1)}, ...), condition=%wide.region_4.5_spmd, body=%wide.region_3.4_spmd.sunk | while | flops 44089344 | bytes 625281 | solution.py:75
  126.8 1.0 convolution_subtract_fusion.3
  127.8 0.9 fusion.109
  128.8 1.6 fusion.108
  130.4 1.5 fusion.110
  132.5 1.0 convolution_subtract_fusion.3
  133.4 0.9 fusion.109
  134.4 1.6 fusion.108
  136.0 1.5 fusion.110
  138.1 1.0 convolution_subtract_fusion.3
  139.0 0.9 fusion.109
  140.0 1.6 fusion.108
  141.6 1.5 fusion.110
  143.1 0.5 constant_dynamic-slice_fusion.2
  143.7 1.0 convolution_subtract_fusion.3
  144.7 0.9 fusion.109
  145.6 1.6 fusion.108
  147.2 1.5 fusion.110
  148.8 1.0 multiply_reduce_fusion
  149.9 1.7 multiply_multiply_fusion
  151.6 46.6 %all-to-all-done.1 = bf16[512,24,128]{2,1,0:T(8,128)(2,1)S(1)} async-done(((bf16[512,24,128]{2,1,0:T(8,128)(2,1)}), bf16[512,24,128]{2,1,0:T(8,128)(2,1)S(1)}, u32[]{:S(2)}, u32[]{:S(2)}) %all-to-all-start.1) | async-done | bytes 3145760 | tf_op jit(solution)/shard_map/all_to_all | solution.py:411
  198.2 3.0 %combine_rows.1 = bf16[128,1024]{1,0:T(8,128)(2,1)} custom-call(s32[10,128]{1,0:T(8,128)S(1)} %bitcast.214, f32[10,128]{1,0:T(8,128)S(1)} %bitcast.215, bf16[12288,128]{1,0:T(8,128)(2,1)S(1)} %bitcast.212), custom_call_target="tpu_custom_call" | custom-call | flops 805306368 | bytes 3145728 | tf_op jit(solution)/shard_map/combine_rows/pallas_call | solution.py:388
  (63 shorter events, 6.7 us)
Async XLA Ops:
  0.6 30.6 %copy-start = (f32[1,4,64,64]{3,2,1,0:T(8,128)S(1)}, f32[1,4,64,64]{3,2,1,0:T(8,128)}, u32[]{:S(2)}) copy-start(f32[1,4,64,64]{3,2,1,0:T(8,128)} %param.24) | copy-start | bytes 196612
  4.7 24.6 %copy-start.7 = (f32[1,256]{1,0:T(1,128)S(1)}, f32[1,256]{1,0:T(1,128)}, u32[]{:S(2)}) copy-start(f32[1,256]{1,0:T(1,128)} %param.22) | copy-start | bytes 3076
  4.7 25.2 %copy-start.8 = (f32[1,256]{1,0:T(1,128)S(1)}, f32[1,256]{1,0:T(1,128)}, u32[]{:S(2)}) copy-start(f32[1,256]{1,0:T(1,128)} %param.23) | copy-start | bytes 3076
  4.7 26.6 %copy-start.6 = (f32[1,256,128]{2,1,0:T(8,128)S(1)}, f32[1,256,128]{2,1,0:T(8,128)}, u32[]{:S(2)}) copy-start(f32[1,256,128]{2,1,0:T(8,128)} %param.20) | copy-start | bytes 393220
  4.7 26.9 %copy-start.3 = (f32[1,256,128]{2,1,0:T(8,128)S(1)}, f32[1,256,128]{2,1,0:T(8,128)}, u32[]{:S(2)}) copy-start(f32[1,256,128]{2,1,0:T(8,128)} %param.19) | copy-start | bytes 393220
  4.7 97.9 %all-to-all-start = ((bf16[512,24,128]{2,1,0:T(8,128)(2,1)}), bf16[512,24,128]{2,1,0:T(8,128)(2,1)}, u32[]{:S(2)}, u32[]{:S(2)}) async-start(bf16[512,24,128]{2,1,0:T(8,128)(2,1)} %bitcast.216), calls=%async_computation | async-start | bytes 6291456 | tf_op jit(solution)/shard_map/all_to_all | solution.py:411
  31.6 1.1 copy-start.4
  32.7 0.7 copy-start.5
  35.5 6.3 %collective-permute-start = (bf16[1,128,128]{2,1,0:T(8,128)(2,1)S(1)}, bf16[1,128,128]{2,1,0:T(8,128)(2,1)S(1)}, u32[]{:S(2)}, u32[]{:S(2)}) collective-permute-start(bf16[1,128,128]{2,1,0:T(8,128)(2,1)S(1)} %fusion.42), channel_id=1, source_target_pairs={{0,64},{64,128},{128,192},{192,256},{256,320},{320,384},{384,448},... | collective-permute-start | bytes 98312 | tf_op jit(solution)/shard_map/ppermute | solution.py:20
  42.0 4.1 %collective-permute-start.1 = (bf16[1,128,128]{2,1,0:T(8,128)(2,1)S(1)}, bf16[1,128,128]{2,1,0:T(8,128)(2,1)S(1)}, u32[]{:S(2)}, u32[]{:S(2)}) collective-permute-start(bf16[1,128,128]{2,1,0:T(8,128)(2,1)S(1)} %fusion.41), channel_id=1, source_target_pairs={{0,64},{64,128},{128,192},{192,256},{256,320},{320,384},{384,448},... | collective-permute-start | bytes 98312 | tf_op jit(solution)/shard_map/ppermute | solution.py:20
  46.3 5.9 %collective-permute-start.2 = (bf16[1,128,128]{2,1,0:T(8,128)(2,1)S(1)}, bf16[1,128,128]{2,1,0:T(8,128)(2,1)S(1)}, u32[]{:S(2)}, u32[]{:S(2)}) collective-permute-start(bf16[1,128,128]{2,1,0:T(8,128)(2,1)S(1)} %fusion.40), channel_id=1, source_target_pairs={{0,64},{64,128},{128,192},{192,256},{256,320},{320,384},{384,448},... | collective-permute-start | bytes 98312 | tf_op jit(solution)/shard_map/ppermute | solution.py:20
  52.3 5.4 %collective-permute-start.3 = (bf16[1,128,128]{2,1,0:T(8,128)(2,1)S(1)}, bf16[1,128,128]{2,1,0:T(8,128)(2,1)S(1)}, u32[]{:S(2)}, u32[]{:S(2)}) collective-permute-start(bf16[1,128,128]{2,1,0:T(8,128)(2,1)S(1)} %fusion.39), channel_id=1, source_target_pairs={{0,64},{64,128},{128,192},{192,256},{256,320},{320,384},{384,448},... | collective-permute-start | bytes 98312 | tf_op jit(solution)/shard_map/ppermute | solution.py:20
  58.0 5.8 %collective-permute-start.4 = (bf16[1,128,128]{2,1,0:T(8,128)(2,1)S(1)}, bf16[1,128,128]{2,1,0:T(8,128)(2,1)S(1)}, u32[]{:S(2)}, u32[]{:S(2)}) collective-permute-start(bf16[1,128,128]{2,1,0:T(8,128)(2,1)S(1)} %fusion.38), channel_id=1, source_target_pairs={{0,64},{64,128},{128,192},{192,256},{256,320},{320,384},{384,448},... | collective-permute-start | bytes 98312 | tf_op jit(solution)/shard_map/ppermute | solution.py:20
  63.9 5.5 %collective-permute-start.5 = (bf16[1,128,128]{2,1,0:T(8,128)(2,1)S(1)}, bf16[1,128,128]{2,1,0:T(8,128)(2,1)S(1)}, u32[]{:S(2)}, u32[]{:S(2)}) collective-permute-start(bf16[1,128,128]{2,1,0:T(8,128)(2,1)S(1)} %fusion.37), channel_id=1, source_target_pairs={{0,64},{64,128},{128,192},{192,256},{256,320},{320,384},{384,448},... | collective-permute-start | bytes 98312 | tf_op jit(solution)/shard_map/ppermute | solution.py:20
  69.5 6.9 %collective-permute-start.6 = (bf16[1,128,128]{2,1,0:T(8,128)(2,1)S(1)}, bf16[1,128,128]{2,1,0:T(8,128)(2,1)S(1)}, u32[]{:S(2)}, u32[]{:S(2)}) collective-permute-start(bf16[1,128,128]{2,1,0:T(8,128)(2,1)S(1)} %fusion.36), channel_id=1, source_target_pairs={{0,64},{64,128},{128,192},{192,256},{256,320},{320,384},{384,448},... | collective-permute-start | bytes 98312 | tf_op jit(solution)/shard_map/ppermute | solution.py:20
  111.3 86.9 %all-to-all-start.1 = ((bf16[512,24,128]{2,1,0:T(8,128)(2,1)}), bf16[512,24,128]{2,1,0:T(8,128)(2,1)S(1)}, u32[]{:S(2)}, u32[]{:S(2)}) async-start(bf16[512,24,128]{2,1,0:T(8,128)(2,1)} %bitcast.222), calls=%async_computation.1 | async-start | bytes 6291456 | tf_op jit(solution)/shard_map/all_to_all | solution.py:411
  122.6 27.3 %copy-start.9 = (f32[128]{0:T(128)S(1)}, f32[128]{0:T(128)}, u32[]{:S(2)}) copy-start(f32[128]{0:T(128)} %param.25) | copy-start | bytes 1540
  122.6 75.6 %copy-start.1 = (s32[128,10]{0,1:T(8,128)S(1)}, s32[128,10]{0,1:T(8,128)}, u32[]{:S(2)}) copy-start(s32[128,10]{0,1:T(8,128)} %param.27) | copy-start | bytes 15364
  122.6 75.6 %copy-start.2 = (f32[128,10]{0,1:T(8,128)S(1)}, f32[128,10]{0,1:T(8,128)}, u32[]{:S(2)}) copy-start(f32[128,10]{0,1:T(8,128)} %param.28) | copy-start | bytes 15364
